TPU v7x, 256 devices: a whole 4x4x8 slice. The times are simulated.
256 devices in a mesh: patch: 16 (over z, core), visit: 16 (over y, x).
Axes of the slice: x: 4, y: 4, z: 8, core: 2. Of those that a mesh axis runs over, the one named last changes fastest.
Arguments:
- blocks: bfloat16 [16, 16, 16, 256, 256], P('patch', 'visit'), may hold values from -6 to 6
- block_patch: int32 [16, 16, 16, 1], P('patch', 'visit'), may hold values from 0 to 15; in each aligned block of 16 rows (0 to 15, 16 to 31, ..., all dimensions but the last counted through in order) at most 2 rows name the same one
- block_slot: int32 [16, 16, 16], P('patch', 'visit'), may hold values from 0 to 7
- block_count: int32 [16, 16], P('patch', 'visit'), may hold values from 12 to 16, as said below
- template: bfloat16 [16, 512, 1024], P('patch', 'visit'), may hold values from -6 to 6
- basis_rows: bfloat16 [9, 21], replicated, may hold values from -1.25 to 1.25
- basis_cols: float32 [9, 21], replicated, may hold values from -1.25 to 1.25
- coeffs: float32 [16, 9], P('visit'), may hold values from -2 to 2
- psf_rows: bfloat16 [16, 2, 25], P('visit'), may hold values from -1.25 to 1.25
- psf_cols: bfloat16 [16, 2, 25], P('visit'), may hold values from -1.25 to 1.25
Outputs:
- filtered: float32 [16, 16, 512, 1024], P('patch', 'visit')
Inputs may be any that keep to these rules, and one draw needn't show every extreme that they name: `block_patch`: among the 16 entries of one list (one patch index and visit) no patch is named more than 2 times, and some list names a patch exactly 2 times. Entries at positions block_count and beyond are unused.
All inputs are finite; a program needn't handle non-finite values.
Results may differ from a plain program's by a relative error of at most 0.005.
Values may be sent and summed in bfloat16 or wider, within the bound.
No kernel may reach another device: no remote copies, remote signals or barrier semaphores. Data moves between devices by JAX's collectives and lax.ppermute only.
A program may use at most 128 MiB of HBM per device.

v0:
```python
import math

import jax
import jax.numpy as jnp
from jax import lax
from jax.sharding import PartitionSpec as P

CAP = 2


def side_by_side(arrays, axis, split_dim, concat_dim, along):
    widths = [math.prod(a.shape[along:]) for a in arrays]
    both = jnp.concatenate(
        [a.reshape(*a.shape[:along], w) for a, w in zip(arrays, widths)], axis=along
    )
    whole = lax.all_to_all(both, axis, split_axis=split_dim, concat_axis=concat_dim, tiled=True)
    blocks = jnp.split(whole, [sum(widths[:k]) for k in range(1, len(widths))], axis=along)
    return tuple(
        (b.reshape(*whole.shape[:along], *a.shape[along:]) for a, b in zip(arrays, blocks))
    )


def one_hot_bands(length, tile_size):
    band_shape = (3, length, tile_size, tile_size)
    side_ids = lax.broadcasted_iota(jnp.int32, band_shape, 0) - 1
    tap_ids = lax.broadcasted_iota(jnp.int32, band_shape, 1)
    inner = lax.broadcasted_iota(jnp.int32, band_shape, 2)
    outer = lax.broadcasted_iota(jnp.int32, band_shape, 3)
    return (side_ids * tile_size + inner - outer + length // 2 == tap_ids).astype(jnp.float32)


def band_tables(kernel_taps, one_hot):
    return jnp.einsum(
        "cl,dlij->cdij", kernel_taps.astype(jnp.float32), one_hot, precision=lax.Precision.HIGHEST
    ).astype(jnp.bfloat16)


def across_columns(source, tables):
    tile_size = tables.shape[-1]
    height, breadth = source.shape
    tile_count = breadth // tile_size
    tiled = source.reshape(height, tile_count, tile_size)
    zero_block = jnp.zeros((height, 1, tile_size), source.dtype)
    left_side = jnp.concatenate([zero_block, tiled[:, :-1]], axis=1)
    right_side = jnp.concatenate([tiled[:, 1:], zero_block], axis=1)
    summed = jnp.einsum("hbt,ctu->chbu", tiled, tables[:, 1], preferred_element_type=jnp.float32)
    half_tile = tile_size // 2
    summed = summed + jnp.einsum(
        "hbt,ctu->chbu",
        left_side[:, :, half_tile:],
        tables[:, 0, half_tile:],
        preferred_element_type=jnp.float32,
    )
    summed = summed + jnp.einsum(
        "hbt,ctu->chbu",
        right_side[:, :, :half_tile],
        tables[:, 2, :half_tile],
        preferred_element_type=jnp.float32,
    )
    return summed.reshape(tables.shape[0], height, breadth)


def across_rows(source, tables):
    tile_size = tables.shape[-1]
    channels, height, breadth = source.shape
    tile_count = height // tile_size
    tiled = source.reshape(channels, tile_count, tile_size, breadth)
    zero_block = jnp.zeros((channels, 1, tile_size, breadth), source.dtype)
    left_side = jnp.concatenate([zero_block, tiled[:, :-1]], axis=1)
    right_side = jnp.concatenate([tiled[:, 1:], zero_block], axis=1)
    summed = jnp.einsum("cbin,cij->bjn", tiled, tables[:, 1], preferred_element_type=jnp.float32)
    half_tile = tile_size // 2
    summed = summed + jnp.einsum(
        "cbin,cij->bjn",
        left_side[:, :, half_tile:],
        tables[:, 0, half_tile:],
        preferred_element_type=jnp.float32,
    )
    summed = summed + jnp.einsum(
        "cbin,cij->bjn",
        right_side[:, :, :half_tile],
        tables[:, 2, :half_tile],
        preferred_element_type=jnp.float32,
    )
    return summed.reshape(height, breadth)


def place_blocks(
    blocks, block_patch, block_slot, block_count, capacity, slot_total, height, breadth
):
    count_here = blocks.shape[2]
    block_edge = blocks.shape[3]
    pieces = blocks.reshape(count_here, block_edge * block_edge)
    destination = block_patch.reshape(count_here)
    slot_index = block_slot.reshape(count_here)
    row_order = lax.broadcasted_iota(jnp.int32, (count_here, count_here), 0)
    col_order = lax.broadcasted_iota(jnp.int32, (count_here, count_here), 1)
    same_patch = destination[:, None] == destination[None, :]
    earlier = jnp.sum((same_patch & (col_order < row_order)).astype(jnp.int32), axis=1)
    target = destination * capacity + earlier
    live_mask = lax.iota(jnp.int32, count_here) < block_count.reshape(())
    n_patch = lax.axis_size("patch")
    places = n_patch * capacity
    place_ids = lax.broadcasted_iota(jnp.int32, (places, count_here), 0)
    picker = ((place_ids == target[None, :]) & live_mask[None, :]).astype(jnp.float32)
    outgoing = jnp.dot(
        picker.astype(jnp.bfloat16), pieces, preferred_element_type=jnp.float32
    ).astype(jnp.bfloat16)
    outgoing = outgoing.reshape(n_patch, capacity, block_edge * block_edge)
    labels = (
        jnp.dot(
            picker, (slot_index - slot_total).astype(jnp.float32), precision=lax.Precision.HIGHEST
        )
        + slot_total
    )
    labels = labels.astype(jnp.bfloat16).reshape(n_patch, capacity)
    arrived, arrived_slots = side_by_side((outgoing, labels), "patch", 0, 0, 2)
    arrived = arrived.reshape(places, block_edge * block_edge)
    slot_ids = lax.broadcasted_iota(jnp.float32, (slot_total, places), 0)
    chosen = (slot_ids == arrived_slots.reshape(1, places).astype(jnp.float32)).astype(jnp.bfloat16)
    placed = jnp.dot(chosen, arrived, preferred_element_type=jnp.float32)
    tall_count = height // block_edge
    wide_count = breadth // block_edge
    placed = placed.reshape(tall_count, wide_count, block_edge, block_edge).transpose(0, 2, 1, 3)
    return placed.reshape(height, breadth)


def per_device(
    blocks,
    block_patch,
    block_slot,
    block_count,
    template,
    basis_rows,
    basis_cols,
    coeffs,
    psf_rows,
    psf_cols,
):
    local_rows = template.shape[1]
    breadth = template.shape[2]
    height = local_rows * lax.axis_size("visit")
    block_edge = blocks.shape[3]
    slot_total = height // block_edge * (breadth // block_edge)
    science = place_blocks(
        blocks, block_patch, block_slot, block_count, CAP, slot_total, height, breadth
    )
    column_hot = one_hot_bands(basis_rows.shape[1], min(128, breadth))
    row_hot = one_hot_bands(basis_cols.shape[1], min(128, height))
    scaled = (coeffs[0][:, None] * basis_cols).astype(jnp.bfloat16)
    start_image = jnp.zeros((height, breadth), jnp.float32)
    all_tables = band_tables(basis_rows, column_hot)
    partial_rows = across_columns(template[0], all_tables).astype(jnp.bfloat16)
    smoothed_all = lax.all_gather(partial_rows, "visit", axis=1, tiled=True)

    def per_stack(model_image, profiles):
        smoothed, col_taps = profiles
        col_table = band_tables(col_taps[None], row_hot)
        return (model_image + across_rows(smoothed[None], col_table), None)

    model_image = lax.scan(per_stack, start_image, (smoothed_all, scaled))[0]
    difference = (science - model_image).astype(jnp.bfloat16)
    psf_column_hot = one_hot_bands(psf_rows.shape[2], min(128, breadth))
    psf_row_hot = one_hot_bands(psf_cols.shape[2], min(128, height))
    blurred = across_columns(difference, band_tables(psf_rows[0], psf_column_hot)).astype(
        jnp.bfloat16
    )
    filtered = across_rows(blurred, band_tables(psf_cols[0], psf_row_hot))
    return filtered[None, None]


def solution(mesh):
    placed = (
        P("patch", "visit", None, None, None),
        P("patch", "visit", None, None),
        P("patch", "visit", None),
        P("patch", "visit"),
        P("patch", "visit", None),
        P(),
        P(),
        P("visit", None),
        P("visit", None, None),
        P("visit", None, None),
    )
    return jax.shard_map(
        per_device,
        mesh=mesh,
        in_specs=placed,
        out_specs=P("patch", "visit", None, None),
        check_vma=False,
    )
```

profile of v0, /device:TPU:1, one launch (start us, length us, event | category | flops | bytes accessed | tf_op | source)
XLA Modules:
  0.0 271.2 jit_solution(4760125843050092103)
XLA Ops:
  7.2 1.4 fusion.30
  8.7 0.7 copy-done.3
  10.5 1.0 copy.144
  12.2 1.2 copy.108
  13.6 3.2 %convolution_convert_fusion = bf16[32,65536]{1,0:T(8,128)(2,1)} fusion(bf16[16,65536]{1,0:T(8,128)(2,1)S(1)} %bitcast.221, s32[16]{0:T(128)S(1)} %multiply_add_fusion.1, pred[16]{0:T(512)(128)(4,1)S(1)} %iota_compare_fusion.20), kind=kOutput, calls=%fused_computation.24 | convolution fusion | flops 69208064 | bytes 6291536 | tf_op jit(solution)/shard_map/dot_general | solution.py:106
  16.8 5.9 %reshape.110 = bf16[16,2,65536]{2,1,0:T(2,128)(2,1)} reshape(bf16[32,65536]{1,0:T(8,128)(2,1)} %convolution_convert_fusion) | data formatting | bytes 8388608 | tf_op jit(solution)/shard_map/reshape | solution.py:109
  23.0 7.9 %pad_maximum_fusion = bf16[16,2,65537]{2,1,0:T(2,128)(2,1)} fusion(bf16[16,2,1]{2,1,0:T(2,128)(2,1)S(1)} %reshape_reshape.5, bf16[16,2,65536]{2,1,0:T(2,128)(2,1)} %reshape.110), kind=kLoop, calls=%fused_computation.28 | loop fusion | flops 8388736 | bytes 8388736 | tf_op jit(solution)/shard_map/concatenate | solution.py:13
  31.0 10.2 %all-to-all-start = ((bf16[16,2,65537]{2,1,0:T(2,128)(2,1)}), bf16[16,2,65537]{2,1,0:T(2,128)(2,1)}, u32[]{:S(2)}, u32[]{:S(2)}) async-start(bf16[16,2,65537]{2,1,0:T(2,128)(2,1)} %pad_maximum_fusion), calls=%async_computation | async-start | bytes 8404992 | tf_op jit(solution)/shard_map/all_to_all | solution.py:16
  41.2 1.5 fusion.36
  43.0 1.5 fusion.35
  44.6 90.3 %all-to-all-done = bf16[16,2,65537]{2,1,0:T(2,128)(2,1)} async-done(((bf16[16,2,65537]{2,1,0:T(2,128)(2,1)}), bf16[16,2,65537]{2,1,0:T(2,128)(2,1)}, u32[]{:S(2)}, u32[]{:S(2)}) %all-to-all-start) | async-done | bytes 4194400 | tf_op jit(solution)/shard_map/all_to_all | solution.py:16
  134.9 7.2 %split.9 = bf16[16,2,65536]{2,1,0:T(2,128)(2,1)} slice(bf16[16,2,65537]{2,1,0:T(2,128)(2,1)} %all-to-all-done), slice={[0:16], [0:2], [0:65536]} | slice | bytes 8388608 | tf_op jit(solution)/shard_map/split | solution.py:17
  142.1 5.4 %reshape.111 = bf16[32,65536]{1,0:T(8,128)(2,1)} reshape(bf16[16,2,65536]{2,1,0:T(2,128)(2,1)} %split.9) | data formatting | bytes 8388608 | tf_op jit(solution)/shard_map/reshape | solution.py:118
  147.6 0.8 convert_reduce_fusion
  148.4 3.0 %fusion.18 = f32[2,4,256,256]{3,1,2,0:T(4,128)S(1)} fusion(bf16[4,256,8,256]{3,2,1,0:T(8,128)(2,1)} %bitcast.217, f32[32]{0:T(128)S(1)} %reshape.114, f32[2,4]{1,0:T(2,128)S(1)} %multiply_add_fusion), kind=kOutput, calls=%fused_computation.30 | convolution fusion | flops 33554688 | bytes 6291616 | tf_op jit(solution)/shard_map/dot_general | solution.py:121
  151.4 1.8 copy.109
  153.2 97.7 %while.11 = (s32[]{:T(128)}, f32[512,1024]{1,0:T(8,128)}, bf16[9,21]{1,0:T(8,128)(2,1)S(1)}, bf16[9,512,1024]{2,1,0:T(8,128)(2,1)}, s32[3]{0:T(128)S(1)}, /*index=5*/s32[]{:T(128)}, s32[]{:T(128)}) while((s32[]{:T(128)}, f32[512,1024]{1,0:T(8,128)}, bf16[9,21]{1,0:T(8,128)(2,1)S(1)}, bf16[9,512,1024]{2,1,0:T(8,128)(2,1)}, ...), condition=%wide.region_2.3_spmd.clone, body=%wide.region_1.2_spmd.clone.sunk | while | flops 288079872 | bytes 33489512 | solution.py:161
  153.8 4.0 %fusion.119 = bf16[1,3,128,128]{3,0,2,1:T(2,128)(2,1)S(1)} fusion(f32[3,21,128,128]{3,2,1,0:T(8,128)S(1)} %fusion.118, bf16[9,21]{1,0:T(8,128)(2,1)S(1)} %get-tuple-element.129, s32[]{:T(128)} %get-tuple-element.120), kind=kOutput, calls=%fused_computation.1.clone.1 | convolution fusion | flops 12386304 | bytes 4227588 | tf_op jit(solution)/shard_map/while/body/eval_jaxpr/cl,dlij->cdij/dot_general | solution.py:33
  157.9 1.3 constant_dynamic-slice_fusion.2
  160.7 1.9 bitcast_add_fusion.4
  163.3 4.0 %fusion.119 = bf16[1,3,128,128]{3,0,2,1:T(2,128)(2,1)S(1)} fusion(f32[3,21,128,128]{3,2,1,0:T(8,128)S(1)} %fusion.118, bf16[9,21]{1,0:T(8,128)(2,1)S(1)} %get-tuple-element.129, s32[]{:T(128)} %get-tuple-element.120), kind=kOutput, calls=%fused_computation.1.clone.1 | convolution fusion | flops 12386304 | bytes 4227588 | tf_op jit(solution)/shard_map/while/body/eval_jaxpr/cl,dlij->cdij/dot_general | solution.py:33
  167.4 1.3 constant_dynamic-slice_fusion.2
  170.2 3.5 %bitcast_add_fusion.4 = f32[512,1024]{1,0:T(8,128)} fusion(f32[128,4,1024]{2,0,1:T(8,128)S(1)} %add_add_fusion.2, f32[512,1024]{1,0:T(8,128)} %get-tuple-element.121, pred[]{:T(512)S(6)} %compare.11), kind=kLoop, calls=%fused_computation.5.clone.1 | loop fusion | flops 1048576 | bytes 6291457 | tf_op jit(solution)/shard_map/while/body/eval_jaxpr/add | solution.py:159
  174.3 4.0 %fusion.119 = bf16[1,3,128,128]{3,0,2,1:T(2,128)(2,1)S(1)} fusion(f32[3,21,128,128]{3,2,1,0:T(8,128)S(1)} %fusion.118, bf16[9,21]{1,0:T(8,128)(2,1)S(1)} %get-tuple-element.129, s32[]{:T(128)} %get-tuple-element.120), kind=kOutput, calls=%fused_computation.1.clone.1 | convolution fusion | flops 12386304 | bytes 4227588 | tf_op jit(solution)/shard_map/while/body/eval_jaxpr/cl,dlij->cdij/dot_general | solution.py:33
  178.4 1.3 constant_dynamic-slice_fusion.2
  181.2 3.5 %bitcast_add_fusion.4 = f32[512,1024]{1,0:T(8,128)} fusion(f32[128,4,1024]{2,0,1:T(8,128)S(1)} %add_add_fusion.2, f32[512,1024]{1,0:T(8,128)} %get-tuple-element.121, pred[]{:T(512)S(6)} %compare.11), kind=kLoop, calls=%fused_computation.5.clone.1 | loop fusion | flops 1048576 | bytes 6291457 | tf_op jit(solution)/shard_map/while/body/eval_jaxpr/add | solution.py:159
  185.3 4.0 %fusion.119 = bf16[1,3,128,128]{3,0,2,1:T(2,128)(2,1)S(1)} fusion(f32[3,21,128,128]{3,2,1,0:T(8,128)S(1)} %fusion.118, bf16[9,21]{1,0:T(8,128)(2,1)S(1)} %get-tuple-element.129, s32[]{:T(128)} %get-tuple-element.120), kind=kOutput, calls=%fused_computation.1.clone.1 | convolution fusion | flops 12386304 | bytes 4227588 | tf_op jit(solution)/shard_map/while/body/eval_jaxpr/cl,dlij->cdij/dot_general | solution.py:33
  189.4 1.3 constant_dynamic-slice_fusion.2
  192.2 3.5 %bitcast_add_fusion.4 = f32[512,1024]{1,0:T(8,128)} fusion(f32[128,4,1024]{2,0,1:T(8,128)S(1)} %add_add_fusion.2, f32[512,1024]{1,0:T(8,128)} %get-tuple-element.121, pred[]{:T(512)S(6)} %compare.11), kind=kLoop, calls=%fused_computation.5.clone.1 | loop fusion | flops 1048576 | bytes 6291457 | tf_op jit(solution)/shard_map/while/body/eval_jaxpr/add | solution.py:159
  196.3 4.0 %fusion.119 = bf16[1,3,128,128]{3,0,2,1:T(2,128)(2,1)S(1)} fusion(f32[3,21,128,128]{3,2,1,0:T(8,128)S(1)} %fusion.118, bf16[9,21]{1,0:T(8,128)(2,1)S(1)} %get-tuple-element.129, s32[]{:T(128)} %get-tuple-element.120), kind=kOutput, calls=%fused_computation.1.clone.1 | convolution fusion | flops 12386304 | bytes 4227588 | tf_op jit(solution)/shard_map/while/body/eval_jaxpr/cl,dlij->cdij/dot_general | solution.py:33
  200.5 1.3 constant_dynamic-slice_fusion.2
  203.3 3.5 %bitcast_add_fusion.4 = f32[512,1024]{1,0:T(8,128)} fusion(f32[128,4,1024]{2,0,1:T(8,128)S(1)} %add_add_fusion.2, f32[512,1024]{1,0:T(8,128)} %get-tuple-element.121, pred[]{:T(512)S(6)} %compare.11), kind=kLoop, calls=%fused_computation.5.clone.1 | loop fusion | flops 1048576 | bytes 6291457 | tf_op jit(solution)/shard_map/while/body/eval_jaxpr/add | solution.py:159
  207.4 3.9 %fusion.119 = bf16[1,3,128,128]{3,0,2,1:T(2,128)(2,1)S(1)} fusion(f32[3,21,128,128]{3,2,1,0:T(8,128)S(1)} %fusion.118, bf16[9,21]{1,0:T(8,128)(2,1)S(1)} %get-tuple-element.129, s32[]{:T(128)} %get-tuple-element.120), kind=kOutput, calls=%fused_computation.1.clone.1 | convolution fusion | flops 12386304 | bytes 4227588 | tf_op jit(solution)/shard_map/while/body/eval_jaxpr/cl,dlij->cdij/dot_general | solution.py:33
  211.5 1.3 constant_dynamic-slice_fusion.2
  214.3 3.5 %bitcast_add_fusion.4 = f32[512,1024]{1,0:T(8,128)} fusion(f32[128,4,1024]{2,0,1:T(8,128)S(1)} %add_add_fusion.2, f32[512,1024]{1,0:T(8,128)} %get-tuple-element.121, pred[]{:T(512)S(6)} %compare.11), kind=kLoop, calls=%fused_computation.5.clone.1 | loop fusion | flops 1048576 | bytes 6291457 | tf_op jit(solution)/shard_map/while/body/eval_jaxpr/add | solution.py:159
  218.4 4.0 %fusion.119 = bf16[1,3,128,128]{3,0,2,1:T(2,128)(2,1)S(1)} fusion(f32[3,21,128,128]{3,2,1,0:T(8,128)S(1)} %fusion.118, bf16[9,21]{1,0:T(8,128)(2,1)S(1)} %get-tuple-element.129, s32[]{:T(128)} %get-tuple-element.120), kind=kOutput, calls=%fused_computation.1.clone.1 | convolution fusion | flops 12386304 | bytes 4227588 | tf_op jit(solution)/shard_map/while/body/eval_jaxpr/cl,dlij->cdij/dot_general | solution.py:33
  222.5 1.3 constant_dynamic-slice_fusion.2
  225.3 3.5 %bitcast_add_fusion.4 = f32[512,1024]{1,0:T(8,128)} fusion(f32[128,4,1024]{2,0,1:T(8,128)S(1)} %add_add_fusion.2, f32[512,1024]{1,0:T(8,128)} %get-tuple-element.121, pred[]{:T(512)S(6)} %compare.11), kind=kLoop, calls=%fused_computation.5.clone.1 | loop fusion | flops 1048576 | bytes 6291457 | tf_op jit(solution)/shard_map/while/body/eval_jaxpr/add | solution.py:159
  229.4 4.0 %fusion.119 = bf16[1,3,128,128]{3,0,2,1:T(2,128)(2,1)S(1)} fusion(f32[3,21,128,128]{3,2,1,0:T(8,128)S(1)} %fusion.118, bf16[9,21]{1,0:T(8,128)(2,1)S(1)} %get-tuple-element.129, s32[]{:T(128)} %get-tuple-element.120), kind=kOutput, calls=%fused_computation.1.clone.1 | convolution fusion | flops 12386304 | bytes 4227588 | tf_op jit(solution)/shard_map/while/body/eval_jaxpr/cl,dlij->cdij/dot_general | solution.py:33
  233.5 1.3 constant_dynamic-slice_fusion.2
  236.3 3.5 %bitcast_add_fusion.4 = f32[512,1024]{1,0:T(8,128)} fusion(f32[128,4,1024]{2,0,1:T(8,128)S(1)} %add_add_fusion.2, f32[512,1024]{1,0:T(8,128)} %get-tuple-element.121, pred[]{:T(512)S(6)} %compare.11), kind=kLoop, calls=%fused_computation.5.clone.1 | loop fusion | flops 1048576 | bytes 6291457 | tf_op jit(solution)/shard_map/while/body/eval_jaxpr/add | solution.py:159
  240.5 4.0 %fusion.119 = bf16[1,3,128,128]{3,0,2,1:T(2,128)(2,1)S(1)} fusion(f32[3,21,128,128]{3,2,1,0:T(8,128)S(1)} %fusion.118, bf16[9,21]{1,0:T(8,128)(2,1)S(1)} %get-tuple-element.129, s32[]{:T(128)} %get-tuple-element.120), kind=kOutput, calls=%fused_computation.1.clone.1 | convolution fusion | flops 12386304 | bytes 4227588 | tf_op jit(solution)/shard_map/while/body/eval_jaxpr/cl,dlij->cdij/dot_general | solution.py:33
  244.6 1.3 constant_dynamic-slice_fusion.2
  247.4 3.5 %bitcast_add_fusion.4 = f32[512,1024]{1,0:T(8,128)} fusion(f32[128,4,1024]{2,0,1:T(8,128)S(1)} %add_add_fusion.2, f32[512,1024]{1,0:T(8,128)} %get-tuple-element.121, pred[]{:T(512)S(6)} %compare.11), kind=kLoop, calls=%fused_computation.5.clone.1 | loop fusion | flops 1048576 | bytes 6291457 | tf_op jit(solution)/shard_map/while/body/eval_jaxpr/add | solution.py:159
  250.9 2.5 subtract_convert_fusion
  256.3 2.0 convert_element_type.117
  258.3 3.0 %copy.67 = bf16[2,4,128,1024]{3,2,0,1:T(8,128)(2,1)S(1)} copy(bf16[2,4,128,1024]{2,1,3,0:T(4,128)(2,1)} %convert_element_type.117) | data formatting | bytes 4194304 | tf_op jit(solution)/shard_map/convert_element_type | solution.py:165
  262.6 1.8 bitcast_add_fusion.1
  (117 shorter events, 26.6 us)
Async XLA Ops:
  6.5 0.7 copy-start
  6.5 146.7 %all-gather.2.cloned.1.call-start = ((), (), s32[]{:S(2)}) async-start(), calls=%async_computation.1 | async-start | bytes 10027008 | tf_op jit(solution)/shard_map/all_gather | solution.py:154
  8.6 0.8 copy-start.3
  10.2 2.0 copy-start.2
  12.2 1.2 copy-start.6
  16.8 5.9 %copy-start.7 = (s32[1,1,16]{2,1,0:T(1,128)S(1)}, s32[1,1,16]{2,1,0:T(1,128)}, u32[]{:S(2)}) copy-start(s32[1,1,16]{2,1,0:T(1,128)} %param.14) | copy-start | bytes 196
  30.9 10.2 %copy-start.8 = (bf16[1,2,25]{2,1,0:T(2,128)(2,1)S(1)}, bf16[1,2,25]{2,1,0:T(2,128)(2,1)}, u32[]{:S(2)}) copy-start(bf16[1,2,25]{2,1,0:T(2,128)(2,1)} %param.21) | copy-start | bytes 304
  31.0 103.9 %all-to-all-start = ((bf16[16,2,65537]{2,1,0:T(2,128)(2,1)}), bf16[16,2,65537]{2,1,0:T(2,128)(2,1)}, u32[]{:S(2)}, u32[]{:S(2)}) async-start(bf16[16,2,65537]{2,1,0:T(2,128)(2,1)} %pad_maximum_fusion), calls=%async_computation | async-start | bytes 8404992 | tf_op jit(solution)/shard_map/all_to_all | solution.py:16
  41.1 1.7 copy-start.4
  41.1 1.7 copy-start.5
  41.2 1.8 copy-start.9
  262.6 1.8 copy-start.1
Sparse Core Ops, SparseCore 0:
  11.7 84.5 all-gather.1
where the time goes:
time: 272 us; the launch traced here: 271 us
  waiting for transfers between devices  90.3 us (33%)
  matrix products  63.3 us (23%)
  other arithmetic  47 us (17%)
  local copies, waits for them, and re-layouts  45.6 us (17%)
  between operations  14.3 us (5%)
  starting transfers between devices  10.2 us (4%)
    all_to_all x1, waiting for transfers between devices, side_by_side(): lax.all_to_all(both, axis, split_axis=split_dim, concat_axis=concat_dim,...  90.3 us
    dot_general x12, matrix products, band_tables(): jnp.einsum('cl,dlij->cdij', kernel_taps.astype(jnp.float32), one_hot, pre...  39.9 us
    add x9, other arithmetic, per_stack(): return (model_image + across_rows(smoothed[None], col_table), None)  30.2 us
    dynamic_slice x9, local copies, waits for them, and re-layouts, per_device(): model_image = lax.scan(per_stack, start_image, (smoothed_all, scaled))[0]  11.7 us
    all_to_all x1, starting transfers between devices, side_by_side(): lax.all_to_all(both, axis, split_axis=split_dim, concat_axis=concat_dim,...  10.2 us
    concatenate x1, other arithmetic, side_by_side(): jnp.concatenate([a.reshape(*a.shape[:along], w) for a, w in zip(arrays, w...  7.94 us
    split x1, local copies, waits for them, and re-layouts, side_by_side(): jnp.split(whole, [sum(widths[:k]) for k in range(1, len(widths))], axis=a...  7.25 us
    reshape x1, local copies, waits for them, and re-layouts, place_blocks(): outgoing = outgoing.reshape(n_patch, capacity, block_edge * block_edge)  5.94 us
  transfers between devices with their start and end apart: 2, of which 1 were waited for; matrix products, arithmetic and copies ran while one was open for 15% of the time, Pallas kernels for 0%

commit v1 on v0

v1 whole, which is shorter than its diff:
```python
import jax
import jax.numpy as jnp
from jax import lax
from jax.experimental import pallas as pl
from jax.experimental.pallas import tpu as pltpu
from jax.sharding import PartitionSpec as P

CAP = 2
LANE = 128
HALO = 64
WINDOW = 256
LAP = 16
F32 = jnp.float32
BF16 = jnp.bfloat16
PARAMS = pltpu.CompilerParams(vmem_limit_bytes=48 * 1024 * 1024)
SMEM = pl.BlockSpec(memory_space=pltpu.SMEM)
VMEM = pl.BlockSpec(memory_space=pltpu.VMEM)
ANY = pl.BlockSpec(memory_space=pl.ANY)


def pack_kernel(patch, slot, count, blocks, outgoing, labels, place, sems):
    entries, edge = blocks.shape[0], blocks.shape[1]
    for row in range(labels.shape[0]):
        for copy in range(CAP):
            labels[row, copy] = -1
    used = jnp.minimum(count[0], entries)

    def send(i, carry):
        target = patch[i]
        copy = jnp.where(labels[target, 0] < 0, 0, 1)
        labels[target, copy] = slot[i]
        place[i] = copy
        move(i, target, copy).start()
        return carry

    def move(i, target, copy):
        start = pl.multiple_of(copy * edge, edge)
        return pltpu.make_async_copy(
            blocks.at[i], outgoing.at[target, pl.ds(start, edge)], sems.at[i]
        )

    def finish(i, carry):
        move(i, patch[i], place[i]).wait()
        return carry

    lax.fori_loop(0, used, send, 0)
    lax.fori_loop(0, used, finish, 0)


def pack(blocks, block_patch, block_slot, block_count, places):
    entries, edge, _ = blocks.shape
    return pl.pallas_call(
        pack_kernel,
        out_shape=(
            jax.ShapeDtypeStruct((places, CAP * edge, edge), blocks.dtype),
            jax.ShapeDtypeStruct((places, CAP), jnp.int32),
        ),
        in_specs=[SMEM, SMEM, SMEM, ANY],
        out_specs=(ANY, SMEM),
        scratch_shapes=[pltpu.SMEM((entries,), jnp.int32), pltpu.SemaphoreType.DMA((entries,))],
        compiler_params=PARAMS,
        name="pack",
    )(block_patch, block_slot, block_count, blocks)


def fill_band(table, taps, index, row0, col0, height, breadth, sign, base):
    length = taps.shape[1]
    for r in range(0, height, 16):
        rows = lax.broadcasted_iota(jnp.int32, (16, breadth), 0)
        cols = lax.broadcasted_iota(jnp.int32, (16, breadth), 1)
        offset = sign * (rows - cols) + (sign * r + base)
        values = jnp.zeros((16, breadth), F32)
        for u in range(length):
            values = jnp.where(offset == u, taps[index, u], values)
        table[pl.ds(row0 + r, 16), pl.ds(col0, breadth)] = values.astype(table.dtype)


def fill_tables(col_table, row_table, col_taps, row_taps):
    half = col_taps.shape[1] // 2
    for k in range(col_taps.shape[0]):
        fill_band(col_table, col_taps, k, 0, k * LANE, WINDOW, LANE, 1, half - HALO)
        for w in range(2):
            fill_band(
                row_table.at[w], row_taps, k, 0, k * WINDOW, WINDOW + LAP, WINDOW, -1,
                half + w * LAP,
            )


def shifted(values):
    rows = values.shape[0]
    edge = jnp.zeros((rows, HALO), F32)
    return jnp.concatenate([edge, values, edge], axis=1).astype(BF16)


def filter_strip(padded, col_table, row_table, stage, strip):
    count = col_table.shape[1] // LANE
    for h in range(2):
        start = strip * WINDOW + h * LANE
        if not isinstance(start, int):
            start = pl.multiple_of(start, LANE)
        for w in range(2):
            across = jnp.dot(
                padded[pl.ds(w * WINDOW, WINDOW), pl.ds(start, WINDOW)],
                col_table[...],
                preferred_element_type=F32,
            ).astype(BF16)
            for k in range(count):
                stage[w, pl.ds(k * WINDOW, WINDOW), pl.ds(h * LANE, LANE)] = across[
                    :, k * LANE : (k + 1) * LANE
                ]
    top = jnp.dot(row_table[0], stage[0], preferred_element_type=F32)
    low = jnp.dot(row_table[1], stage[1], preferred_element_type=F32)
    cut = WINDOW - LAP
    return top[:cut], top[cut:] + low[: 2 * LAP], low[2 * LAP :]


def store_strip(target, parts, strip):
    start = strip * WINDOW
    if not isinstance(start, int):
        start = pl.multiple_of(start, LANE)
    row = 0
    for part in parts:
        target[pl.ds(row, part.shape[0]), pl.ds(start, WINDOW)] = part
        row += part.shape[0]


def make_model(pieces, me, basis_rows, scaled, psf_rows, psf_cols):
    parts = len(pieces)
    local_rows, breadth = pieces[0].shape
    height = parts * local_rows
    basis, components = basis_rows.shape[0], psf_rows.shape[0]

    def kernel(*refs):
        sources = refs[:parts]
        (position, basis_taps, scaled_taps, psf_row_taps, psf_col_taps, model, psf_col_table,
         psf_row_table, padded, col_table, row_table, stage) = refs[parts:]
        fill_tables(col_table, row_table, basis_taps, scaled_taps)
        for d, source in enumerate(sources):
            owner = lax.rem(position[0] - d + parts, parts)
            padded[pl.ds(pl.multiple_of(owner * local_rows, local_rows), local_rows), :] = shifted(
                source[...].astype(F32)
            )

        def strip(j, carry):
            store_strip(model, filter_strip(padded, col_table, row_table, stage, j), j)
            return carry

        lax.fori_loop(0, breadth // WINDOW, strip, 0)
        fill_tables(psf_col_table, psf_row_table, psf_row_taps, psf_col_taps)

    return pl.pallas_call(
        kernel,
        out_shape=(
            jax.ShapeDtypeStruct((height, breadth), F32),
            jax.ShapeDtypeStruct((WINDOW, components * LANE), BF16),
            jax.ShapeDtypeStruct((2, WINDOW + LAP, components * WINDOW), BF16),
        ),
        in_specs=[VMEM] * parts + [SMEM] * 5,
        out_specs=(VMEM, VMEM, VMEM),
        scratch_shapes=[
            pltpu.VMEM((height, breadth + 2 * HALO), BF16),
            pltpu.VMEM((WINDOW, basis * LANE), BF16),
            pltpu.VMEM((2, WINDOW + LAP, basis * WINDOW), BF16),
            pltpu.VMEM((2, basis * WINDOW, WINDOW), BF16),
        ],
        compiler_params=PARAMS,
        name="model",
    )(*pieces, me, basis_rows, scaled, psf_rows, psf_cols)


def finish_kernel(labels, arrived, model, col_table, row_table, out, held, total, padded, stage,
                  result, sems, out_sems):
    sources = labels.shape[0]
    edge = held.shape[1]
    height, breadth = total.shape
    wide = breadth // edge

    def fetch(t):
        p, c = lax.div(t, CAP), lax.rem(t, CAP)
        start = pl.multiple_of(c * edge, edge)
        copy = pltpu.make_async_copy(arrived.at[p, pl.ds(start, edge)], held.at[t], sems.at[t])
        return labels[p, c], copy

    def begin(t, carry):
        label, copy = fetch(t)

        @pl.when(label >= 0)
        def _():
            copy.start()

        return carry

    def add(t, carry):
        label, copy = fetch(t)

        @pl.when(label >= 0)
        def _():
            copy.wait()
            row = pl.multiple_of(lax.div(label, wide) * edge, edge)
            col = pl.multiple_of(lax.rem(label, wide) * edge, edge)
            here = (pl.ds(row, edge), pl.ds(col, edge))
            total[here] = total[here] + held[t].astype(F32)

        return carry

    lax.fori_loop(0, sources * CAP, begin, 0)
    total[...] = -model[...]
    lax.fori_loop(0, sources * CAP, add, 0)
    for r in range(0, height, LANE):
        padded[pl.ds(r, LANE), :] = shifted(total[pl.ds(r, LANE), :])
    copies = []
    for j in range(breadth // WINDOW):
        store_strip(result, filter_strip(padded, col_table, row_table, stage, j), j)
        here = (pl.ds(0, height), pl.ds(j * WINDOW, WINDOW))
        copies.append(pltpu.make_async_copy(result.at[here], out.at[here], out_sems.at[j]))
        copies[-1].start()
    for copy in copies:
        copy.wait()


def finish(labels, arrived, model, col_table, row_table):
    height, breadth = model.shape
    sources, edge = labels.shape[0], arrived.shape[2]
    components = col_table.shape[1] // LANE
    return pl.pallas_call(
        finish_kernel,
        out_shape=jax.ShapeDtypeStruct((height, breadth), F32),
        in_specs=[SMEM, ANY, VMEM, VMEM, VMEM],
        out_specs=ANY,
        scratch_shapes=[
            pltpu.VMEM((sources * CAP, edge, edge), BF16),
            pltpu.VMEM((height, breadth), F32),
            pltpu.VMEM((height, breadth + 2 * HALO), BF16),
            pltpu.VMEM((2, components * WINDOW, WINDOW), BF16),
            pltpu.VMEM((height, breadth), F32),
            pltpu.SemaphoreType.DMA((sources * CAP,)),
            pltpu.SemaphoreType.DMA((breadth // WINDOW,)),
        ],
        compiler_params=PARAMS,
        name="finish",
    )(labels, arrived, model, col_table, row_table)


def per_device(
    blocks,
    block_patch,
    block_slot,
    block_count,
    template,
    basis_rows,
    basis_cols,
    coeffs,
    psf_rows,
    psf_cols,
):
    n_patch, n_visit = lax.axis_size("patch"), lax.axis_size("visit")
    outgoing, labels = pack(
        blocks[0, 0],
        block_patch.reshape(-1),
        block_slot.reshape(-1),
        block_count.reshape(-1),
        n_patch,
    )
    arrived_labels = lax.all_to_all(labels, "patch", 0, 0, tiled=True)
    arrived = lax.all_to_all(outgoing, "patch", 0, 0, tiled=True)
    rows = template[0]
    pieces = [rows]
    for d in range(1, n_visit):
        ring = [(i, (i + d) % n_visit) for i in range(n_visit)]
        pieces.append(lax.ppermute(rows, "visit", ring))
    scaled = coeffs[0][:, None] * basis_cols
    me = lax.axis_index("visit").reshape(1).astype(jnp.int32)
    model, col_table, row_table = make_model(
        pieces, me, basis_rows.astype(F32), scaled, psf_rows[0].astype(F32),
        psf_cols[0].astype(F32),
    )
    filtered = finish(arrived_labels, arrived, model, col_table, row_table)
    return filtered[None, None]


def solution(mesh):
    placed = (
        P("patch", "visit", None, None, None),
        P("patch", "visit", None, None),
        P("patch", "visit", None),
        P("patch", "visit"),
        P("patch", "visit", None),
        P(),
        P(),
        P("visit", None),
        P("visit", None, None),
        P("visit", None, None),
    )
    return jax.shard_map(
        per_device,
        mesh=mesh,
        in_specs=placed,
        out_specs=P("patch", "visit", None, None),
        check_vma=False,
    )
```

time: 272 us -> 128 us (0.47)
  matrix products: 63.3 us -> 0 us
  other arithmetic: 47 us -> 0.08 us
  waiting for transfers between devices: 90.3 us -> 46 us
  local copies, waits for them, and re-layouts: 45.6 us -> 10.3 us
  starting transfers between devices: 10.2 us -> 31.9 us
  Pallas kernels: 0 us -> 21.4 us
  blocking collectives: 0 us -> 16.8 us
  between operations: 14.3 us -> 0.93 us
    dot_general x51 -> x0, matrix products: 63.3 us -> none  [the longest x12 39.9 us: band_tables(): jnp.einsum('cl,dlij->cdij', kernel_taps.astype(jnp.float32), one_hot, pre...]
    all_to_all x1, waiting for transfers between devices: 90.3 us -> 44.9 us  [per_device(): arrived = lax.all_to_all(outgoing, 'patch', 0, 0, tiled=True)]
    add x10 -> x0, other arithmetic: 30.2 us -> none  [the longest x9 30.2 us: per_stack(): return (model_image + across_rows(smoothed[None], col_table), None)]
    ppermute x0 -> x15, starting transfers between devices: none -> 26.8 us  [per_device(): pieces.append(lax.ppermute(rows, 'visit', ring))]
    pallas_call x0 -> x3, Pallas kernels: none -> 21.4 us  [the longest x1 13.3 us: make_model(): pl.pallas_call(kernel, out_shape=(jax.ShapeDtypeStruct((height, breadth),...]
    all_to_all x0 -> x1, blocking collectives: none -> 16.8 us  [per_device(): arrived_labels = lax.all_to_all(labels, 'patch', 0, 0, tiled=True)]
    dynamic_slice x9 -> x0, local copies, waits for them, and re-layouts: 11.7 us -> none  [per_device(): model_image = lax.scan(per_stack, start_image, (smoothed_all, scaled))[0]]
    reshape x2 -> x0, local copies, waits for them, and re-layouts: 11.4 us -> none  [the longest x1 5.94 us: place_blocks(): outgoing = outgoing.reshape(n_patch, capacity, block_edge * block_edge)]
  transfers between devices with their start and end apart: 2 -> 16, of which waited for: 1 -> 2; matrix products, arithmetic and copies ran while one was open for 15% -> 0% of each run, Pallas kernels for 0% -> 10%
where the time goes in v1:
time: 128 us; the launch traced here: 127 us
  waiting for transfers between devices  46 us (36%)
  starting transfers between devices  31.9 us (25%)
  Pallas kernels  21.4 us (17%)
  blocking collectives  16.8 us (13%)
  local copies, waits for them, and re-layouts  10.3 us (8%)
    all_to_all x1, waiting for transfers between devices, per_device(): arrived = lax.all_to_all(outgoing, 'patch', 0, 0, tiled=True)  44.9 us
    ppermute x15, starting transfers between devices, per_device(): pieces.append(lax.ppermute(rows, 'visit', ring))  26.8 us
    all_to_all x1, blocking collectives, per_device(): arrived_labels = lax.all_to_all(labels, 'patch', 0, 0, tiled=True)  16.8 us
    pallas_call x1, Pallas kernels, make_model(): pl.pallas_call(kernel, out_shape=(jax.ShapeDtypeStruct((height, breadth),...  13.3 us
    unnamed x38, local copies, waits for them, and re-layouts  10.3 us
    pallas_call x1, Pallas kernels, finish(): pl.pallas_call(finish_kernel, out_shape=jax.ShapeDtypeStruct((height, bre...  5.44 us
    all_to_all x1, starting transfers between devices, per_device(): arrived = lax.all_to_all(outgoing, 'patch', 0, 0, tiled=True)  5.07 us
    pallas_call x1, Pallas kernels, pack(): pl.pallas_call(pack_kernel, out_shape=(jax.ShapeDtypeStruct((places, CAP...  2.67 us
  transfers between devices with their start and end apart: 16, of which 2 were waited for; matrix products, arithmetic and copies ran while one was open for 0% of the time, Pallas kernels for 10%

profile of v1, /device:TPU:1, one launch (start us, length us, event | category | flops | bytes accessed | tf_op | source)
XLA Modules:
  0.0 127.4 jit_solution(16362546781686905238)
XLA Ops:
  0.7 1.6 %copy-done = bf16[1,1,16,256,256]{4,3,2,1,0:T(8,128)(2,1)S(1)} copy-done((bf16[1,1,16,256,256]{4,3,2,1,0:T(8,128)(2,1)S(1)}, bf16[1,1,16,256,256]{4,3,2,1,0:T(8,128)(2,1)}, u32[]{:S(2)}) %copy-start) | copy-done | bytes 2097176
  2.2 0.7 copy-done.12
  2.9 0.7 copy-done.13
  3.6 2.7 %pack.1 = (bf16[16,512,256]{2,1,0:T(8,128)(2,1)}, s32[16,2]{1,0:T(8,128)S(1)}) custom-call(s32[16]{0:T(128)S(1)} %bitcast.38, s32[16]{0:T(128)S(1)} %bitcast.39, s32[1]{0:T(128)} %bitcast.18.count, bf16[16,256,256]{2,1,0:T(8,128)(2,1)S(1)} %bitcast.19), custom_call_target="tpu_custom_call" | custom-call | tf_op jit(solution)/shard_map/pack/pallas_call | solution.py:52
  6.2 16.8 %all_to_all.16 = s32[16,1,2]{2,1,0:T(1,128)S(1)} all-to-all(s32[16,1,2]{2,1,0:T(1,128)S(1)} %bitcast.37), channel_id=1, replica_groups=mesh['patch'=16,'visit'=16] {'patch'}, dimensions={0} | all-to-all | bytes 256 | tf_op jit(solution)/shard_map/all_to_all | solution.py:264
  23.0 0.0 copy-start.18
  23.0 0.0 copy-start.15
  23.0 5.1 %all-to-all-start.1 = ((bf16[16,512,256]{2,1,0:T(8,128)(2,1)}), bf16[16,512,256]{2,1,0:T(8,128)(2,1)}, u32[]{:S(2)}, u32[]{:S(2)}) async-start(bf16[16,512,256]{2,1,0:T(8,128)(2,1)} %get-tuple-element.11), calls=%async_computation.1 | async-start | bytes 8388608 | tf_op jit(solution)/shard_map/all_to_all | solution.py:265
  28.1 1.4 %collective-permute-start = (bf16[32,1024]{1,0:T(8,128)(2,1)S(1)}, bf16[32,1024]{1,0:T(8,128)(2,1)S(1)}, u32[]{:S(2)}, u32[]{:S(2)}) collective-permute-start(bf16[32,1024]{1,0:T(8,128)(2,1)S(1)} %bitcast.20), channel_id=1, source_target_pairs={{0,1},{1,2},{2,3},{3,4},{4,5},{5,6},{6,7},{7,8},{8,9},{9,10},{10,1... | collective-permute-start | bytes 196616 | tf_op jit(solution)/shard_map/ppermute | solution.py:270
  29.5 2.4 %collective-permute-start.1 = (bf16[32,1024]{1,0:T(8,128)(2,1)S(1)}, bf16[32,1024]{1,0:T(8,128)(2,1)S(1)}, u32[]{:S(2)}, u32[]{:S(2)}) collective-permute-start(bf16[32,1024]{1,0:T(8,128)(2,1)S(1)} %bitcast.21), channel_id=1, source_target_pairs={{0,2},{1,3},{2,4},{3,5},{4,6},{5,7},{6,8},{7,9},{8,10},{9,11},{10,... | collective-permute-start | bytes 196616 | tf_op jit(solution)/shard_map/ppermute | solution.py:270
  31.9 2.2 %collective-permute-start.2 = (bf16[32,1024]{1,0:T(8,128)(2,1)S(1)}, bf16[32,1024]{1,0:T(8,128)(2,1)S(1)}, u32[]{:S(2)}, u32[]{:S(2)}) collective-permute-start(bf16[32,1024]{1,0:T(8,128)(2,1)S(1)} %bitcast.22), channel_id=1, source_target_pairs={{0,3},{1,4},{2,5},{3,6},{4,7},{5,8},{6,9},{7,10},{8,11},{9,12},{10... | collective-permute-start | bytes 196616 | tf_op jit(solution)/shard_map/ppermute | solution.py:270
  34.0 1.2 collective-permute-start.3
  35.3 1.1 collective-permute-start.4
  36.3 0.0 collective-permute-done.refs_1_
  36.3 1.2 collective-permute-start.5
  37.5 0.0 collective-permute-done.1.refs_2_
  37.6 3.2 %collective-permute-start.6 = (bf16[32,1024]{1,0:T(8,128)(2,1)S(1)}, bf16[32,1024]{1,0:T(8,128)(2,1)S(1)}, u32[]{:S(2)}, u32[]{:S(2)}) collective-permute-start(bf16[32,1024]{1,0:T(8,128)(2,1)S(1)} %bitcast.26), channel_id=1, source_target_pairs={{0,7},{1,8},{2,9},{3,10},{4,11},{5,12},{6,13},{7,14},{8,15},{9,0},... | collective-permute-start | bytes 196616 | tf_op jit(solution)/shard_map/ppermute | solution.py:270
  40.8 1.6 %collective-permute-start.7 = (bf16[32,1024]{1,0:T(8,128)(2,1)S(1)}, bf16[32,1024]{1,0:T(8,128)(2,1)S(1)}, u32[]{:S(2)}, u32[]{:S(2)}) collective-permute-start(bf16[32,1024]{1,0:T(8,128)(2,1)S(1)} %bitcast.27), channel_id=1, source_target_pairs={{0,8},{1,9},{2,10},{3,11},{4,12},{5,13},{6,14},{7,15},{8,0},{9,1},... | collective-permute-start | bytes 196616 | tf_op jit(solution)/shard_map/ppermute | solution.py:270
  42.4 1.7 %collective-permute-start.8 = (bf16[32,1024]{1,0:T(8,128)(2,1)S(1)}, bf16[32,1024]{1,0:T(8,128)(2,1)S(1)}, u32[]{:S(2)}, u32[]{:S(2)}) collective-permute-start(bf16[32,1024]{1,0:T(8,128)(2,1)S(1)} %bitcast.28), channel_id=1, source_target_pairs={{0,9},{1,10},{2,11},{3,12},{4,13},{5,14},{6,15},{7,0},{8,1},{9,2},... | collective-permute-start | bytes 196616 | tf_op jit(solution)/shard_map/ppermute | solution.py:270
  44.1 0.0 collective-permute-done.4.refs_5_
  44.1 3.1 %collective-permute-start.9 = (bf16[32,1024]{1,0:T(8,128)(2,1)S(1)}, bf16[32,1024]{1,0:T(8,128)(2,1)S(1)}, u32[]{:S(2)}, u32[]{:S(2)}) collective-permute-start(bf16[32,1024]{1,0:T(8,128)(2,1)S(1)} %bitcast.29), channel_id=1, source_target_pairs={{0,10},{1,11},{2,12},{3,13},{4,14},{5,15},{6,0},{7,1},{8,2},{9,3},... | collective-permute-start | bytes 196616 | tf_op jit(solution)/shard_map/ppermute | solution.py:270
  47.2 0.1 broadcast_multiply_fusion.refs_18_
  47.3 0.0 collective-permute-done.5.refs_6_
  47.3 3.0 %collective-permute-start.10 = (bf16[32,1024]{1,0:T(8,128)(2,1)S(1)}, bf16[32,1024]{1,0:T(8,128)(2,1)S(1)}, u32[]{:S(2)}, u32[]{:S(2)}) collective-permute-start(bf16[32,1024]{1,0:T(8,128)(2,1)S(1)} %bitcast.30), channel_id=1, source_target_pairs={{0,11},{1,12},{2,13},{3,14},{4,15},{5,0},{6,1},{7,2},{8,3},{9,4},{... | collective-permute-start | bytes 196616 | tf_op jit(solution)/shard_map/ppermute | solution.py:270
  50.3 2.1 %collective-permute-start.11 = (bf16[32,1024]{1,0:T(8,128)(2,1)S(1)}, bf16[32,1024]{1,0:T(8,128)(2,1)S(1)}, u32[]{:S(2)}, u32[]{:S(2)}) collective-permute-start(bf16[32,1024]{1,0:T(8,128)(2,1)S(1)} %bitcast.31), channel_id=1, source_target_pairs={{0,12},{1,13},{2,14},{3,15},{4,0},{5,1},{6,2},{7,3},{8,4},{9,5},{1... | collective-permute-start | bytes 196616 | tf_op jit(solution)/shard_map/ppermute | solution.py:270
  52.3 0.0 collective-permute-done.7.refs_8_
  52.4 0.0 collective-permute-start.12
  52.4 0.0 collective-permute-done.8.refs_9_
  52.4 0.7 collective-permute-start.13
  53.0 0.0 collective-permute-done.9.refs_10_
  53.0 2.1 %collective-permute-start.14 = (bf16[32,1024]{1,0:T(8,128)(2,1)S(1)}, bf16[32,1024]{1,0:T(8,128)(2,1)S(1)}, u32[]{:S(2)}, u32[]{:S(2)}) collective-permute-start(bf16[32,1024]{1,0:T(8,128)(2,1)S(1)} %bitcast.34), channel_id=1, source_target_pairs={{0,15},{1,0},{2,1},{3,2},{4,3},{5,4},{6,5},{7,6},{8,7},{9,8},{10,9... | collective-permute-start | bytes 196616 | tf_op jit(solution)/shard_map/ppermute | solution.py:270
  55.1 0.0 copy-start.2
  55.2 0.6 copy-done.2
  55.8 0.6 copy-done.4
  56.4 1.1 collective-permute-done.12.refs_13_
  57.5 0.6 copy-done.6
  58.1 0.0 collective-permute-done.13.refs_14_
  58.1 0.6 copy-done.8
  58.7 0.0 collective-permute-done.14.refs_15_
  58.8 0.6 copy-done.10
  59.4 0.8 copy-done.3
  60.2 0.8 copy-done.5
  61.1 0.8 copy-done.7
  61.9 0.8 copy-done.9
  62.7 0.8 copy-done.11
  63.6 13.3 %model.1 = (f32[512,1024]{1,0:T(8,128)S(1)}, bf16[256,256]{1,0:T(8,128)(2,1)S(1)}, bf16[2,272,512]{2,1,0:T(8,128)(2,1)S(1)}) custom-call(bf16[32,1024]{1,0:T(8,128)(2,1)S(1)} %bitcast.35, bf16[32,1024]{1,0:T(8,128)(2,1)S(1)} %collective-permute-done.refs_1_, bf16[32,1024]{1,0:T(8,128)(2,1)S(1)} %collective-permute-done.1.refs_2_, ...), custom_call_target="tpu_custom_call" | custom-call | tf_op jit(solution)/shard_map/model/pallas_call | solution.py:151
  76.9 44.9 %all-to-all-done.1.arrived = bf16[16,512,256]{2,1,0:T(8,128)(2,1)} async-done(((bf16[16,512,256]{2,1,0:T(8,128)(2,1)}), bf16[16,512,256]{2,1,0:T(8,128)(2,1)}, u32[]{:S(2)}, u32[]{:S(2)}) %all-to-all-start.1) | async-done | bytes 4194336 | tf_op jit(solution)/shard_map/all_to_all | solution.py:265
  121.8 5.4 %finish.1 = f32[512,1024]{1,0:T(8,128)} custom-call(s32[16,2]{1,0:T(8,128)S(1)} %bitcast.36, bf16[16,512,256]{2,1,0:T(8,128)(2,1)} %all-to-all-done.1.arrived, f32[512,1024]{1,0:T(8,128)S(1)} %get-tuple-element.12.model, bf16[256,256]{1,0:T(8,128)(2,1)S(1)} %get-tuple-element.13.col_table, bf16[2,272,512]{2,1,0:T(8,128)(2,1)S(1)} %get-tuple-element.14.row_table), custom_call_target="tpu_custom_call" | custom-call | tf_op jit(solution)/shard_map/finish/pallas_call | solution.py:225
  (29 shorter events, 0.1 us)
Async XLA Ops:
  0.7 1.6 %copy-start = (bf16[1,1,16,256,256]{4,3,2,1,0:T(8,128)(2,1)S(1)}, bf16[1,1,16,256,256]{4,3,2,1,0:T(8,128)(2,1)}, u32[]{:S(2)}) copy-start(bf16[1,1,16,256,256]{4,3,2,1,0:T(8,128)(2,1)} %param.10) | copy-start | bytes 6291460
  2.2 0.7 copy-start.12
  2.9 0.7 copy-start.13
  23.0 5.1 %copy-start.1 = (bf16[1,32,1024]{2,1,0:T(8,128)(2,1)S(1)}, bf16[1,32,1024]{2,1,0:T(8,128)(2,1)}, u32[]{:S(2)}) copy-start(bf16[1,32,1024]{2,1,0:T(8,128)(2,1)} %param.14) | copy-start | bytes 196612
  23.0 24.2 %copy-start.14 = (f32[9,21]{1,0:T(8,128)S(1)}, f32[9,21]{1,0:T(8,128)}, u32[]{:S(2)}) copy-start(f32[9,21]{1,0:T(8,128)} %param.16) | copy-start | bytes 2272
  23.0 24.2 %copy-start.16 = (f32[1,9]{1,0:T(1,128)S(1)}, f32[1,9]{1,0:T(1,128)}, u32[]{:S(2)}) copy-start(f32[1,9]{1,0:T(1,128)} %param.17) | copy-start | bytes 112
  23.0 32.1 %copy-start.17 = (bf16[1,2,25]{2,1,0:T(2,128)(2,1)S(1)}, bf16[1,2,25]{2,1,0:T(2,128)(2,1)}, u32[]{:S(2)}) copy-start(bf16[1,2,25]{2,1,0:T(2,128)(2,1)} %param.19) | copy-start | bytes 304
  23.0 32.1 %copy-start.18 = (bf16[1,2,25]{2,1,0:T(2,128)(2,1)S(1)}, bf16[1,2,25]{2,1,0:T(2,128)(2,1)}, u32[]{:S(2)}) copy-start(bf16[1,2,25]{2,1,0:T(2,128)(2,1)} %param.18) | copy-start | bytes 304
  23.0 32.1 %copy-start.15 = (bf16[9,21]{1,0:T(8,128)(2,1)S(1)}, bf16[9,21]{1,0:T(8,128)(2,1)}, u32[]{:S(2)}) copy-start(bf16[9,21]{1,0:T(8,128)(2,1)} %param.15) | copy-start | bytes 1138
  23.0 98.8 %all-to-all-start.1 = ((bf16[16,512,256]{2,1,0:T(8,128)(2,1)}), bf16[16,512,256]{2,1,0:T(8,128)(2,1)}, u32[]{:S(2)}, u32[]{:S(2)}) async-start(bf16[16,512,256]{2,1,0:T(8,128)(2,1)} %get-tuple-element.11), calls=%async_computation.1 | async-start | bytes 8388608 | tf_op jit(solution)/shard_map/all_to_all | solution.py:265
  28.1 8.2 %collective-permute-start = (bf16[32,1024]{1,0:T(8,128)(2,1)S(1)}, bf16[32,1024]{1,0:T(8,128)(2,1)S(1)}, u32[]{:S(2)}, u32[]{:S(2)}) collective-permute-start(bf16[32,1024]{1,0:T(8,128)(2,1)S(1)} %bitcast.20), channel_id=1, source_target_pairs={{0,1},{1,2},{2,3},{3,4},{4,5},{5,6},{6,7},{7,8},{8,9},{9,10},{10,1... | collective-permute-start | bytes 196616 | tf_op jit(solution)/shard_map/ppermute | solution.py:270
  29.5 8.1 %collective-permute-start.1 = (bf16[32,1024]{1,0:T(8,128)(2,1)S(1)}, bf16[32,1024]{1,0:T(8,128)(2,1)S(1)}, u32[]{:S(2)}, u32[]{:S(2)}) collective-permute-start(bf16[32,1024]{1,0:T(8,128)(2,1)S(1)} %bitcast.21), channel_id=1, source_target_pairs={{0,2},{1,3},{2,4},{3,5},{4,6},{5,7},{6,8},{7,9},{8,10},{9,11},{10,... | collective-permute-start | bytes 196616 | tf_op jit(solution)/shard_map/ppermute | solution.py:270
  31.9 9.0 %collective-permute-start.2 = (bf16[32,1024]{1,0:T(8,128)(2,1)S(1)}, bf16[32,1024]{1,0:T(8,128)(2,1)S(1)}, u32[]{:S(2)}, u32[]{:S(2)}) collective-permute-start(bf16[32,1024]{1,0:T(8,128)(2,1)S(1)} %bitcast.22), channel_id=1, source_target_pairs={{0,3},{1,4},{2,5},{3,6},{4,7},{5,8},{6,9},{7,10},{8,11},{9,12},{10... | collective-permute-start | bytes 196616 | tf_op jit(solution)/shard_map/ppermute | solution.py:270
  34.0 8.4 %collective-permute-start.3 = (bf16[32,1024]{1,0:T(8,128)(2,1)S(1)}, bf16[32,1024]{1,0:T(8,128)(2,1)S(1)}, u32[]{:S(2)}, u32[]{:S(2)}) collective-permute-start(bf16[32,1024]{1,0:T(8,128)(2,1)S(1)} %bitcast.23), channel_id=1, source_target_pairs={{0,4},{1,5},{2,6},{3,7},{4,8},{5,9},{6,10},{7,11},{8,12},{9,13},{1... | collective-permute-start | bytes 196616 | tf_op jit(solution)/shard_map/ppermute | solution.py:270
  35.3 8.9 %collective-permute-start.4 = (bf16[32,1024]{1,0:T(8,128)(2,1)S(1)}, bf16[32,1024]{1,0:T(8,128)(2,1)S(1)}, u32[]{:S(2)}, u32[]{:S(2)}) collective-permute-start(bf16[32,1024]{1,0:T(8,128)(2,1)S(1)} %bitcast.24), channel_id=1, source_target_pairs={{0,5},{1,6},{2,7},{3,8},{4,9},{5,10},{6,11},{7,12},{8,13},{9,14},{... | collective-permute-start | bytes 196616 | tf_op jit(solution)/shard_map/ppermute | solution.py:270
  36.3 11.0 %collective-permute-start.5 = (bf16[32,1024]{1,0:T(8,128)(2,1)S(1)}, bf16[32,1024]{1,0:T(8,128)(2,1)S(1)}, u32[]{:S(2)}, u32[]{:S(2)}) collective-permute-start(bf16[32,1024]{1,0:T(8,128)(2,1)S(1)} %bitcast.25), channel_id=1, source_target_pairs={{0,6},{1,7},{2,8},{3,9},{4,10},{5,11},{6,12},{7,13},{8,14},{9,15},... | collective-permute-start | bytes 196616 | tf_op jit(solution)/shard_map/ppermute | solution.py:270
  37.6 12.7 %collective-permute-start.6 = (bf16[32,1024]{1,0:T(8,128)(2,1)S(1)}, bf16[32,1024]{1,0:T(8,128)(2,1)S(1)}, u32[]{:S(2)}, u32[]{:S(2)}) collective-permute-start(bf16[32,1024]{1,0:T(8,128)(2,1)S(1)} %bitcast.26), channel_id=1, source_target_pairs={{0,7},{1,8},{2,9},{3,10},{4,11},{5,12},{6,13},{7,14},{8,15},{9,0},... | collective-permute-start | bytes 196616 | tf_op jit(solution)/shard_map/ppermute | solution.py:270
  40.8 11.5 %collective-permute-start.7 = (bf16[32,1024]{1,0:T(8,128)(2,1)S(1)}, bf16[32,1024]{1,0:T(8,128)(2,1)S(1)}, u32[]{:S(2)}, u32[]{:S(2)}) collective-permute-start(bf16[32,1024]{1,0:T(8,128)(2,1)S(1)} %bitcast.27), channel_id=1, source_target_pairs={{0,8},{1,9},{2,10},{3,11},{4,12},{5,13},{6,14},{7,15},{8,0},{9,1},... | collective-permute-start | bytes 196616 | tf_op jit(solution)/shard_map/ppermute | solution.py:270
  42.4 10.0 %collective-permute-start.8 = (bf16[32,1024]{1,0:T(8,128)(2,1)S(1)}, bf16[32,1024]{1,0:T(8,128)(2,1)S(1)}, u32[]{:S(2)}, u32[]{:S(2)}) collective-permute-start(bf16[32,1024]{1,0:T(8,128)(2,1)S(1)} %bitcast.28), channel_id=1, source_target_pairs={{0,9},{1,10},{2,11},{3,12},{4,13},{5,14},{6,15},{7,0},{8,1},{9,2},... | collective-permute-start | bytes 196616 | tf_op jit(solution)/shard_map/ppermute | solution.py:270
  44.1 8.9 %collective-permute-start.9 = (bf16[32,1024]{1,0:T(8,128)(2,1)S(1)}, bf16[32,1024]{1,0:T(8,128)(2,1)S(1)}, u32[]{:S(2)}, u32[]{:S(2)}) collective-permute-start(bf16[32,1024]{1,0:T(8,128)(2,1)S(1)} %bitcast.29), channel_id=1, source_target_pairs={{0,10},{1,11},{2,12},{3,13},{4,14},{5,15},{6,0},{7,1},{8,2},{9,3},... | collective-permute-start | bytes 196616 | tf_op jit(solution)/shard_map/ppermute | solution.py:270
  47.3 7.8 %collective-permute-start.10 = (bf16[32,1024]{1,0:T(8,128)(2,1)S(1)}, bf16[32,1024]{1,0:T(8,128)(2,1)S(1)}, u32[]{:S(2)}, u32[]{:S(2)}) collective-permute-start(bf16[32,1024]{1,0:T(8,128)(2,1)S(1)} %bitcast.30), channel_id=1, source_target_pairs={{0,11},{1,12},{2,13},{3,14},{4,15},{5,0},{6,1},{7,2},{8,3},{9,4},{... | collective-permute-start | bytes 196616 | tf_op jit(solution)/shard_map/ppermute | solution.py:270
  50.3 5.5 %collective-permute-start.11 = (bf16[32,1024]{1,0:T(8,128)(2,1)S(1)}, bf16[32,1024]{1,0:T(8,128)(2,1)S(1)}, u32[]{:S(2)}, u32[]{:S(2)}) collective-permute-start(bf16[32,1024]{1,0:T(8,128)(2,1)S(1)} %bitcast.31), channel_id=1, source_target_pairs={{0,12},{1,13},{2,14},{3,15},{4,0},{5,1},{6,2},{7,3},{8,4},{9,5},{1... | collective-permute-start | bytes 196616 | tf_op jit(solution)/shard_map/ppermute | solution.py:270
  52.4 5.1 %collective-permute-start.12 = (bf16[32,1024]{1,0:T(8,128)(2,1)S(1)}, bf16[32,1024]{1,0:T(8,128)(2,1)S(1)}, u32[]{:S(2)}, u32[]{:S(2)}) collective-permute-start(bf16[32,1024]{1,0:T(8,128)(2,1)S(1)} %bitcast.32), channel_id=1, source_target_pairs={{0,13},{1,14},{2,15},{3,0},{4,1},{5,2},{6,3},{7,4},{8,5},{9,6},{10... | collective-permute-start | bytes 196616 | tf_op jit(solution)/shard_map/ppermute | solution.py:270
  52.4 5.7 %collective-permute-start.13 = (bf16[32,1024]{1,0:T(8,128)(2,1)S(1)}, bf16[32,1024]{1,0:T(8,128)(2,1)S(1)}, u32[]{:S(2)}, u32[]{:S(2)}) collective-permute-start(bf16[32,1024]{1,0:T(8,128)(2,1)S(1)} %bitcast.33), channel_id=1, source_target_pairs={{0,14},{1,15},{2,0},{3,1},{4,2},{5,3},{6,4},{7,5},{8,6},{9,7},{10,... | collective-permute-start | bytes 196616 | tf_op jit(solution)/shard_map/ppermute | solution.py:270
  53.0 5.7 %collective-permute-start.14 = (bf16[32,1024]{1,0:T(8,128)(2,1)S(1)}, bf16[32,1024]{1,0:T(8,128)(2,1)S(1)}, u32[]{:S(2)}, u32[]{:S(2)}) collective-permute-start(bf16[32,1024]{1,0:T(8,128)(2,1)S(1)} %bitcast.34), channel_id=1, source_target_pairs={{0,15},{1,0},{2,1},{3,2},{4,3},{5,4},{6,5},{7,6},{8,7},{9,8},{10,9... | collective-permute-start | bytes 196616 | tf_op jit(solution)/shard_map/ppermute | solution.py:270
  55.1 0.6 copy-start.2
  55.8 0.6 copy-start.4
  57.5 0.6 copy-start.6
  58.1 0.6 copy-start.8
  58.8 0.6 copy-start.10
  59.4 0.8 copy-start.3
  60.2 0.8 copy-start.5
  61.1 0.8 copy-start.7
  61.9 0.8 copy-start.9
  62.7 0.8 copy-start.11

commit v2 on v1

v2 whole, which is shorter than its diff:
```python
import jax
import jax.numpy as jnp
from jax import lax
from jax.experimental import pallas as pl
from jax.experimental.pallas import tpu as pltpu
from jax.sharding import PartitionSpec as P

CORES = 2
NOTE_ROWS = 16
NOTE_WORDS = 8
LANE = 128
HALO = 64
WINDOW = 256
LAP = 16
F32 = jnp.float32
BF16 = jnp.bfloat16
PARAMS = pltpu.CompilerParams(vmem_limit_bytes=48 * 1024 * 1024)
SMEM = pl.BlockSpec(memory_space=pltpu.SMEM)
VMEM = pl.BlockSpec(memory_space=pltpu.VMEM)
HBM = pl.BlockSpec(memory_space=pltpu.HBM)


def scan_entries(lists, first, second, extra, chips, here):
    patch, count, entries = lists
    for q in range(first.shape[0]):
        first[q] = -1
        second[q] = -1
    for d in range(chips):
        extra[d] = -1

    def visit(i, left_over):
        q = patch[i]
        again = first[q] >= 0
        d = lax.rem(lax.div(q, CORES) - here + chips, chips)
        taken = extra[d] >= 0

        @pl.when(jnp.logical_not(again))
        def _():
            first[q] = i

        @pl.when(again)
        def _():
            second[q] = i

        @pl.when(jnp.logical_and(again, jnp.logical_not(taken)))
        def _():
            extra[d] = i

        return left_over + jnp.logical_and(again, taken).astype(jnp.int32)

    return lax.fori_loop(0, jnp.minimum(count[0], entries), visit, jnp.int32(0))


def load_lists(sources, targets, sems):
    copies = [
        pltpu.make_async_copy(source, target, sems.at[n])
        for n, (source, target) in enumerate(zip(sources, targets))
    ]
    for copy in copies:
        copy.start()
    for copy in copies:
        copy.wait()


def run_copies(copies):
    for wanted, copy in copies:
        pl.when(wanted)(copy.start)
    for wanted, copy in copies:
        pl.when(wanted)(copy.wait)


def pack_extra_kernel(patch_in, count_in, blocks, after, *refs):
    chips = len(refs) - 7
    outs = refs[:chips]
    patch, count, first, second, extra, list_sems, sems = refs[chips:]
    load_lists((patch_in, count_in), (patch, count), list_sems)
    here = lax.div(lax.axis_index("patch"), CORES)
    scan_entries((patch, count, blocks.shape[0]), first, second, extra, chips, here)
    copies = []
    for d in range(chips):
        i = extra[d]
        copy = pltpu.make_async_copy(blocks.at[jnp.maximum(i, 0)], outs[d], sems.at[d])
        copies.append((i >= 0, copy))
    run_copies(copies)


def pack_extra(blocks, block_patch, block_count, after, places):
    entries, edge, _ = blocks.shape
    chips = places // CORES
    return pl.pallas_call(
        pack_extra_kernel,
        out_shape=(jax.ShapeDtypeStruct((edge, edge), blocks.dtype),) * chips,
        in_specs=[HBM] * 4,
        out_specs=(HBM,) * chips,
        scratch_shapes=[
            pltpu.SMEM((entries,), jnp.int32),
            pltpu.SMEM((1,), jnp.int32),
            pltpu.SMEM((places,), jnp.int32),
            pltpu.SMEM((places,), jnp.int32),
            pltpu.SMEM((chips,), jnp.int32),
            pltpu.SemaphoreType.DMA((2,)),
            pltpu.SemaphoreType.DMA((chips,)),
        ],
        compiler_params=PARAMS,
        name="pack_extra",
    )(block_patch, block_count, blocks, after)


def pack_main_kernel(patch_in, slot_in, count_in, blocks, outgoing, patch, slot, count,
                     first, second, extra, notes, list_sems, sems, note_sem):
    places = outgoing.shape[0]
    edge = blocks.shape[1]
    chips = places // CORES
    load_lists((patch_in, slot_in, count_in), (patch, slot, count), list_sems)
    here = lax.div(lax.axis_index("patch"), CORES)
    left_over = scan_entries((patch, count, blocks.shape[0]), first, second, extra, chips, here)
    copies = []
    for q in range(places):
        i = first[q]
        copy = pltpu.make_async_copy(
            blocks.at[jnp.maximum(i, 0)], outgoing.at[q, pl.ds(0, edge)], sems.at[q]
        )
        copies.append((i >= 0, copy))
    for wanted, copy in copies:
        pl.when(wanted)(copy.start)
    lane = lax.broadcasted_iota(jnp.int32, (NOTE_ROWS, edge), 1)
    for q in range(places):
        i, j = first[q], second[q]
        e = extra[lax.rem(q // CORES - here + chips, chips)]
        words = (
            jnp.where(i >= 0, slot[jnp.maximum(i, 0)], -1),
            jnp.where(e >= 0, lax.rem(patch[jnp.maximum(e, 0)], CORES), -1),
            jnp.where(e >= 0, slot[jnp.maximum(e, 0)], -1),
            left_over,
            jnp.where(j >= 0, slot[jnp.maximum(j, 0)], -1),
        )
        row = jnp.zeros((NOTE_ROWS, edge), jnp.int32)
        for n, word in enumerate(words):
            row = jnp.where(lane == n, word, row)
        notes[q] = row.astype(F32).astype(notes.dtype)
    note_copy = pltpu.make_async_copy(notes, outgoing.at[:, pl.ds(edge, NOTE_ROWS)], note_sem)
    note_copy.start()
    for wanted, copy in copies:
        pl.when(wanted)(copy.wait)
    note_copy.wait()


def pack_main(blocks, block_patch, block_slot, block_count, places):
    entries, edge, _ = blocks.shape
    return pl.pallas_call(
        pack_main_kernel,
        out_shape=jax.ShapeDtypeStruct((places, edge + NOTE_ROWS, edge), blocks.dtype),
        in_specs=[HBM] * 4,
        out_specs=HBM,
        scratch_shapes=[
            pltpu.SMEM((entries,), jnp.int32),
            pltpu.SMEM((entries,), jnp.int32),
            pltpu.SMEM((1,), jnp.int32),
            pltpu.SMEM((places,), jnp.int32),
            pltpu.SMEM((places,), jnp.int32),
            pltpu.SMEM((places // CORES,), jnp.int32),
            pltpu.VMEM((places, NOTE_ROWS, edge), blocks.dtype),
            pltpu.SemaphoreType.DMA((3,)),
            pltpu.SemaphoreType.DMA((places,)),
            pltpu.SemaphoreType.DMA,
        ],
        compiler_params=PARAMS,
        name="pack_main",
    )(block_patch, block_slot, block_count, blocks)


def pack_second_kernel(patch_in, count_in, blocks, outgoing, patch, count, first, second, extra,
                       list_sems, sems):
    places = outgoing.shape[0]
    chips = places // CORES
    load_lists((patch_in, count_in), (patch, count), list_sems)
    here = lax.div(lax.axis_index("patch"), CORES)
    scan_entries((patch, count, blocks.shape[0]), first, second, extra, chips, here)
    copies = []
    for q in range(places):
        i = second[q]
        copy = pltpu.make_async_copy(blocks.at[jnp.maximum(i, 0)], outgoing.at[q], sems.at[q])
        copies.append((i >= 0, copy))
    run_copies(copies)


def pack_second(blocks, block_patch, block_count, places):
    entries, edge, _ = blocks.shape
    return pl.pallas_call(
        pack_second_kernel,
        out_shape=jax.ShapeDtypeStruct((places, edge, edge), blocks.dtype),
        in_specs=[HBM] * 3,
        out_specs=HBM,
        scratch_shapes=[
            pltpu.SMEM((entries,), jnp.int32),
            pltpu.SMEM((1,), jnp.int32),
            pltpu.SMEM((places,), jnp.int32),
            pltpu.SMEM((places,), jnp.int32),
            pltpu.SMEM((places // CORES,), jnp.int32),
            pltpu.SemaphoreType.DMA((2,)),
            pltpu.SemaphoreType.DMA((places,)),
        ],
        compiler_params=PARAMS,
        name="pack_second",
    )(block_patch, block_count, blocks)


def fill_band(table, taps, index, row0, col0, height, breadth, sign, base):
    length = taps.shape[1]
    for r in range(0, height, 16):
        rows = lax.broadcasted_iota(jnp.int32, (16, breadth), 0)
        cols = lax.broadcasted_iota(jnp.int32, (16, breadth), 1)
        offset = sign * (rows - cols) + (sign * r + base)
        values = jnp.zeros((16, breadth), F32)
        for u in range(length):
            values = jnp.where(offset == u, taps[index, u], values)
        table[pl.ds(row0 + r, 16), pl.ds(col0, breadth)] = values.astype(table.dtype)


def fill_tables(col_table, row_table, col_taps, row_taps):
    half = col_taps.shape[1] // 2
    for k in range(col_taps.shape[0]):
        fill_band(col_table, col_taps, k, 0, k * LANE, WINDOW, LANE, 1, half - HALO)
        for w in range(2):
            fill_band(
                row_table.at[w], row_taps, k, 0, k * WINDOW, WINDOW + LAP, WINDOW, -1,
                half + w * LAP,
            )


def shifted(values):
    rows = values.shape[0]
    edge = jnp.zeros((rows, HALO), F32)
    return jnp.concatenate([edge, values, edge], axis=1).astype(BF16)


def filter_strip(padded, col_table, row_table, stage, strip):
    count = col_table.shape[1] // LANE
    for h in range(2):
        start = strip * WINDOW + h * LANE
        if not isinstance(start, int):
            start = pl.multiple_of(start, LANE)
        for w in range(2):
            across = jnp.dot(
                padded[pl.ds(w * WINDOW, WINDOW), pl.ds(start, WINDOW)],
                col_table[...],
                preferred_element_type=F32,
            ).astype(BF16)
            for k in range(count):
                stage[w, pl.ds(k * WINDOW, WINDOW), pl.ds(h * LANE, LANE)] = across[
                    :, k * LANE : (k + 1) * LANE
                ]
    top = jnp.dot(row_table[0], stage[0], preferred_element_type=F32)
    low = jnp.dot(row_table[1], stage[1], preferred_element_type=F32)
    cut = WINDOW - LAP
    return top[:cut], top[cut:] + low[: 2 * LAP], low[2 * LAP :]


def store_strip(target, parts, strip):
    start = strip * WINDOW
    if not isinstance(start, int):
        start = pl.multiple_of(start, LANE)
    row = 0
    for part in parts:
        target[pl.ds(row, part.shape[0]), pl.ds(start, WINDOW)] = part
        row += part.shape[0]


def make_model(pieces, me, basis_rows, scaled, psf_rows, psf_cols):
    parts = len(pieces)
    group_rows, breadth = pieces[0].shape
    local_rows = group_rows // parts
    height = parts * group_rows
    basis, components = basis_rows.shape[0], psf_rows.shape[0]

    def kernel(*refs):
        sources = refs[:parts]
        (position, basis_taps, scaled_taps, psf_row_taps, psf_col_taps, model, psf_col_table,
         psf_row_table, padded, col_table, row_table, stage) = refs[parts:]
        fill_tables(col_table, row_table, basis_taps, scaled_taps)
        y, x = lax.div(position[0], parts), lax.rem(position[0], parts)
        for dy, source in enumerate(sources):
            for dx in range(parts):
                owner = lax.rem(y - dy + parts, parts) * parts + lax.rem(x - dx + parts, parts)
                start = pl.multiple_of(owner * local_rows, local_rows)
                padded[pl.ds(start, local_rows), :] = shifted(
                    source[pl.ds(dx * local_rows, local_rows), :].astype(F32)
                )

        def strip(j, carry):
            store_strip(model, filter_strip(padded, col_table, row_table, stage, j), j)
            return carry

        lax.fori_loop(0, breadth // WINDOW, strip, 0)
        fill_tables(psf_col_table, psf_row_table, psf_row_taps, psf_col_taps)

    return pl.pallas_call(
        kernel,
        out_shape=(
            jax.ShapeDtypeStruct((height, breadth), F32),
            jax.ShapeDtypeStruct((WINDOW, components * LANE), BF16),
            jax.ShapeDtypeStruct((2, WINDOW + LAP, components * WINDOW), BF16),
        ),
        in_specs=[VMEM] * parts + [SMEM] * 5,
        out_specs=(VMEM, VMEM, VMEM),
        scratch_shapes=[
            pltpu.VMEM((height, breadth + 2 * HALO), BF16),
            pltpu.VMEM((WINDOW, basis * LANE), BF16),
            pltpu.VMEM((2, WINDOW + LAP, basis * WINDOW), BF16),
            pltpu.VMEM((2, basis * WINDOW, WINDOW), BF16),
        ],
        compiler_params=PARAMS,
        name="model",
    )(*pieces, me, basis_rows, scaled, psf_rows, psf_cols)


def spot_of(label, edge, wide):
    row = pl.multiple_of(lax.div(label, wide) * edge, edge)
    col = pl.multiple_of(lax.rem(label, wide) * edge, edge)
    return pl.ds(row, edge), pl.ds(col, edge)


def add_first(notes, main, model):
    height, breadth = model.shape
    places, edge = main.shape[0], main.shape[2]

    def kernel(words, blocks, model_in, total):
        total[...] = -model_in[...]

        def step(p, carry):
            label = words[p, 0]

            @pl.when(label >= 0)
            def _():
                spot = spot_of(label, edge, breadth // edge)
                total[spot] = total[spot] + blocks[p, pl.ds(0, edge), :].astype(F32)

            return carry

        lax.fori_loop(0, places, step, 0)

    return pl.pallas_call(
        kernel,
        out_shape=jax.ShapeDtypeStruct((height, breadth), F32),
        in_specs=[SMEM, VMEM, VMEM],
        out_specs=VMEM,
        compiler_params=PARAMS,
        name="add_first",
    )(notes, main, model)


def no_second(shape, dtype):
    return pl.pallas_call(
        lambda out: None,
        out_shape=jax.ShapeDtypeStruct(shape, dtype),
        out_specs=HBM,
        compiler_params=PARAMS,
        name="no_second",
    )()


def finish(notes, own, other, second, total, col_table, row_table):
    height, breadth = total.shape
    places, edge = notes.shape[0], second.shape[1]
    components = col_table.shape[1] // LANE
    chips = len(own)
    wide = breadth // edge

    def kernel(*refs):
        words, by_core = refs[0], (refs[1 : 1 + chips], refs[1 + chips : 1 + 2 * chips])
        (by_source, total_in, col_taps, row_taps, out, held, image, padded, stage, result, sems,
         out_sems) = refs[1 + 2 * chips:]
        here = lax.axis_index("patch")
        core, chip = lax.rem(here, CORES), lax.div(here, CORES)
        left_over = words[0, 3]
        for p in range(1, places):
            left_over = left_over + words[p, 3]
        image[...] = total_in[...]

        @pl.when(left_over == 0)
        def _():
            for n in range(CORES):
                for d in range(chips):
                    sender = lax.rem(core + n, CORES)
                    p = lax.rem(chip - d + chips, chips) * CORES + sender
                    label = words[p, 2]

                    @pl.when(words[p, 1] == core)
                    def _(block=by_core[n][d], label=label):
                        spot = spot_of(label, edge, wide)
                        image[spot] = image[spot] + block[...].astype(F32)

        @pl.when(left_over > 0)
        def _():
            def begin(p, carry):
                @pl.when(words[p, 4] >= 0)
                def _():
                    pltpu.make_async_copy(by_source.at[p], held.at[p], sems.at[p]).start()

                return carry

            def add(p, carry):
                @pl.when(words[p, 4] >= 0)
                def _():
                    pltpu.make_async_copy(by_source.at[p], held.at[p], sems.at[p]).wait()
                    spot = spot_of(words[p, 4], edge, wide)
                    image[spot] = image[spot] + held[p].astype(F32)

                return carry

            lax.fori_loop(0, places, begin, 0)
            lax.fori_loop(0, places, add, 0)

        for r in range(0, height, LANE):
            padded[pl.ds(r, LANE), :] = shifted(image[pl.ds(r, LANE), :])
        copies = []
        for j in range(breadth // WINDOW):
            store_strip(result, filter_strip(padded, col_taps, row_taps, stage, j), j)
            spot = (pl.ds(0, height), pl.ds(j * WINDOW, WINDOW))
            copies.append(pltpu.make_async_copy(result.at[spot], out.at[spot], out_sems.at[j]))
            copies[-1].start()
        for copy in copies:
            copy.wait()

    return pl.pallas_call(
        kernel,
        out_shape=jax.ShapeDtypeStruct((height, breadth), F32),
        in_specs=[SMEM] + [VMEM] * (2 * chips) + [HBM] + [VMEM] * 3,
        out_specs=HBM,
        scratch_shapes=[
            pltpu.VMEM((places, edge, edge), BF16),
            pltpu.VMEM((height, breadth), F32),
            pltpu.VMEM((height, breadth + 2 * HALO), BF16),
            pltpu.VMEM((2, components * WINDOW, WINDOW), BF16),
            pltpu.VMEM((height, breadth), F32),
            pltpu.SemaphoreType.DMA((places,)),
            pltpu.SemaphoreType.DMA((breadth // WINDOW,)),
        ],
        compiler_params=PARAMS,
        name="finish",
    )(notes, *own, *other, second, total, col_table, row_table)


def per_device(
    blocks,
    block_patch,
    block_slot,
    block_count,
    template,
    basis_rows,
    basis_cols,
    coeffs,
    psf_rows,
    psf_cols,
):
    n_patch, n_visit = lax.axis_size("patch"), lax.axis_size("visit")
    chips = n_patch // CORES
    side = 4
    assert side * side == n_visit
    pieces, patches = blocks[0, 0], block_patch.reshape(-1)
    slots, count = block_slot.reshape(-1), block_count.reshape(-1)

    def to_chip(d):
        return [(i, (i + CORES * d) % n_patch) for i in range(n_patch)]

    outgoing = pack_main(pieces, patches, slots, count, n_patch)
    arrived = lax.all_to_all(outgoing, "patch", 0, 0, tiled=True)

    def along_x(d):
        return [(i, i // side * side + (i + d) % side) for i in range(n_visit)]

    def along_y(d):
        return [(i, (i + side * d) % n_visit) for i in range(n_visit)]

    rows = template[0]
    near = [rows] + [lax.ppermute(rows, "visit", along_x(d)) for d in range(1, side)]
    near = jnp.concatenate(near, axis=0)
    groups = [near] + [lax.ppermute(near, "visit", along_y(d)) for d in range(1, side)]
    scaled = coeffs[0][:, None] * basis_cols
    me = lax.axis_index("visit").reshape(1).astype(jnp.int32)
    model, col_table, row_table = make_model(
        groups, me, basis_rows.astype(F32), scaled, psf_rows[0].astype(F32),
        psf_cols[0].astype(F32),
    )
    extra = pack_extra(pieces, patches, count, col_table, n_patch)
    neighbour = [(i, i ^ 1) for i in range(n_patch)]
    own, other = list(extra), [None] * chips
    for d in sorted(range(chips), key=lambda d: min(d, chips - d)):
        if d:
            own[d] = lax.ppermute(extra[d], "patch", to_chip(d))
        other[d] = lax.ppermute(own[d], "patch", neighbour)
    edge = pieces.shape[1]
    notes = arrived[:, edge, :NOTE_WORDS].astype(jnp.int32)
    total = add_first(notes, arrived, model)

    def by_source():
        second = pack_second(pieces, patches, count, n_patch)
        return lax.all_to_all(second, "patch", 0, 0, tiled=True)

    def by_chip():
        return no_second((n_patch, edge, edge), pieces.dtype)

    second = lax.cond(jnp.any(notes[:, 3] > 0), by_source, by_chip)
    filtered = finish(notes, own, other, second, total, col_table, row_table)
    return filtered[None, None]


def solution(mesh):
    placed = (
        P("patch", "visit", None, None, None),
        P("patch", "visit", None, None),
        P("patch", "visit", None),
        P("patch", "visit"),
        P("patch", "visit", None),
        P(),
        P(),
        P("visit", None),
        P("visit", None, None),
        P("visit", None, None),
    )
    return jax.shard_map(
        per_device,
        mesh=mesh,
        in_specs=placed,
        out_specs=P("patch", "visit", None, None),
        check_vma=False,
    )
```

time: 128 us -> 158 us (1.23)
  Pallas kernels: 21.4 us -> 76.1 us
  blocking collectives: 16.8 us -> 0 us
  waiting for transfers between devices: 46 us -> 30.9 us
  starting transfers between devices: 31.9 us -> 41.6 us
  local copies, waits for them, and re-layouts: 10.3 us -> 6.05 us
    pallas_call x2 -> x5, Pallas kernels: 8.12 us -> 62.7 us  [the longest x1 53.9 us: pack_main(): pl.pallas_call(pack_main_kernel, out_shape=jax.ShapeDtypeStruct((places,...]
    all_to_all x1, waiting for transfers between devices: 44.9 us -> 0.01 us  [per_device(): arrived = lax.all_to_all(outgoing, 'patch', 0, 0, tiled=True)]
    ppermute x15 -> x21, waiting for transfers between devices: 1.14 us -> 30.9 us  [the longest x7 18.4 us: per_device(): own[d] = lax.ppermute(extra[d], 'patch', to_chip(d))]
    all_to_all x1 -> x0, blocking collectives: 16.8 us -> none  [per_device(): arrived_labels = lax.all_to_all(labels, 'patch', 0, 0, tiled=True)]
    all_to_all x1, starting transfers between devices: 5.07 us -> 14.1 us  [per_device(): arrived = lax.all_to_all(outgoing, 'patch', 0, 0, tiled=True)]
    unnamed x38, local copies, waits for them, and re-layouts: 10.3 us -> 5.98 us
    ppermute x15 -> x21, starting transfers between devices: 26.8 us -> 27.5 us  [the longest x7 14.9 us: per_device(): own[d] = lax.ppermute(extra[d], 'patch', to_chip(d))]
  transfers between devices with their start and end apart: 16 -> 22, of which waited for: 2 -> 9; matrix products, arithmetic and copies ran while one was open for 0% -> 1% of each run, Pallas kernels for 10% -> 11%
where the time goes in v2:
time: 158 us
  Pallas kernels  76.1 us (48%)
  starting transfers between devices  41.6 us (26%)
  waiting for transfers between devices  30.9 us (20%)
  local copies, waits for them, and re-layouts  6.05 us (4%)
  between operations  1.75 us (1%)
    pallas_call x1, Pallas kernels, pack_main(): pl.pallas_call(pack_main_kernel, out_shape=jax.ShapeDtypeStruct((places,...  53.9 us
    ppermute x7, waiting for transfers between devices, per_device(): own[d] = lax.ppermute(extra[d], 'patch', to_chip(d))  18.4 us
    ppermute x7, starting transfers between devices, per_device(): own[d] = lax.ppermute(extra[d], 'patch', to_chip(d))  14.9 us
    all_to_all x1, starting transfers between devices, per_device(): arrived = lax.all_to_all(outgoing, 'patch', 0, 0, tiled=True)  14.1 us
    pallas_call x1, Pallas kernels, make_model(): pl.pallas_call(kernel, out_shape=(jax.ShapeDtypeStruct((height, breadth),...  13.3 us
    ppermute x3, waiting for transfers between devices, per_device(): lax.ppermute(near, 'visit', along_y(d))  9.74 us
    unnamed x38, local copies, waits for them, and re-layouts  5.98 us
    ppermute x3, starting transfers between devices, per_device(): lax.ppermute(near, 'visit', along_y(d))  4.81 us
  transfers between devices with their start and end apart: 22, of which 9 were waited for; matrix products, arithmetic and copies ran while one was open for 1% of the time, Pallas kernels for 11%

profile of v2, /device:TPU:1, one launch (start us, length us, event | category | flops | bytes accessed | tf_op | source)
XLA Modules:
  0.0 157.9 jit_solution(14248463692127497903)
XLA Ops:
  0.7 0.6 copy-done.10
  1.3 53.9 %pack_main.1 = bf16[16,272,256]{2,1,0:T(8,128)(2,1)} custom-call(s32[16]{0:T(128)} %bitcast.30, s32[16]{0:T(128)S(1)} %bitcast.22, s32[1]{0:T(128)} %bitcast.18.count_in, bf16[16,256,256]{2,1,0:T(8,128)(2,1)} %bitcast.23), custom_call_target="tpu_custom_call" | custom-call | tf_op jit(solution)/shard_map/pack_main/pallas_call | solution.py:150
  55.3 0.0 copy-start.17
  55.3 14.1 %all-to-all-start.1 = ((bf16[16,272,256]{2,1,0:T(8,128)(2,1)}), bf16[16,272,256]{2,1,0:T(8,128)(2,1)}, u32[]{:S(2)}, u32[]{:S(2)}) async-start(bf16[16,272,256]{2,1,0:T(8,128)(2,1)} %pack_main.1), calls=%async_computation.1 | async-start | bytes 4456448 | tf_op jit(solution)/shard_map/all_to_all | solution.py:467
  69.4 0.7 collective-permute-start
  70.2 2.1 %collective-permute-start.1 = (bf16[32,1024]{1,0:T(8,128)(2,1)S(1)}, bf16[32,1024]{1,0:T(8,128)(2,1)S(1)}, u32[]{:S(2)}, u32[]{:S(2)}) collective-permute-start(bf16[32,1024]{1,0:T(8,128)(2,1)S(1)} %bitcast.27), channel_id=1, source_target_pairs={{0,2},{1,3},{2,0},{3,1},{4,6},{5,7},{6,4},{7,5},{8,10},{9,11},{10,... | collective-permute-start | bytes 196616 | tf_op jit(solution)/shard_map/ppermute | solution.py:476
  72.3 1.5 collective-permute-start.2
  73.8 0.5 collective-permute-done
  74.3 1.6 %collective-permute-done.1 = bf16[32,1024]{1,0:T(8,128)(2,1)S(1)} collective-permute-done((bf16[32,1024]{1,0:T(8,128)(2,1)S(1)}, bf16[32,1024]{1,0:T(8,128)(2,1)S(1)}, u32[]{:S(2)}, u32[]{:S(2)}) %collective-permute-start.1) | collective-permute-done | bytes 65568 | tf_op jit(solution)/shard_map/ppermute | solution.py:476
  75.9 0.6 collective-permute-done.2
  76.5 1.6 %collective-permute-start.3 = (bf16[128,1024]{1,0:T(8,128)(2,1)S(1)}, bf16[128,1024]{1,0:T(8,128)(2,1)S(1)}, u32[]{:S(2)}, u32[]{:S(2)}) collective-permute-start(bf16[128,1024]{1,0:T(8,128)(2,1)S(1)} %pad_maximum_fusion.refs_0_), channel_id=1, source_target_pairs={{0,4},{1,5},{2,6},{3,7},{4,8},{5,9},{6,10},{7,11},{8,12},{9,13},{1... | collective-permute-start | bytes 786440 | tf_op jit(solution)/shard_map/ppermute | solution.py:478
  78.2 2.3 %collective-permute-start.4 = (bf16[128,1024]{1,0:T(8,128)(2,1)S(1)}, bf16[128,1024]{1,0:T(8,128)(2,1)S(1)}, u32[]{:S(2)}, u32[]{:S(2)}) collective-permute-start(bf16[128,1024]{1,0:T(8,128)(2,1)S(1)} %pad_maximum_fusion.refs_0_), channel_id=1, source_target_pairs={{0,8},{1,9},{2,10},{3,11},{4,12},{5,13},{6,14},{7,15},{8,0},{9,1},... | collective-permute-start | bytes 786440 | tf_op jit(solution)/shard_map/ppermute | solution.py:478
  80.5 0.9 collective-permute-start.5
  81.4 0.1 broadcast_multiply_fusion.refs_6_
  81.5 3.3 %collective-permute-done.3.refs_1_ = bf16[128,1024]{1,0:T(8,128)(2,1)S(1)} collective-permute-done((bf16[128,1024]{1,0:T(8,128)(2,1)S(1)}, bf16[128,1024]{1,0:T(8,128)(2,1)S(1)}, u32[]{:S(2)}, u32[]{:S(2)}) %collective-permute-start.3) | collective-permute-done | bytes 262176 | tf_op jit(solution)/shard_map/ppermute | solution.py:478
  84.7 6.5 %collective-permute-done.4.refs_2_ = bf16[128,1024]{1,0:T(8,128)(2,1)S(1)} collective-permute-done((bf16[128,1024]{1,0:T(8,128)(2,1)S(1)}, bf16[128,1024]{1,0:T(8,128)(2,1)S(1)}, u32[]{:S(2)}, u32[]{:S(2)}) %collective-permute-start.4) | collective-permute-done | bytes 262176 | tf_op jit(solution)/shard_map/ppermute | solution.py:478
  91.2 0.7 copy-done
  91.9 0.7 copy-done.2
  92.6 0.9 copy-done.1
  93.6 0.9 copy-done.3
  94.5 13.3 %model.1 = (f32[512,1024]{1,0:T(8,128)S(1)}, bf16[256,256]{1,0:T(8,128)(2,1)S(1)}, bf16[2,272,512]{2,1,0:T(8,128)(2,1)S(1)}) custom-call(bf16[128,1024]{1,0:T(8,128)(2,1)S(1)} %pad_maximum_fusion.refs_0_, bf16[128,1024]{1,0:T(8,128)(2,1)S(1)} %collective-permute-done.3.refs_1_, bf16[128,1024]{1,0:T(8,128)(2,1)S(1)} %copy-done.1, ...), custom_call_target="tpu_custom_call" | custom-call | tf_op jit(solution)/shard_map/model/pallas_call | solution.py:297
  107.9 1.9 %pack_extra.1 = (bf16[256,256]{1,0:T(8,128)(2,1)S(1)}, bf16[256,256]{1,0:T(8,128)(2,1)S(1)}, bf16[256,256]{1,0:T(8,128)(2,1)S(1)}, bf16[256,256]{1,0:T(8,128)(2,...) custom-call(s32[16]{0:T(128)S(1)} %bitcast.31, ...), custom_call_target="tpu_custom_call" | custom-call | tf_op jit(solution)/shard_map/pack_extra/pallas_call | solution.py:90
  109.8 1.6 collective-permute-start.6
  111.4 2.1 %collective-permute-start.7 = (bf16[256,256]{1,0:T(8,128)(2,1)S(1)}, bf16[256,256]{1,0:T(8,128)(2,1)S(1)}, u32[]{:S(2)}, u32[]{:S(2)}) collective-permute-start(bf16[256,256]{1,0:T(8,128)(2,1)S(1)} %get-tuple-element.31), channel_id=1, source_target_pairs={{0,64},{16,80},{32,96},{48,112},{64,128},{80,144},{96,160},{112,17... | collective-permute-start | bytes 393224 | tf_op jit(solution)/shard_map/ppermute | solution.py:490
  113.5 2.4 %collective-permute-start.8 = (bf16[256,256]{1,0:T(8,128)(2,1)S(1)}, bf16[256,256]{1,0:T(8,128)(2,1)S(1)}, u32[]{:S(2)}, u32[]{:S(2)}) collective-permute-start(bf16[256,256]{1,0:T(8,128)(2,1)S(1)} %get-tuple-element.32), channel_id=1, source_target_pairs={{0,96},{16,112},{32,128},{48,144},{64,160},{80,176},{96,192},{112,... | collective-permute-start | bytes 393224 | tf_op jit(solution)/shard_map/ppermute | solution.py:490
  115.9 2.0 %collective-permute-start.9 = (bf16[256,256]{1,0:T(8,128)(2,1)S(1)}, bf16[256,256]{1,0:T(8,128)(2,1)S(1)}, u32[]{:S(2)}, u32[]{:S(2)}) collective-permute-start(bf16[256,256]{1,0:T(8,128)(2,1)S(1)} %get-tuple-element.33), channel_id=1, source_target_pairs={{0,128},{16,144},{32,160},{48,176},{64,192},{80,208},{96,224},{112... | collective-permute-start | bytes 393224 | tf_op jit(solution)/shard_map/ppermute | solution.py:490
  117.9 2.6 %collective-permute-start.10 = (bf16[256,256]{1,0:T(8,128)(2,1)S(1)}, bf16[256,256]{1,0:T(8,128)(2,1)}, u32[]{:S(2)}, u32[]{:S(2)}) collective-permute-start(bf16[256,256]{1,0:T(8,128)(2,1)S(1)} %get-tuple-element.34), channel_id=1, source_target_pairs={{0,160},{16,176},{32,192},{48,208},{64,224},{80,240},{96,0},{112,1... | collective-permute-start | bytes 393224 | tf_op jit(solution)/shard_map/ppermute | solution.py:490
  120.5 3.1 %collective-permute-done.6.refs_2_ = bf16[256,256]{1,0:T(8,128)(2,1)S(1)} collective-permute-done((bf16[256,256]{1,0:T(8,128)(2,1)S(1)}, bf16[256,256]{1,0:T(8,128)(2,1)S(1)}, u32[]{:S(2)}, u32[]{:S(2)}) %collective-permute-start.6) | collective-permute-done | bytes 131104 | tf_op jit(solution)/shard_map/ppermute | solution.py:490
  123.6 2.1 %collective-permute-start.11 = (bf16[256,256]{1,0:T(8,128)(2,1)S(1)}, bf16[256,256]{1,0:T(8,128)(2,1)}, u32[]{:S(2)}, u32[]{:S(2)}) collective-permute-start(bf16[256,256]{1,0:T(8,128)(2,1)S(1)} %get-tuple-element.35), channel_id=1, source_target_pairs={{0,192},{16,208},{32,224},{48,240},{64,0},{80,16},{96,32},{112,48}... | collective-permute-start | bytes 393224 | tf_op jit(solution)/shard_map/ppermute | solution.py:490
  125.7 3.0 %collective-permute-done.7.refs_3_ = bf16[256,256]{1,0:T(8,128)(2,1)S(1)} collective-permute-done((bf16[256,256]{1,0:T(8,128)(2,1)S(1)}, bf16[256,256]{1,0:T(8,128)(2,1)S(1)}, u32[]{:S(2)}, u32[]{:S(2)}) %collective-permute-start.7) | collective-permute-done | bytes 131104 | tf_op jit(solution)/shard_map/ppermute | solution.py:490
  128.6 2.2 %collective-permute-start.12 = (bf16[256,256]{1,0:T(8,128)(2,1)S(1)}, bf16[256,256]{1,0:T(8,128)(2,1)}, u32[]{:S(2)}, u32[]{:S(2)}) collective-permute-start(bf16[256,256]{1,0:T(8,128)(2,1)S(1)} %get-tuple-element.36), channel_id=1, source_target_pairs={{0,224},{16,240},{32,0},{48,16},{64,32},{80,48},{96,64},{112,80},{... | collective-permute-start | bytes 393224 | tf_op jit(solution)/shard_map/ppermute | solution.py:490
  130.8 9.1 %collective-permute-done.8.refs_4_ = bf16[256,256]{1,0:T(8,128)(2,1)S(1)} collective-permute-done((bf16[256,256]{1,0:T(8,128)(2,1)S(1)}, bf16[256,256]{1,0:T(8,128)(2,1)S(1)}, u32[]{:S(2)}, u32[]{:S(2)}) %collective-permute-start.8) | collective-permute-done | bytes 131104 | tf_op jit(solution)/shard_map/ppermute | solution.py:490
  139.9 1.0 collective-permute-start.13
  141.0 3.2 %collective-permute-done.9.refs_5_ = bf16[256,256]{1,0:T(8,128)(2,1)S(1)} collective-permute-done((bf16[256,256]{1,0:T(8,128)(2,1)S(1)}, bf16[256,256]{1,0:T(8,128)(2,1)S(1)}, u32[]{:S(2)}, u32[]{:S(2)}) %collective-permute-start.9) | collective-permute-done | bytes 131104 | tf_op jit(solution)/shard_map/ppermute | solution.py:490
  144.2 0.8 collective-permute-start.14
  145.0 0.5 collective-permute-start.16
  145.5 0.1 collective-permute-start.17
  145.6 0.7 copy-done.4
  146.3 0.4 collective-permute-start.18
  146.7 0.7 copy-done.6
  147.4 0.1 collective-permute-start.19
  147.4 0.7 copy-done.8
  148.1 0.4 collective-permute-start.20
  148.5 0.8 slice_convert_fusion
  149.3 0.1 copy.14
  149.4 0.7 compare_reduce_fusion
  150.8 2.5 %add_first.1.refs_18_ = f32[512,1024]{1,0:T(8,128)S(1)} custom-call(s32[16,8]{1,0:T(8,128)S(1)} %bitcast.20, bf16[16,272,256]{2,1,0:T(8,128)(2,1)} %all-to-all-done.1.blocks, f32[512,1024]{1,0:T(8,128)S(1)} %get-tuple-element.37.model_in), custom_call_target="tpu_custom_call" | custom-call | tf_op jit(solution)/shard_map/add_first/pallas_call | solution.py:342
  153.3 4.4 %finish.1 = f32[512,1024]{1,0:T(8,128)} custom-call(s32[16,8]{1,0:T(8,128)S(1)} %bitcast.21, bf16[256,256]{1,0:T(8,128)(2,1)S(1)} %get-tuple-element.29.refs_1_, bf16[256,256]{1,0:T(8,128)(2,1)S(1)} %collective-permute-done.6.refs_2_, bf16[256,256]{1,0:T(8,128)(2,1)S(1)} %collective-permute-done.7.refs_3_, ...), custom_call_target="tpu_custom_call" | custom-call | tf_op jit(solution)/shard_map/finish/pallas_call | solution.py:425
  (48 shorter events, 0.2 us)
Async XLA Ops:
  0.7 0.7 copy-start.10
  55.2 14.2 %copy-start.12 = (bf16[1,32,1024]{2,1,0:T(8,128)(2,1)S(1)}, bf16[1,32,1024]{2,1,0:T(8,128)(2,1)}, u32[]{:S(2)}) copy-start(bf16[1,32,1024]{2,1,0:T(8,128)(2,1)} %param.16) | copy-start | bytes 196612
  55.3 26.1 %copy-start.17 = (bf16[1,2,25]{2,1,0:T(2,128)(2,1)S(1)}, bf16[1,2,25]{2,1,0:T(2,128)(2,1)}, u32[]{:S(2)}) copy-start(bf16[1,2,25]{2,1,0:T(2,128)(2,1)} %param.21) | copy-start | bytes 304
  55.3 26.1 %copy-start.18 = (bf16[1,2,25]{2,1,0:T(2,128)(2,1)S(1)}, bf16[1,2,25]{2,1,0:T(2,128)(2,1)}, u32[]{:S(2)}) copy-start(bf16[1,2,25]{2,1,0:T(2,128)(2,1)} %param.20) | copy-start | bytes 304
  55.3 26.1 %copy-start.15 = (bf16[9,21]{1,0:T(8,128)(2,1)S(1)}, bf16[9,21]{1,0:T(8,128)(2,1)}, u32[]{:S(2)}) copy-start(bf16[9,21]{1,0:T(8,128)(2,1)} %param.17) | copy-start | bytes 1138
  55.3 26.1 %copy-start.13 = (f32[9,21]{1,0:T(8,128)S(1)}, f32[9,21]{1,0:T(8,128)}, u32[]{:S(2)}) copy-start(f32[9,21]{1,0:T(8,128)} %param.18) | copy-start | bytes 2272
  55.3 26.1 %copy-start.16 = (f32[1,9]{1,0:T(1,128)S(1)}, f32[1,9]{1,0:T(1,128)}, u32[]{:S(2)}) copy-start(f32[1,9]{1,0:T(1,128)} %param.19) | copy-start | bytes 112
  55.3 52.6 %copy-start.14 = (s32[1,1,16,1]{2,3,1,0:T(1,128)S(1)}, s32[1,1,16,1]{2,3,1,0:T(1,128)}, u32[]{:S(2)}) copy-start(s32[1,1,16,1]{2,3,1,0:T(1,128)} %param.13) | copy-start | bytes 196
  55.3 93.2 %all-to-all-start.1 = ((bf16[16,272,256]{2,1,0:T(8,128)(2,1)}), bf16[16,272,256]{2,1,0:T(8,128)(2,1)}, u32[]{:S(2)}, u32[]{:S(2)}) async-start(bf16[16,272,256]{2,1,0:T(8,128)(2,1)} %pack_main.1), calls=%async_computation.1 | async-start | bytes 4456448 | tf_op jit(solution)/shard_map/all_to_all | solution.py:467
  69.4 4.8 %collective-permute-start = (bf16[32,1024]{1,0:T(8,128)(2,1)S(1)}, bf16[32,1024]{1,0:T(8,128)(2,1)S(1)}, u32[]{:S(2)}, u32[]{:S(2)}) collective-permute-start(bf16[32,1024]{1,0:T(8,128)(2,1)S(1)} %bitcast.26), channel_id=1, source_target_pairs={{0,1},{1,2},{2,3},{3,0},{4,5},{5,6},{6,7},{7,4},{8,9},{9,10},{10,1... | collective-permute-start | bytes 196616 | tf_op jit(solution)/shard_map/ppermute | solution.py:476
  70.2 5.7 %collective-permute-start.1 = (bf16[32,1024]{1,0:T(8,128)(2,1)S(1)}, bf16[32,1024]{1,0:T(8,128)(2,1)S(1)}, u32[]{:S(2)}, u32[]{:S(2)}) collective-permute-start(bf16[32,1024]{1,0:T(8,128)(2,1)S(1)} %bitcast.27), channel_id=1, source_target_pairs={{0,2},{1,3},{2,0},{3,1},{4,6},{5,7},{6,4},{7,5},{8,10},{9,11},{10,... | collective-permute-start | bytes 196616 | tf_op jit(solution)/shard_map/ppermute | solution.py:476
  72.3 4.2 %collective-permute-start.2 = (bf16[32,1024]{1,0:T(8,128)(2,1)S(1)}, bf16[32,1024]{1,0:T(8,128)(2,1)S(1)}, u32[]{:S(2)}, u32[]{:S(2)}) collective-permute-start(bf16[32,1024]{1,0:T(8,128)(2,1)S(1)} %bitcast.28), channel_id=1, source_target_pairs={{0,3},{1,0},{2,1},{3,2},{4,7},{5,4},{6,5},{7,6},{8,11},{9,8},{10,9... | collective-permute-start | bytes 196616 | tf_op jit(solution)/shard_map/ppermute | solution.py:476
  76.5 8.2 %collective-permute-start.3 = (bf16[128,1024]{1,0:T(8,128)(2,1)S(1)}, bf16[128,1024]{1,0:T(8,128)(2,1)S(1)}, u32[]{:S(2)}, u32[]{:S(2)}) collective-permute-start(bf16[128,1024]{1,0:T(8,128)(2,1)S(1)} %pad_maximum_fusion.refs_0_), channel_id=1, source_target_pairs={{0,4},{1,5},{2,6},{3,7},{4,8},{5,9},{6,10},{7,11},{8,12},{9,13},{1... | collective-permute-start | bytes 786440 | tf_op jit(solution)/shard_map/ppermute | solution.py:478
  78.2 13.0 %collective-permute-start.4 = (bf16[128,1024]{1,0:T(8,128)(2,1)S(1)}, bf16[128,1024]{1,0:T(8,128)(2,1)S(1)}, u32[]{:S(2)}, u32[]{:S(2)}) collective-permute-start(bf16[128,1024]{1,0:T(8,128)(2,1)S(1)} %pad_maximum_fusion.refs_0_), channel_id=1, source_target_pairs={{0,8},{1,9},{2,10},{3,11},{4,12},{5,13},{6,14},{7,15},{8,0},{9,1},... | collective-permute-start | bytes 786440 | tf_op jit(solution)/shard_map/ppermute | solution.py:478
  80.5 11.5 %collective-permute-start.5 = (bf16[128,1024]{1,0:T(8,128)(2,1)S(1)}, bf16[128,1024]{1,0:T(8,128)(2,1)S(1)}, u32[]{:S(2)}, u32[]{:S(2)}) collective-permute-start(bf16[128,1024]{1,0:T(8,128)(2,1)S(1)} %pad_maximum_fusion.refs_0_), channel_id=1, source_target_pairs={{0,12},{1,13},{2,14},{3,15},{4,0},{5,1},{6,2},{7,3},{8,4},{9,5},{1... | collective-permute-start | bytes 786440 | tf_op jit(solution)/shard_map/ppermute | solution.py:478
  91.2 0.7 copy-start
  91.9 0.7 copy-start.2
  92.6 0.9 copy-start.1
  93.6 0.9 copy-start.3
  109.8 13.7 %collective-permute-start.6 = (bf16[256,256]{1,0:T(8,128)(2,1)S(1)}, bf16[256,256]{1,0:T(8,128)(2,1)S(1)}, u32[]{:S(2)}, u32[]{:S(2)}) collective-permute-start(bf16[256,256]{1,0:T(8,128)(2,1)S(1)} %get-tuple-element.30), channel_id=1, source_target_pairs={{0,32},{16,48},{32,64},{48,80},{64,96},{80,112},{96,128},{112,144}... | collective-permute-start | bytes 393224 | tf_op jit(solution)/shard_map/ppermute | solution.py:490
  111.4 17.2 %collective-permute-start.7 = (bf16[256,256]{1,0:T(8,128)(2,1)S(1)}, bf16[256,256]{1,0:T(8,128)(2,1)S(1)}, u32[]{:S(2)}, u32[]{:S(2)}) collective-permute-start(bf16[256,256]{1,0:T(8,128)(2,1)S(1)} %get-tuple-element.31), channel_id=1, source_target_pairs={{0,64},{16,80},{32,96},{48,112},{64,128},{80,144},{96,160},{112,17... | collective-permute-start | bytes 393224 | tf_op jit(solution)/shard_map/ppermute | solution.py:490
  113.5 26.5 %collective-permute-start.8 = (bf16[256,256]{1,0:T(8,128)(2,1)S(1)}, bf16[256,256]{1,0:T(8,128)(2,1)S(1)}, u32[]{:S(2)}, u32[]{:S(2)}) collective-permute-start(bf16[256,256]{1,0:T(8,128)(2,1)S(1)} %get-tuple-element.32), channel_id=1, source_target_pairs={{0,96},{16,112},{32,128},{48,144},{64,160},{80,176},{96,192},{112,... | collective-permute-start | bytes 393224 | tf_op jit(solution)/shard_map/ppermute | solution.py:490
  115.9 28.3 %collective-permute-start.9 = (bf16[256,256]{1,0:T(8,128)(2,1)S(1)}, bf16[256,256]{1,0:T(8,128)(2,1)S(1)}, u32[]{:S(2)}, u32[]{:S(2)}) collective-permute-start(bf16[256,256]{1,0:T(8,128)(2,1)S(1)} %get-tuple-element.33), channel_id=1, source_target_pairs={{0,128},{16,144},{32,160},{48,176},{64,192},{80,208},{96,224},{112... | collective-permute-start | bytes 393224 | tf_op jit(solution)/shard_map/ppermute | solution.py:490
  117.9 27.1 %collective-permute-start.10 = (bf16[256,256]{1,0:T(8,128)(2,1)S(1)}, bf16[256,256]{1,0:T(8,128)(2,1)}, u32[]{:S(2)}, u32[]{:S(2)}) collective-permute-start(bf16[256,256]{1,0:T(8,128)(2,1)S(1)} %get-tuple-element.34), channel_id=1, source_target_pairs={{0,160},{16,176},{32,192},{48,208},{64,224},{80,240},{96,0},{112,1... | collective-permute-start | bytes 393224 | tf_op jit(solution)/shard_map/ppermute | solution.py:490
  123.6 21.4 %collective-permute-start.11 = (bf16[256,256]{1,0:T(8,128)(2,1)S(1)}, bf16[256,256]{1,0:T(8,128)(2,1)}, u32[]{:S(2)}, u32[]{:S(2)}) collective-permute-start(bf16[256,256]{1,0:T(8,128)(2,1)S(1)} %get-tuple-element.35), channel_id=1, source_target_pairs={{0,192},{16,208},{32,224},{48,240},{64,0},{80,16},{96,32},{112,48}... | collective-permute-start | bytes 393224 | tf_op jit(solution)/shard_map/ppermute | solution.py:490
  128.6 16.9 %collective-permute-start.12 = (bf16[256,256]{1,0:T(8,128)(2,1)S(1)}, bf16[256,256]{1,0:T(8,128)(2,1)}, u32[]{:S(2)}, u32[]{:S(2)}) collective-permute-start(bf16[256,256]{1,0:T(8,128)(2,1)S(1)} %get-tuple-element.36), channel_id=1, source_target_pairs={{0,224},{16,240},{32,0},{48,16},{64,32},{80,48},{96,64},{112,80},{... | collective-permute-start | bytes 393224 | tf_op jit(solution)/shard_map/ppermute | solution.py:490
  139.9 5.7 %collective-permute-start.13 = (bf16[256,256]{1,0:T(8,128)(2,1)S(1)}, bf16[256,256]{1,0:T(8,128)(2,1)S(1)}, u32[]{:S(2)}, u32[]{:S(2)}) collective-permute-start(bf16[256,256]{1,0:T(8,128)(2,1)S(1)} %get-tuple-element.29.refs_1_), channel_id=1, source_target_pairs={{0,16},{16,0},{32,48},{48,32},{64,80},{80,64},{96,112},{112,96},{1... | collective-permute-start | bytes 393224 | tf_op jit(solution)/shard_map/ppermute | solution.py:491
  144.2 2.5 %collective-permute-start.14 = (bf16[256,256]{1,0:T(8,128)(2,1)S(1)}, bf16[256,256]{1,0:T(8,128)(2,1)S(1)}, u32[]{:S(2)}, u32[]{:S(2)}) collective-permute-start(bf16[256,256]{1,0:T(8,128)(2,1)S(1)} %collective-permute-done.6.refs_2_), channel_id=1, source_target_pairs={{0,16},{16,0},{32,48},{48,32},{64,80},{80,64},{96,112},{112,96},{1... | collective-permute-start | bytes 393224 | tf_op jit(solution)/shard_map/ppermute | solution.py:491
  145.0 2.4 %collective-permute-start.15 = (bf16[256,256]{1,0:T(8,128)(2,1)S(1)}, bf16[256,256]{1,0:T(8,128)(2,1)S(1)}, u32[]{:S(2)}, u32[]{:S(2)}) collective-permute-start(bf16[256,256]{1,0:T(8,128)(2,1)S(1)} %collective-permute-done.7.refs_3_), channel_id=1, source_target_pairs={{0,16},{16,0},{32,48},{48,32},{64,80},{80,64},{96,112},{112,96},{1... | collective-permute-start | bytes 393224 | tf_op jit(solution)/shard_map/ppermute | solution.py:491
  145.0 8.2 %collective-permute-start.16 = (bf16[256,256]{1,0:T(8,128)(2,1)S(1)}, bf16[256,256]{1,0:T(8,128)(2,1)}, u32[]{:S(2)}, u32[]{:S(2)}) collective-permute-start(bf16[256,256]{1,0:T(8,128)(2,1)S(1)} %collective-permute-done.8.refs_4_), channel_id=1, source_target_pairs={{0,16},{16,0},{32,48},{48,32},{64,80},{80,64},{96,112},{112,96},{1... | collective-permute-start | bytes 393224 | tf_op jit(solution)/shard_map/ppermute | solution.py:491
  145.5 7.7 %collective-permute-start.17 = (bf16[256,256]{1,0:T(8,128)(2,1)S(1)}, bf16[256,256]{1,0:T(8,128)(2,1)}, u32[]{:S(2)}, u32[]{:S(2)}) collective-permute-start(bf16[256,256]{1,0:T(8,128)(2,1)S(1)} %collective-permute-done.9.refs_5_), channel_id=1, source_target_pairs={{0,16},{16,0},{32,48},{48,32},{64,80},{80,64},{96,112},{112,96},{1... | collective-permute-start | bytes 393224 | tf_op jit(solution)/shard_map/ppermute | solution.py:491
  145.6 0.7 copy-start.4
  146.3 7.0 %collective-permute-start.18 = (bf16[256,256]{1,0:T(8,128)(2,1)}, bf16[256,256]{1,0:T(8,128)(2,1)}, u32[]{:S(2)}, u32[]{:S(2)}) collective-permute-start(bf16[256,256]{1,0:T(8,128)(2,1)} %collective-permute-done.10.refs_6_), channel_id=1, source_target_pairs={{0,16},{16,0},{32,48},{48,32},{64,80},{80,64},{96,112},{112,96},{1... | collective-permute-start | bytes 393224 | tf_op jit(solution)/shard_map/ppermute | solution.py:491
  146.7 0.7 copy-start.6
  147.4 5.9 %collective-permute-start.19 = (bf16[256,256]{1,0:T(8,128)(2,1)}, bf16[256,256]{1,0:T(8,128)(2,1)}, u32[]{:S(2)}, u32[]{:S(2)}) collective-permute-start(bf16[256,256]{1,0:T(8,128)(2,1)} %collective-permute-done.11.refs_7_), channel_id=1, source_target_pairs={{0,16},{16,0},{32,48},{48,32},{64,80},{80,64},{96,112},{112,96},{1... | collective-permute-start | bytes 393224 | tf_op jit(solution)/shard_map/ppermute | solution.py:491
  147.4 0.7 copy-start.8
  148.1 5.2 %collective-permute-start.20 = (bf16[256,256]{1,0:T(8,128)(2,1)}, bf16[256,256]{1,0:T(8,128)(2,1)}, u32[]{:S(2)}, u32[]{:S(2)}) collective-permute-start(bf16[256,256]{1,0:T(8,128)(2,1)} %collective-permute-done.12.refs_8_), channel_id=1, source_target_pairs={{0,16},{16,0},{32,48},{48,32},{64,80},{80,64},{96,112},{112,96},{1... | collective-permute-start | bytes 393224 | tf_op jit(solution)/shard_map/ppermute | solution.py:491
  150.7 2.6 %copy-start.5 = (bf16[256,256]{1,0:T(8,128)(2,1)S(1)}, bf16[256,256]{1,0:T(8,128)(2,1)}, u32[]{:S(2)}) copy-start(bf16[256,256]{1,0:T(8,128)(2,1)} %copy-done.4) | copy-start | bytes 393220
  150.7 2.6 %copy-start.7 = (bf16[256,256]{1,0:T(8,128)(2,1)S(1)}, bf16[256,256]{1,0:T(8,128)(2,1)}, u32[]{:S(2)}) copy-start(bf16[256,256]{1,0:T(8,128)(2,1)} %copy-done.6) | copy-start | bytes 393220
  150.7 2.6 %copy-start.9 = (bf16[256,256]{1,0:T(8,128)(2,1)S(1)}, bf16[256,256]{1,0:T(8,128)(2,1)}, u32[]{:S(2)}) copy-start(bf16[256,256]{1,0:T(8,128)(2,1)} %copy-done.8) | copy-start | bytes 393220
  150.7 2.6 %copy-start.11 = (bf16[16,256,256]{2,1,0:T(8,128)(2,1)S(1)}, bf16[16,256,256]{2,1,0:T(8,128)(2,1)}, u32[]{:S(2)}) copy-start(bf16[16,256,256]{2,1,0:T(8,128)(2,1)} %get-tuple-element.41.refs_17_) | copy-start | bytes 6291460

commit v3 on v2

--- a/solution.py
+++ b/solution.py
@@ -51,82 +51,55 @@
     return lax.fori_loop(0, jnp.minimum(count[0], entries), visit, jnp.int32(0))
 
 
-def load_lists(sources, targets, sems):
-    copies = [
-        pltpu.make_async_copy(source, target, sems.at[n])
-        for n, (source, target) in enumerate(zip(sources, targets))
+def copy_entry(blocks, i, target):
+    @pl.when(i >= 0)
+    def _():
+        target[...] = blocks[jnp.maximum(i, 0)]
+
+
+def list_scratch(places):
+    return [
+        pltpu.SMEM((places,), jnp.int32),
+        pltpu.SMEM((places,), jnp.int32),
+        pltpu.SMEM((places // CORES,), jnp.int32),
     ]
-    for copy in copies:
-        copy.start()
-    for copy in copies:
-        copy.wait()
-
-
-def run_copies(copies):
-    for wanted, copy in copies:
-        pl.when(wanted)(copy.start)
-    for wanted, copy in copies:
-        pl.when(wanted)(copy.wait)
-
-
-def pack_extra_kernel(patch_in, count_in, blocks, after, *refs):
-    chips = len(refs) - 7
+
+
+def pack_extra_kernel(patch, count, blocks, after, *refs):
+    chips = len(refs) - 3
     outs = refs[:chips]
-    patch, count, first, second, extra, list_sems, sems = refs[chips:]
-    load_lists((patch_in, count_in), (patch, count), list_sems)
+    first, second, extra = refs[chips:]
     here = lax.div(lax.axis_index("patch"), CORES)
     scan_entries((patch, count, blocks.shape[0]), first, second, extra, chips, here)
-    copies = []
     for d in range(chips):
-        i = extra[d]
-        copy = pltpu.make_async_copy(blocks.at[jnp.maximum(i, 0)], outs[d], sems.at[d])
-        copies.append((i >= 0, copy))
-    run_copies(copies)
+        copy_entry(blocks, extra[d], outs[d])
 
 
 def pack_extra(blocks, block_patch, block_count, after, places):
-    entries, edge, _ = blocks.shape
+    edge = blocks.shape[1]
     chips = places // CORES
     return pl.pallas_call(
         pack_extra_kernel,
         out_shape=(jax.ShapeDtypeStruct((edge, edge), blocks.dtype),) * chips,
-        in_specs=[HBM] * 4,
-        out_specs=(HBM,) * chips,
-        scratch_shapes=[
-            pltpu.SMEM((entries,), jnp.int32),
-            pltpu.SMEM((1,), jnp.int32),
-            pltpu.SMEM((places,), jnp.int32),
-            pltpu.SMEM((places,), jnp.int32),
-            pltpu.SMEM((chips,), jnp.int32),
-            pltpu.SemaphoreType.DMA((2,)),
-            pltpu.SemaphoreType.DMA((chips,)),
-        ],
+        in_specs=[SMEM, SMEM, VMEM, VMEM],
+        out_specs=(VMEM,) * chips,
+        scratch_shapes=list_scratch(places),
         compiler_params=PARAMS,
         name="pack_extra",
     )(block_patch, block_count, blocks, after)
 
 
-def pack_main_kernel(patch_in, slot_in, count_in, blocks, outgoing, patch, slot, count,
-                     first, second, extra, notes, list_sems, sems, note_sem):
+def pack_main_kernel(patch, slot, count, blocks, outgoing, first, second, extra):
     places = outgoing.shape[0]
     edge = blocks.shape[1]
     chips = places // CORES
-    load_lists((patch_in, slot_in, count_in), (patch, slot, count), list_sems)
     here = lax.div(lax.axis_index("patch"), CORES)
     left_over = scan_entries((patch, count, blocks.shape[0]), first, second, extra, chips, here)
-    copies = []
-    for q in range(places):
-        i = first[q]
-        copy = pltpu.make_async_copy(
-            blocks.at[jnp.maximum(i, 0)], outgoing.at[q, pl.ds(0, edge)], sems.at[q]
-        )
-        copies.append((i >= 0, copy))
-    for wanted, copy in copies:
-        pl.when(wanted)(copy.start)
     lane = lax.broadcasted_iota(jnp.int32, (NOTE_ROWS, edge), 1)
     for q in range(places):
         i, j = first[q], second[q]
         e = extra[lax.rem(q // CORES - here + chips, chips)]
+        copy_entry(blocks, i, outgoing.at[q, pl.ds(0, edge)])
         words = (
             jnp.where(i >= 0, slot[jnp.maximum(i, 0)], -1),
             jnp.where(e >= 0, lax.rem(patch[jnp.maximum(e, 0)], CORES), -1),
@@ -137,69 +110,38 @@
         row = jnp.zeros((NOTE_ROWS, edge), jnp.int32)
         for n, word in enumerate(words):
             row = jnp.where(lane == n, word, row)
-        notes[q] = row.astype(F32).astype(notes.dtype)
-    note_copy = pltpu.make_async_copy(notes, outgoing.at[:, pl.ds(edge, NOTE_ROWS)], note_sem)
-    note_copy.start()
-    for wanted, copy in copies:
-        pl.when(wanted)(copy.wait)
-    note_copy.wait()
+        outgoing[q, pl.ds(edge, NOTE_ROWS), :] = row.astype(F32).astype(outgoing.dtype)
 
 
 def pack_main(blocks, block_patch, block_slot, block_count, places):
-    entries, edge, _ = blocks.shape
+    edge = blocks.shape[1]
     return pl.pallas_call(
         pack_main_kernel,
         out_shape=jax.ShapeDtypeStruct((places, edge + NOTE_ROWS, edge), blocks.dtype),
-        in_specs=[HBM] * 4,
-        out_specs=HBM,
-        scratch_shapes=[
-            pltpu.SMEM((entries,), jnp.int32),
-            pltpu.SMEM((entries,), jnp.int32),
-            pltpu.SMEM((1,), jnp.int32),
-            pltpu.SMEM((places,), jnp.int32),
-            pltpu.SMEM((places,), jnp.int32),
-            pltpu.SMEM((places // CORES,), jnp.int32),
-            pltpu.VMEM((places, NOTE_ROWS, edge), blocks.dtype),
-            pltpu.SemaphoreType.DMA((3,)),
-            pltpu.SemaphoreType.DMA((places,)),
-            pltpu.SemaphoreType.DMA,
-        ],
+        in_specs=[SMEM, SMEM, SMEM, VMEM],
+        out_specs=VMEM,
+        scratch_shapes=list_scratch(places),
         compiler_params=PARAMS,
         name="pack_main",
     )(block_patch, block_slot, block_count, blocks)
 
 
-def pack_second_kernel(patch_in, count_in, blocks, outgoing, patch, count, first, second, extra,
-                       list_sems, sems):
+def pack_second_kernel(patch, count, blocks, outgoing, first, second, extra):
     places = outgoing.shape[0]
-    chips = places // CORES
-    load_lists((patch_in, count_in), (patch, count), list_sems)
     here = lax.div(lax.axis_index("patch"), CORES)
-    scan_entries((patch, count, blocks.shape[0]), first, second, extra, chips, here)
-    copies = []
+    scan_entries((patch, count, blocks.shape[0]), first, second, extra, places // CORES, here)
     for q in range(places):
-        i = second[q]
-        copy = pltpu.make_async_copy(blocks.at[jnp.maximum(i, 0)], outgoing.at[q], sems.at[q])
-        copies.append((i >= 0, copy))
-    run_copies(copies)
+        copy_entry(blocks, second[q], outgoing.at[q])
 
 
 def pack_second(blocks, block_patch, block_count, places):
-    entries, edge, _ = blocks.shape
+    edge = blocks.shape[1]
     return pl.pallas_call(
         pack_second_kernel,
         out_shape=jax.ShapeDtypeStruct((places, edge, edge), blocks.dtype),
-        in_specs=[HBM] * 3,
-        out_specs=HBM,
-        scratch_shapes=[
-            pltpu.SMEM((entries,), jnp.int32),
-            pltpu.SMEM((1,), jnp.int32),
-            pltpu.SMEM((places,), jnp.int32),
-            pltpu.SMEM((places,), jnp.int32),
-            pltpu.SMEM((places // CORES,), jnp.int32),
-            pltpu.SemaphoreType.DMA((2,)),
-            pltpu.SemaphoreType.DMA((places,)),
-        ],
+        in_specs=[SMEM, SMEM, VMEM],
+        out_specs=VMEM,
+        scratch_shapes=list_scratch(places),
         compiler_params=PARAMS,
         name="pack_second",
     )(block_patch, block_count, blocks)
@@ -275,7 +217,7 @@
 
     def kernel(*refs):
         sources = refs[:parts]
-        (position, basis_taps, scaled_taps, psf_row_taps, psf_col_taps, model, psf_col_table,
+        (position, basis_taps, scaled_taps, psf_row_taps, psf_col_taps, less, psf_col_table,
          psf_row_table, padded, col_table, row_table, stage) = refs[parts:]
         fill_tables(col_table, row_table, basis_taps, scaled_taps)
         y, x = lax.div(position[0], parts), lax.rem(position[0], parts)
@@ -288,7 +230,8 @@
                 )
 
         def strip(j, carry):
-            store_strip(model, filter_strip(padded, col_table, row_table, stage, j), j)
+            parts = filter_strip(padded, col_table, row_table, stage, j)
+            store_strip(less, [-part for part in parts], j)
             return carry
 
         lax.fori_loop(0, breadth // WINDOW, strip, 0)
@@ -320,12 +263,12 @@
     return pl.ds(row, edge), pl.ds(col, edge)
 
 
-def add_first(notes, main, model):
-    height, breadth = model.shape
+def add_first(notes, main, model_negative):
+    height, breadth = model_negative.shape
     places, edge = main.shape[0], main.shape[2]
 
-    def kernel(words, blocks, model_in, total):
-        total[...] = -model_in[...]
+    def kernel(words, blocks, less, total):
+        total[...] = less[...]
 
         def step(p, carry):
             label = words[p, 0]
@@ -346,7 +289,7 @@
         out_specs=VMEM,
         compiler_params=PARAMS,
         name="add_first",
-    )(notes, main, model)
+    )(notes, main, model_negative)
 
 
 def no_second(shape, dtype):
@@ -478,20 +421,14 @@
     groups = [near] + [lax.ppermute(near, "visit", along_y(d)) for d in range(1, side)]
     scaled = coeffs[0][:, None] * basis_cols
     me = lax.axis_index("visit").reshape(1).astype(jnp.int32)
-    model, col_table, row_table = make_model(
+    total, col_table, row_table = make_model(
         groups, me, basis_rows.astype(F32), scaled, psf_rows[0].astype(F32),
         psf_cols[0].astype(F32),
     )
     extra = pack_extra(pieces, patches, count, col_table, n_patch)
-    neighbour = [(i, i ^ 1) for i in range(n_patch)]
-    own, other = list(extra), [None] * chips
-    for d in sorted(range(chips), key=lambda d: min(d, chips - d)):
-        if d:
-            own[d] = lax.ppermute(extra[d], "patch", to_chip(d))
-        other[d] = lax.ppermute(own[d], "patch", neighbour)
     edge = pieces.shape[1]
     notes = arrived[:, edge, :NOTE_WORDS].astype(jnp.int32)
-    total = add_first(notes, arrived, model)
+    total = add_first(notes, arrived, total)
 
     def by_source():
         second = pack_second(pieces, patches, count, n_patch)
@@ -501,6 +438,14 @@
         return no_second((n_patch, edge, edge), pieces.dtype)
 
     second = lax.cond(jnp.any(notes[:, 3] > 0), by_source, by_chip)
+    neighbour = [(i, i ^ 1) for i in range(n_patch)]
+    own, other = list(extra), [None] * chips
+    near_last = sorted(range(1, chips), key=lambda d: -min(d, chips - d))
+    for d in near_last:
+        own[d] = lax.ppermute(extra[d], "patch", to_chip(d))
+    for d in [0] + near_last:
+        own[d], _ = lax.optimization_barrier((own[d], second))
+        other[d] = lax.ppermute(own[d], "patch", neighbour)
     filtered = finish(notes, own, other, second, total, col_table, row_table)
     return filtered[None, None]
 

time: 158 us -> 103 us (0.65)
  Pallas kernels: 76.1 us -> 26.3 us
  waiting for transfers between devices: 30.9 us -> 26.2 us
    pallas_call x1, Pallas kernels: 53.9 us -> 3.69 us  [pack_main(): pl.pallas_call(pack_main_kernel, out_shape=jax.ShapeDtypeStruct((places,...]
    ppermute x7, waiting for transfers between devices: 18.4 us -> 6.94 us  [per_device(): own[d] = lax.ppermute(extra[d], 'patch', to_chip(d))]
    ppermute x8, starting transfers between devices: 3.38 us -> 9.18 us  [per_device(): other[d] = lax.ppermute(own[d], 'patch', neighbour)]
    all_to_all x1, starting transfers between devices: 14.1 us -> 10.1 us  [per_device(): arrived = lax.all_to_all(outgoing, 'patch', 0, 0, tiled=True)]
    ppermute x3, waiting for transfers between devices: 9.74 us -> 13.7 us  [per_device(): lax.ppermute(near, 'visit', along_y(d))]
    ppermute x3, waiting for transfers between devices: 2.73 us -> 5.56 us  [per_device(): lax.ppermute(rows, 'visit', along_x(d))]
    unnamed x38 -> x30, local copies, waits for them, and re-layouts: 5.98 us -> 5.3 us
  transfers between devices with their start and end apart: 22 -> 22, of which waited for: 9 -> 8; matrix products, arithmetic and copies ran while one was open for 1% -> 2% of each run, Pallas kernels for 11% -> 18%
where the time goes in v3:
time: 103 us
  starting transfers between devices  41.4 us (40%)
  Pallas kernels  26.3 us (26%)
  waiting for transfers between devices  26.2 us (25%)
  local copies, waits for them, and re-layouts  5.37 us (5%)
  between operations  1.6 us (2%)
  other arithmetic  1.5 us (1%)
    ppermute x7, starting transfers between devices, per_device(): own[d] = lax.ppermute(extra[d], 'patch', to_chip(d))  14.6 us
    ppermute x3, waiting for transfers between devices, per_device(): lax.ppermute(near, 'visit', along_y(d))  13.7 us
    pallas_call x1, Pallas kernels, make_model(): pl.pallas_call(kernel, out_shape=(jax.ShapeDtypeStruct((height, breadth),...  13.3 us
    all_to_all x1, starting transfers between devices, per_device(): arrived = lax.all_to_all(outgoing, 'patch', 0, 0, tiled=True)  10.1 us
    ppermute x8, starting transfers between devices, per_device(): other[d] = lax.ppermute(own[d], 'patch', neighbour)  9.18 us
    ppermute x7, waiting for transfers between devices, per_device(): own[d] = lax.ppermute(extra[d], 'patch', to_chip(d))  6.94 us
    ppermute x3, waiting for transfers between devices, per_device(): lax.ppermute(rows, 'visit', along_x(d))  5.56 us
    unnamed x30, local copies, waits for them, and re-layouts  5.3 us
  transfers between devices with their start and end apart: 22, of which 8 were waited for; matrix products, arithmetic and copies ran while one was open for 2% of the time, Pallas kernels for 18%

profile of v3, /device:TPU:1, one launch (start us, length us, event | category | flops | bytes accessed | tf_op | source)
XLA Modules:
  0.0 102.6 jit_solution(18411860628640817107)
XLA Ops:
  0.7 0.6 copy-done.4
  1.3 3.7 %pack_main.1 = bf16[16,272,256]{2,1,0:T(8,128)(2,1)} custom-call(s32[16]{0:T(128)} %bitcast.30, s32[16]{0:T(128)S(1)} %bitcast.22, s32[1]{0:T(128)} %bitcast.18.count, bf16[16,256,256]{2,1,0:T(8,128)(2,1)} %bitcast.23), custom_call_target="tpu_custom_call" | custom-call | tf_op jit(solution)/shard_map/pack_main/pallas_call | solution.py:118
  5.0 0.0 copy-start.9
  5.0 0.0 copy-start.12
  5.1 10.1 %all-to-all-start.1 = ((bf16[16,272,256]{2,1,0:T(8,128)(2,1)}), bf16[16,272,256]{2,1,0:T(8,128)(2,1)}, u32[]{:S(2)}, u32[]{:S(2)}) async-start(bf16[16,272,256]{2,1,0:T(8,128)(2,1)} %pack_main.1), calls=%async_computation.1 | async-start | bytes 4456448 | tf_op jit(solution)/shard_map/all_to_all | solution.py:410
  15.1 2.6 %collective-permute-start.2 = (bf16[32,1024]{1,0:T(8,128)(2,1)S(1)}, bf16[32,1024]{1,0:T(8,128)(2,1)S(1)}, u32[]{:S(2)}, u32[]{:S(2)}) collective-permute-start(bf16[32,1024]{1,0:T(8,128)(2,1)S(1)} %bitcast.26), channel_id=1, source_target_pairs={{0,3},{1,0},{2,1},{3,2},{4,7},{5,4},{6,5},{7,6},{8,11},{9,8},{10,9... | collective-permute-start | bytes 196616 | tf_op jit(solution)/shard_map/ppermute | solution.py:419
  17.7 0.5 collective-permute-start.1
  18.2 0.6 collective-permute-start
  18.8 0.2 collective-permute-done.2
  19.0 3.7 %collective-permute-done.1 = bf16[32,1024]{1,0:T(8,128)(2,1)S(1)} collective-permute-done((bf16[32,1024]{1,0:T(8,128)(2,1)S(1)}, bf16[32,1024]{1,0:T(8,128)(2,1)S(1)}, u32[]{:S(2)}, u32[]{:S(2)}) %collective-permute-start.1) | collective-permute-done | bytes 65568 | tf_op jit(solution)/shard_map/ppermute | solution.py:419
  22.7 1.6 %collective-permute-done = bf16[32,1024]{1,0:T(8,128)(2,1)S(1)} collective-permute-done((bf16[32,1024]{1,0:T(8,128)(2,1)S(1)}, bf16[32,1024]{1,0:T(8,128)(2,1)S(1)}, u32[]{:S(2)}, u32[]{:S(2)}) %collective-permute-start) | collective-permute-done | bytes 65568 | tf_op jit(solution)/shard_map/ppermute | solution.py:419
  24.4 2.9 %collective-permute-start.5 = (bf16[128,1024]{1,0:T(8,128)(2,1)S(1)}, bf16[128,1024]{1,0:T(8,128)(2,1)S(1)}, u32[]{:S(2)}, u32[]{:S(2)}) collective-permute-start(bf16[128,1024]{1,0:T(8,128)(2,1)S(1)} %pad_maximum_fusion.refs_0_), channel_id=1, source_target_pairs={{0,12},{1,13},{2,14},{3,15},{4,0},{5,1},{6,2},{7,3},{8,4},{9,5},{1... | collective-permute-start | bytes 786440 | tf_op jit(solution)/shard_map/ppermute | solution.py:421
  27.3 0.3 collective-permute-start.4
  27.6 0.7 collective-permute-start.3
  28.3 0.1 broadcast_multiply_fusion.refs_6_
  28.4 9.3 %collective-permute-done.5.refs_3_ = bf16[128,1024]{1,0:T(8,128)(2,1)S(1)} collective-permute-done((bf16[128,1024]{1,0:T(8,128)(2,1)S(1)}, bf16[128,1024]{1,0:T(8,128)(2,1)S(1)}, u32[]{:S(2)}, u32[]{:S(2)}) %collective-permute-start.5) | collective-permute-done | bytes 262176 | tf_op jit(solution)/shard_map/ppermute | solution.py:421
  37.7 0.7 copy-done
  38.4 4.4 %collective-permute-done.3.refs_1_ = bf16[128,1024]{1,0:T(8,128)(2,1)S(1)} collective-permute-done((bf16[128,1024]{1,0:T(8,128)(2,1)S(1)}, bf16[128,1024]{1,0:T(8,128)(2,1)S(1)}, u32[]{:S(2)}, u32[]{:S(2)}) %collective-permute-start.3) | collective-permute-done | bytes 262176 | tf_op jit(solution)/shard_map/ppermute | solution.py:421
  42.8 0.7 copy-done.2
  43.5 0.9 copy-done.1
  44.4 0.9 copy-done.3
  45.4 13.3 %model.1 = (f32[512,1024]{1,0:T(8,128)S(1)}, bf16[256,256]{1,0:T(8,128)(2,1)S(1)}, bf16[2,272,512]{2,1,0:T(8,128)(2,1)S(1)}) custom-call(bf16[128,1024]{1,0:T(8,128)(2,1)S(1)} %pad_maximum_fusion.refs_0_, bf16[128,1024]{1,0:T(8,128)(2,1)S(1)} %copy-done.3, bf16[128,1024]{1,0:T(8,128)(2,1)S(1)} %copy-done.1, ...), custom_call_target="tpu_custom_call" | custom-call | tf_op jit(solution)/shard_map/model/pallas_call | solution.py:240
  58.7 2.8 %pack_extra.1 = (bf16[256,256]{1,0:T(8,128)(2,1)S(1)}, bf16[256,256]{1,0:T(8,128)(2,1)}, bf16[256,256]{1,0:T(8,128)(2,1)}, bf16[256,256]{1,0:T(8,128)(2,1)S(1)},...) custom-call(s32[16]{0:T(128)S(1)} %bitcast.31, ...), custom_call_target="tpu_custom_call" | custom-call | tf_op jit(solution)/shard_map/pack_extra/pallas_call | solution.py:81
  61.6 0.7 copy-done.5
  62.2 0.7 copy-done.6
  62.9 0.8 collective-permute-start.6
  63.7 2.1 %collective-permute-start.7 = (bf16[256,256]{1,0:T(8,128)(2,1)}, bf16[256,256]{1,0:T(8,128)(2,1)S(1)}, u32[]{:S(2)}, u32[]{:S(2)}) collective-permute-start(bf16[256,256]{1,0:T(8,128)(2,1)} %get-tuple-element.41), channel_id=1, source_target_pairs={{0,64},{16,80},{32,96},{48,112},{64,128},{80,144},{96,160},{112,17... | collective-permute-start | bytes 393224 | tf_op jit(solution)/shard_map/ppermute | solution.py:445
  65.8 1.8 %collective-permute-start.10 = (bf16[256,256]{1,0:T(8,128)(2,1)}, bf16[256,256]{1,0:T(8,128)(2,1)S(1)}, u32[]{:S(2)}, u32[]{:S(2)}) collective-permute-start(bf16[256,256]{1,0:T(8,128)(2,1)} %get-tuple-element.47), channel_id=1, source_target_pairs={{0,160},{16,176},{32,192},{48,208},{64,224},{80,240},{96,0},{112,1... | collective-permute-start | bytes 393224 | tf_op jit(solution)/shard_map/ppermute | solution.py:445
  67.6 2.8 %collective-permute-start.11 = (bf16[256,256]{1,0:T(8,128)(2,1)}, bf16[256,256]{1,0:T(8,128)(2,1)S(1)}, u32[]{:S(2)}, u32[]{:S(2)}) collective-permute-start(bf16[256,256]{1,0:T(8,128)(2,1)} %get-tuple-element.49), channel_id=1, source_target_pairs={{0,192},{16,208},{32,224},{48,240},{64,0},{80,16},{96,32},{112,48}... | collective-permute-start | bytes 393224 | tf_op jit(solution)/shard_map/ppermute | solution.py:445
  70.4 1.4 %collective-permute-start.12 = (bf16[256,256]{1,0:T(8,128)(2,1)}, bf16[256,256]{1,0:T(8,128)(2,1)}, u32[]{:S(2)}, u32[]{:S(2)}) collective-permute-start(bf16[256,256]{1,0:T(8,128)(2,1)} %get-tuple-element.51), channel_id=1, source_target_pairs={{0,224},{16,240},{32,0},{48,16},{64,32},{80,48},{96,64},{112,80},{... | collective-permute-start | bytes 393224 | tf_op jit(solution)/shard_map/ppermute | solution.py:445
  71.8 0.8 slice_convert_fusion
  72.5 0.1 copy.14
  72.6 0.6 compare_reduce_fusion
  73.8 0.2 conditional.1
  74.1 2.3 %collective-permute-start.9 = (bf16[256,256]{1,0:T(8,128)(2,1)}, bf16[256,256]{1,0:T(8,128)(2,1)S(1)}, u32[]{:S(2)}, u32[]{:S(2)}) collective-permute-start(bf16[256,256]{1,0:T(8,128)(2,1)} %copy-done.6), channel_id=1, source_target_pairs={{0,128},{16,144},{32,160},{48,176},{64,192},{80,208},{96,224},{112... | collective-permute-start | bytes 393224 | tf_op jit(solution)/shard_map/ppermute | solution.py:445
  76.3 3.4 %collective-permute-start.8 = (bf16[256,256]{1,0:T(8,128)(2,1)}, bf16[256,256]{1,0:T(8,128)(2,1)S(1)}, u32[]{:S(2)}, u32[]{:S(2)}) collective-permute-start(bf16[256,256]{1,0:T(8,128)(2,1)} %copy-done.5), channel_id=1, source_target_pairs={{0,96},{16,112},{32,128},{48,144},{64,160},{80,176},{96,192},{112,... | collective-permute-start | bytes 393224 | tf_op jit(solution)/shard_map/ppermute | solution.py:445
  79.8 1.6 %collective-permute-start.13 = (bf16[256,256]{1,0:T(8,128)(2,1)S(1)}, bf16[256,256]{1,0:T(8,128)(2,1)S(1)}, u32[]{:S(2)}, u32[]{:S(2)}) collective-permute-start(bf16[256,256]{1,0:T(8,128)(2,1)S(1)} %get-tuple-element.38.refs_1_), channel_id=1, source_target_pairs={{0,16},{16,0},{32,48},{48,32},{64,80},{80,64},{96,112},{112,96},{1... | collective-permute-start | bytes 393224 | tf_op jit(solution)/shard_map/ppermute | solution.py:448
  81.4 3.7 %collective-permute-done.11.refs_7_ = bf16[256,256]{1,0:T(8,128)(2,1)S(1)} collective-permute-done((bf16[256,256]{1,0:T(8,128)(2,1)}, bf16[256,256]{1,0:T(8,128)(2,1)S(1)}, u32[]{:S(2)}, u32[]{:S(2)}) %collective-permute-start.11) | collective-permute-done | bytes 131104 | tf_op jit(solution)/shard_map/ppermute | solution.py:445
  85.1 0.6 collective-permute-start.14
  85.7 1.2 %collective-permute-done.12.refs_8_ = bf16[256,256]{1,0:T(8,128)(2,1)} collective-permute-done((bf16[256,256]{1,0:T(8,128)(2,1)}, bf16[256,256]{1,0:T(8,128)(2,1)}, u32[]{:S(2)}, u32[]{:S(2)}) %collective-permute-start.12) | collective-permute-done | bytes 131104 | tf_op jit(solution)/shard_map/ppermute | solution.py:445
  86.9 2.6 %collective-permute-start.15 = (bf16[256,256]{1,0:T(8,128)(2,1)S(1)}, bf16[256,256]{1,0:T(8,128)(2,1)S(1)}, u32[]{:S(2)}, u32[]{:S(2)}) collective-permute-start(bf16[256,256]{1,0:T(8,128)(2,1)S(1)} %collective-permute-done.7.refs_3_), channel_id=1, source_target_pairs={{0,16},{16,0},{32,48},{48,32},{64,80},{80,64},{96,112},{112,96},{1... | collective-permute-start | bytes 393224 | tf_op jit(solution)/shard_map/ppermute | solution.py:448
  89.4 2.1 %collective-permute-done.8.refs_4_ = bf16[256,256]{1,0:T(8,128)(2,1)S(1)} collective-permute-done((bf16[256,256]{1,0:T(8,128)(2,1)}, bf16[256,256]{1,0:T(8,128)(2,1)S(1)}, u32[]{:S(2)}, u32[]{:S(2)}) %collective-permute-start.8) | collective-permute-done | bytes 131104 | tf_op jit(solution)/shard_map/ppermute | solution.py:445
  91.5 3.3 %collective-permute-start.16 = (bf16[256,256]{1,0:T(8,128)(2,1)S(1)}, bf16[256,256]{1,0:T(8,128)(2,1)S(1)}, u32[]{:S(2)}, u32[]{:S(2)}) collective-permute-start(bf16[256,256]{1,0:T(8,128)(2,1)S(1)} %collective-permute-done.8.refs_4_), channel_id=1, source_target_pairs={{0,16},{16,0},{32,48},{48,32},{64,80},{80,64},{96,112},{112,96},{1... | collective-permute-start | bytes 393224 | tf_op jit(solution)/shard_map/ppermute | solution.py:448
  94.9 0.5 collective-permute-start.18
  95.4 0.1 collective-permute-start.19
  95.5 0.4 collective-permute-start.20
  95.9 2.4 %add_first.1.refs_18_ = f32[512,1024]{1,0:T(8,128)S(1)} custom-call(s32[16,8]{1,0:T(8,128)S(1)} %bitcast.20, bf16[16,272,256]{2,1,0:T(8,128)(2,1)} %all-to-all-done.1.blocks, f32[512,1024]{1,0:T(8,128)S(1)} %get-tuple-element.53.less), custom_call_target="tpu_custom_call" | custom-call | tf_op jit(solution)/shard_map/add_first/pallas_call | solution.py:285
  98.4 4.0 %finish.1 = f32[512,1024]{1,0:T(8,128)} custom-call(s32[16,8]{1,0:T(8,128)S(1)} %bitcast.21, bf16[256,256]{1,0:T(8,128)(2,1)S(1)} %get-tuple-element.38.refs_1_, bf16[256,256]{1,0:T(8,128)(2,1)S(1)} %collective-permute-done.6.refs_2_, bf16[256,256]{1,0:T(8,128)(2,1)S(1)} %collective-permute-done.7.refs_3_, ...), custom_call_target="tpu_custom_call" | custom-call | tf_op jit(solution)/shard_map/finish/pallas_call | solution.py:368
  (40 shorter events, 0.1 us)
Async XLA Ops:
  0.7 0.7 copy-start.4
  5.0 10.1 %copy-start.8 = (bf16[1,32,1024]{2,1,0:T(8,128)(2,1)S(1)}, bf16[1,32,1024]{2,1,0:T(8,128)(2,1)}, u32[]{:S(2)}) copy-start(bf16[1,32,1024]{2,1,0:T(8,128)(2,1)} %param.16) | copy-start | bytes 196612
  5.0 23.3 %copy-start.13 = (bf16[1,2,25]{2,1,0:T(2,128)(2,1)S(1)}, bf16[1,2,25]{2,1,0:T(2,128)(2,1)}, u32[]{:S(2)}) copy-start(bf16[1,2,25]{2,1,0:T(2,128)(2,1)} %param.21) | copy-start | bytes 304
  5.0 23.3 %copy-start.14 = (bf16[1,2,25]{2,1,0:T(2,128)(2,1)S(1)}, bf16[1,2,25]{2,1,0:T(2,128)(2,1)}, u32[]{:S(2)}) copy-start(bf16[1,2,25]{2,1,0:T(2,128)(2,1)} %param.20) | copy-start | bytes 304
  5.0 23.3 %copy-start.11 = (bf16[9,21]{1,0:T(8,128)(2,1)S(1)}, bf16[9,21]{1,0:T(8,128)(2,1)}, u32[]{:S(2)}) copy-start(bf16[9,21]{1,0:T(8,128)(2,1)} %param.17) | copy-start | bytes 1138
  5.0 23.3 %copy-start.9 = (f32[9,21]{1,0:T(8,128)S(1)}, f32[9,21]{1,0:T(8,128)}, u32[]{:S(2)}) copy-start(f32[9,21]{1,0:T(8,128)} %param.18) | copy-start | bytes 2272
  5.0 23.3 %copy-start.12 = (f32[1,9]{1,0:T(1,128)S(1)}, f32[1,9]{1,0:T(1,128)}, u32[]{:S(2)}) copy-start(f32[1,9]{1,0:T(1,128)} %param.19) | copy-start | bytes 112
  5.0 53.7 %copy-start.10 = (s32[1,1,16,1]{2,3,1,0:T(1,128)S(1)}, s32[1,1,16,1]{2,3,1,0:T(1,128)}, u32[]{:S(2)}) copy-start(s32[1,1,16,1]{2,3,1,0:T(1,128)} %param.13) | copy-start | bytes 196
  5.1 66.7 %all-to-all-start.1 = ((bf16[16,272,256]{2,1,0:T(8,128)(2,1)}), bf16[16,272,256]{2,1,0:T(8,128)(2,1)}, u32[]{:S(2)}, u32[]{:S(2)}) async-start(bf16[16,272,256]{2,1,0:T(8,128)(2,1)} %pack_main.1), calls=%async_computation.1 | async-start | bytes 4456448 | tf_op jit(solution)/shard_map/all_to_all | solution.py:410
  15.1 3.9 %collective-permute-start.2 = (bf16[32,1024]{1,0:T(8,128)(2,1)S(1)}, bf16[32,1024]{1,0:T(8,128)(2,1)S(1)}, u32[]{:S(2)}, u32[]{:S(2)}) collective-permute-start(bf16[32,1024]{1,0:T(8,128)(2,1)S(1)} %bitcast.26), channel_id=1, source_target_pairs={{0,3},{1,0},{2,1},{3,2},{4,7},{5,4},{6,5},{7,6},{8,11},{9,8},{10,9... | collective-permute-start | bytes 196616 | tf_op jit(solution)/shard_map/ppermute | solution.py:419
  17.7 5.0 %collective-permute-start.1 = (bf16[32,1024]{1,0:T(8,128)(2,1)S(1)}, bf16[32,1024]{1,0:T(8,128)(2,1)S(1)}, u32[]{:S(2)}, u32[]{:S(2)}) collective-permute-start(bf16[32,1024]{1,0:T(8,128)(2,1)S(1)} %bitcast.27), channel_id=1, source_target_pairs={{0,2},{1,3},{2,0},{3,1},{4,6},{5,7},{6,4},{7,5},{8,10},{9,11},{10,... | collective-permute-start | bytes 196616 | tf_op jit(solution)/shard_map/ppermute | solution.py:419
  18.2 6.2 %collective-permute-start = (bf16[32,1024]{1,0:T(8,128)(2,1)S(1)}, bf16[32,1024]{1,0:T(8,128)(2,1)S(1)}, u32[]{:S(2)}, u32[]{:S(2)}) collective-permute-start(bf16[32,1024]{1,0:T(8,128)(2,1)S(1)} %bitcast.28), channel_id=1, source_target_pairs={{0,1},{1,2},{2,3},{3,0},{4,5},{5,6},{6,7},{7,4},{8,9},{9,10},{10,1... | collective-permute-start | bytes 196616 | tf_op jit(solution)/shard_map/ppermute | solution.py:419
  24.4 13.3 %collective-permute-start.5 = (bf16[128,1024]{1,0:T(8,128)(2,1)S(1)}, bf16[128,1024]{1,0:T(8,128)(2,1)S(1)}, u32[]{:S(2)}, u32[]{:S(2)}) collective-permute-start(bf16[128,1024]{1,0:T(8,128)(2,1)S(1)} %pad_maximum_fusion.refs_0_), channel_id=1, source_target_pairs={{0,12},{1,13},{2,14},{3,15},{4,0},{5,1},{6,2},{7,3},{8,4},{9,5},{1... | collective-permute-start | bytes 786440 | tf_op jit(solution)/shard_map/ppermute | solution.py:421
  27.3 10.4 %collective-permute-start.4 = (bf16[128,1024]{1,0:T(8,128)(2,1)S(1)}, bf16[128,1024]{1,0:T(8,128)(2,1)S(1)}, u32[]{:S(2)}, u32[]{:S(2)}) collective-permute-start(bf16[128,1024]{1,0:T(8,128)(2,1)S(1)} %pad_maximum_fusion.refs_0_), channel_id=1, source_target_pairs={{0,8},{1,9},{2,10},{3,11},{4,12},{5,13},{6,14},{7,15},{8,0},{9,1},... | collective-permute-start | bytes 786440 | tf_op jit(solution)/shard_map/ppermute | solution.py:421
  27.6 15.2 %collective-permute-start.3 = (bf16[128,1024]{1,0:T(8,128)(2,1)S(1)}, bf16[128,1024]{1,0:T(8,128)(2,1)S(1)}, u32[]{:S(2)}, u32[]{:S(2)}) collective-permute-start(bf16[128,1024]{1,0:T(8,128)(2,1)S(1)} %pad_maximum_fusion.refs_0_), channel_id=1, source_target_pairs={{0,4},{1,5},{2,6},{3,7},{4,8},{5,9},{6,10},{7,11},{8,12},{9,13},{1... | collective-permute-start | bytes 786440 | tf_op jit(solution)/shard_map/ppermute | solution.py:421
  37.7 0.7 copy-start
  42.8 0.7 copy-start.2
  43.5 0.9 copy-start.1
  44.4 0.9 copy-start.3
  61.6 0.7 copy-start.5
  62.2 0.7 copy-start.6
  62.9 13.5 %collective-permute-start.6 = (bf16[256,256]{1,0:T(8,128)(2,1)}, bf16[256,256]{1,0:T(8,128)(2,1)S(1)}, u32[]{:S(2)}, u32[]{:S(2)}) collective-permute-start(bf16[256,256]{1,0:T(8,128)(2,1)} %get-tuple-element.39), channel_id=1, source_target_pairs={{0,32},{16,48},{32,64},{48,80},{64,96},{80,112},{96,128},{112,144}... | collective-permute-start | bytes 393224 | tf_op jit(solution)/shard_map/ppermute | solution.py:445
  63.7 10.4 %collective-permute-start.7 = (bf16[256,256]{1,0:T(8,128)(2,1)}, bf16[256,256]{1,0:T(8,128)(2,1)S(1)}, u32[]{:S(2)}, u32[]{:S(2)}) collective-permute-start(bf16[256,256]{1,0:T(8,128)(2,1)} %get-tuple-element.41), channel_id=1, source_target_pairs={{0,64},{16,80},{32,96},{48,112},{64,128},{80,144},{96,160},{112,17... | collective-permute-start | bytes 393224 | tf_op jit(solution)/shard_map/ppermute | solution.py:445
  65.8 14.0 %collective-permute-start.10 = (bf16[256,256]{1,0:T(8,128)(2,1)}, bf16[256,256]{1,0:T(8,128)(2,1)S(1)}, u32[]{:S(2)}, u32[]{:S(2)}) collective-permute-start(bf16[256,256]{1,0:T(8,128)(2,1)} %get-tuple-element.47), channel_id=1, source_target_pairs={{0,160},{16,176},{32,192},{48,208},{64,224},{80,240},{96,0},{112,1... | collective-permute-start | bytes 393224 | tf_op jit(solution)/shard_map/ppermute | solution.py:445
  67.6 17.4 %collective-permute-start.11 = (bf16[256,256]{1,0:T(8,128)(2,1)}, bf16[256,256]{1,0:T(8,128)(2,1)S(1)}, u32[]{:S(2)}, u32[]{:S(2)}) collective-permute-start(bf16[256,256]{1,0:T(8,128)(2,1)} %get-tuple-element.49), channel_id=1, source_target_pairs={{0,192},{16,208},{32,224},{48,240},{64,0},{80,16},{96,32},{112,48}... | collective-permute-start | bytes 393224 | tf_op jit(solution)/shard_map/ppermute | solution.py:445
  70.4 16.5 %collective-permute-start.12 = (bf16[256,256]{1,0:T(8,128)(2,1)}, bf16[256,256]{1,0:T(8,128)(2,1)}, u32[]{:S(2)}, u32[]{:S(2)}) collective-permute-start(bf16[256,256]{1,0:T(8,128)(2,1)} %get-tuple-element.51), channel_id=1, source_target_pairs={{0,224},{16,240},{32,0},{48,16},{64,32},{80,48},{96,64},{112,80},{... | collective-permute-start | bytes 393224 | tf_op jit(solution)/shard_map/ppermute | solution.py:445
  74.1 15.4 %collective-permute-start.9 = (bf16[256,256]{1,0:T(8,128)(2,1)}, bf16[256,256]{1,0:T(8,128)(2,1)S(1)}, u32[]{:S(2)}, u32[]{:S(2)}) collective-permute-start(bf16[256,256]{1,0:T(8,128)(2,1)} %copy-done.6), channel_id=1, source_target_pairs={{0,128},{16,144},{32,160},{48,176},{64,192},{80,208},{96,224},{112... | collective-permute-start | bytes 393224 | tf_op jit(solution)/shard_map/ppermute | solution.py:445
  76.3 15.2 %collective-permute-start.8 = (bf16[256,256]{1,0:T(8,128)(2,1)}, bf16[256,256]{1,0:T(8,128)(2,1)S(1)}, u32[]{:S(2)}, u32[]{:S(2)}) collective-permute-start(bf16[256,256]{1,0:T(8,128)(2,1)} %copy-done.5), channel_id=1, source_target_pairs={{0,96},{16,112},{32,128},{48,144},{64,160},{80,176},{96,192},{112,... | collective-permute-start | bytes 393224 | tf_op jit(solution)/shard_map/ppermute | solution.py:445
  79.8 15.1 %collective-permute-start.13 = (bf16[256,256]{1,0:T(8,128)(2,1)S(1)}, bf16[256,256]{1,0:T(8,128)(2,1)S(1)}, u32[]{:S(2)}, u32[]{:S(2)}) collective-permute-start(bf16[256,256]{1,0:T(8,128)(2,1)S(1)} %get-tuple-element.38.refs_1_), channel_id=1, source_target_pairs={{0,16},{16,0},{32,48},{48,32},{64,80},{80,64},{96,112},{112,96},{1... | collective-permute-start | bytes 393224 | tf_op jit(solution)/shard_map/ppermute | solution.py:448
  85.1 10.3 %collective-permute-start.14 = (bf16[256,256]{1,0:T(8,128)(2,1)S(1)}, bf16[256,256]{1,0:T(8,128)(2,1)S(1)}, u32[]{:S(2)}, u32[]{:S(2)}) collective-permute-start(bf16[256,256]{1,0:T(8,128)(2,1)S(1)} %collective-permute-done.6.refs_2_), channel_id=1, source_target_pairs={{0,16},{16,0},{32,48},{48,32},{64,80},{80,64},{96,112},{112,96},{1... | collective-permute-start | bytes 393224 | tf_op jit(solution)/shard_map/ppermute | solution.py:448
  86.9 8.6 %collective-permute-start.15 = (bf16[256,256]{1,0:T(8,128)(2,1)S(1)}, bf16[256,256]{1,0:T(8,128)(2,1)S(1)}, u32[]{:S(2)}, u32[]{:S(2)}) collective-permute-start(bf16[256,256]{1,0:T(8,128)(2,1)S(1)} %collective-permute-done.7.refs_3_), channel_id=1, source_target_pairs={{0,16},{16,0},{32,48},{48,32},{64,80},{80,64},{96,112},{112,96},{1... | collective-permute-start | bytes 393224 | tf_op jit(solution)/shard_map/ppermute | solution.py:448
  91.5 6.8 %collective-permute-start.16 = (bf16[256,256]{1,0:T(8,128)(2,1)S(1)}, bf16[256,256]{1,0:T(8,128)(2,1)S(1)}, u32[]{:S(2)}, u32[]{:S(2)}) collective-permute-start(bf16[256,256]{1,0:T(8,128)(2,1)S(1)} %collective-permute-done.8.refs_4_), channel_id=1, source_target_pairs={{0,16},{16,0},{32,48},{48,32},{64,80},{80,64},{96,112},{112,96},{1... | collective-permute-start | bytes 393224 | tf_op jit(solution)/shard_map/ppermute | solution.py:448
  94.9 3.5 %collective-permute-start.17 = (bf16[256,256]{1,0:T(8,128)(2,1)S(1)}, bf16[256,256]{1,0:T(8,128)(2,1)S(1)}, u32[]{:S(2)}, u32[]{:S(2)}) collective-permute-start(bf16[256,256]{1,0:T(8,128)(2,1)S(1)} %collective-permute-done.9.refs_5_), channel_id=1, source_target_pairs={{0,16},{16,0},{32,48},{48,32},{64,80},{80,64},{96,112},{112,96},{1... | collective-permute-start | bytes 393224 | tf_op jit(solution)/shard_map/ppermute | solution.py:448
  94.9 3.5 %collective-permute-start.18 = (bf16[256,256]{1,0:T(8,128)(2,1)S(1)}, bf16[256,256]{1,0:T(8,128)(2,1)S(1)}, u32[]{:S(2)}, u32[]{:S(2)}) collective-permute-start(bf16[256,256]{1,0:T(8,128)(2,1)S(1)} %collective-permute-done.10.refs_6_), channel_id=1, source_target_pairs={{0,16},{16,0},{32,48},{48,32},{64,80},{80,64},{96,112},{112,96},{1... | collective-permute-start | bytes 393224 | tf_op jit(solution)/shard_map/ppermute | solution.py:448
  95.4 3.0 %collective-permute-start.19 = (bf16[256,256]{1,0:T(8,128)(2,1)S(1)}, bf16[256,256]{1,0:T(8,128)(2,1)S(1)}, u32[]{:S(2)}, u32[]{:S(2)}) collective-permute-start(bf16[256,256]{1,0:T(8,128)(2,1)S(1)} %collective-permute-done.11.refs_7_), channel_id=1, source_target_pairs={{0,16},{16,0},{32,48},{48,32},{64,80},{80,64},{96,112},{112,96},{1... | collective-permute-start | bytes 393224 | tf_op jit(solution)/shard_map/ppermute | solution.py:448
  95.5 2.9 %collective-permute-start.20 = (bf16[256,256]{1,0:T(8,128)(2,1)}, bf16[256,256]{1,0:T(8,128)(2,1)S(1)}, u32[]{:S(2)}, u32[]{:S(2)}) collective-permute-start(bf16[256,256]{1,0:T(8,128)(2,1)} %collective-permute-done.12.refs_8_), channel_id=1, source_target_pairs={{0,16},{16,0},{32,48},{48,32},{64,80},{80,64},{96,112},{112,96},{1... | collective-permute-start | bytes 393224 | tf_op jit(solution)/shard_map/ppermute | solution.py:448
  95.9 2.5 %copy-start.7 = (bf16[16,256,256]{2,1,0:T(8,128)(2,1)S(1)}, bf16[16,256,256]{2,1,0:T(8,128)(2,1)}, u32[]{:S(2)}) copy-start(bf16[16,256,256]{2,1,0:T(8,128)(2,1)} %get-tuple-element.57.refs_17_) | copy-start | bytes 6291460

commit v4 on v3

--- a/solution.py
+++ b/solution.py
@@ -441,10 +441,14 @@
     neighbour = [(i, i ^ 1) for i in range(n_patch)]
     own, other = list(extra), [None] * chips
     near_last = sorted(range(1, chips), key=lambda d: -min(d, chips - d))
-    for d in near_last:
+    early, last = near_last[:-2], near_last[-2:]
+    for d in early:
         own[d] = lax.ppermute(extra[d], "patch", to_chip(d))
-    for d in [0] + near_last:
-        own[d], _ = lax.optimization_barrier((own[d], second))
+    for d in last:
+        waiting, _ = lax.optimization_barrier((extra[d], second))
+        own[d] = lax.ppermute(waiting, "patch", to_chip(d))
+    for d in [0] + early + last:
+        own[d], _ = lax.optimization_barrier((own[d], total if d in last else second))
         other[d] = lax.ppermute(own[d], "patch", neighbour)
     filtered = finish(notes, own, other, second, total, col_table, row_table)
     return filtered[None, None]

time: 103 us -> 104 us (level)
  waiting for transfers between devices: 26.2 us -> 30.2 us
  starting transfers between devices: 41.4 us -> 38 us
    ppermute x8, starting transfers between devices: 9.18 us -> 5.11 us  [per_device(): other[d] = lax.ppermute(own[d], 'patch', neighbour)]
    ppermute x7 -> x5, waiting for transfers between devices: 6.94 us -> 9.78 us  [per_device(): own[d] = lax.ppermute(extra[d], 'patch', to_chip(d))]
    ppermute x0 -> x2, starting transfers between devices: none -> 2.68 us  [per_device(): own[d] = lax.ppermute(waiting, 'patch', to_chip(d))]
    ppermute x7 -> x5, starting transfers between devices: 14.6 us -> 12.7 us  [per_device(): own[d] = lax.ppermute(extra[d], 'patch', to_chip(d))]
    ppermute x8, waiting for transfers between devices: 0.02 us -> 1.25 us  [per_device(): other[d] = lax.ppermute(own[d], 'patch', neighbour)]
  transfers between devices with their start and end apart: 22 -> 22, of which waited for: 8 -> 12; matrix products, arithmetic and copies ran while one was open for 2% -> 2% of each run, Pallas kernels for 18% -> 18%
where the time goes in v4:
time: 104 us; the launch traced here: 103 us
  starting transfers between devices  38 us (37%)
  waiting for transfers between devices  30.2 us (29%)
  Pallas kernels  26.5 us (25%)
  local copies, waits for them, and re-layouts  5.36 us (5%)
  between operations  1.57 us (2%)
  other arithmetic  1.5 us (1%)
    ppermute x3, waiting for transfers between devices, per_device(): lax.ppermute(near, 'visit', along_y(d))  13.5 us
    pallas_call x1, Pallas kernels, make_model(): pl.pallas_call(kernel, out_shape=(jax.ShapeDtypeStruct((height, breadth),...  13.3 us
    ppermute x5, starting transfers between devices, per_device(): own[d] = lax.ppermute(extra[d], 'patch', to_chip(d))  12.7 us
    all_to_all x1, starting transfers between devices, per_device(): arrived = lax.all_to_all(outgoing, 'patch', 0, 0, tiled=True)  10 us
    ppermute x5, waiting for transfers between devices, per_device(): own[d] = lax.ppermute(extra[d], 'patch', to_chip(d))  9.78 us
    ppermute x3, waiting for transfers between devices, per_device(): lax.ppermute(rows, 'visit', along_x(d))  5.65 us
    unnamed x30, local copies, waits for them, and re-layouts  5.28 us
    ppermute x8, starting transfers between devices, per_device(): other[d] = lax.ppermute(own[d], 'patch', neighbour)  5.11 us
  transfers between devices with their start and end apart: 22, of which 12 were waited for; matrix products, arithmetic and copies ran while one was open for 2% of the time, Pallas kernels for 18%

profile of v4, /device:TPU:1, one launch (start us, length us, event | category | flops | bytes accessed | tf_op | source)
XLA Modules:
  0.0 103.4 jit_solution(2261731969709211894)
XLA Ops:
  0.7 0.6 copy-done.4
  1.3 3.8 %pack_main.1 = bf16[16,272,256]{2,1,0:T(8,128)(2,1)} custom-call(s32[16]{0:T(128)} %bitcast.30, s32[16]{0:T(128)S(1)} %bitcast.22, s32[1]{0:T(128)} %bitcast.18.count, bf16[16,256,256]{2,1,0:T(8,128)(2,1)} %bitcast.23), custom_call_target="tpu_custom_call" | custom-call | tf_op jit(solution)/shard_map/pack_main/pallas_call | solution.py:118
  5.1 10.0 %all-to-all-start.1 = ((bf16[16,272,256]{2,1,0:T(8,128)(2,1)}), bf16[16,272,256]{2,1,0:T(8,128)(2,1)}, u32[]{:S(2)}, u32[]{:S(2)}) async-start(bf16[16,272,256]{2,1,0:T(8,128)(2,1)} %pack_main.1), calls=%async_computation.1 | async-start | bytes 4456448 | tf_op jit(solution)/shard_map/all_to_all | solution.py:410
  15.2 2.6 %collective-permute-start.2 = (bf16[32,1024]{1,0:T(8,128)(2,1)S(1)}, bf16[32,1024]{1,0:T(8,128)(2,1)S(1)}, u32[]{:S(2)}, u32[]{:S(2)}) collective-permute-start(bf16[32,1024]{1,0:T(8,128)(2,1)S(1)} %bitcast.26), channel_id=1, source_target_pairs={{0,3},{1,0},{2,1},{3,2},{4,7},{5,4},{6,5},{7,6},{8,11},{9,8},{10,9... | collective-permute-start | bytes 196616 | tf_op jit(solution)/shard_map/ppermute | solution.py:419
  17.8 0.4 collective-permute-start.1
  18.2 0.6 collective-permute-start
  18.8 0.3 collective-permute-done.2
  19.1 3.7 %collective-permute-done.1 = bf16[32,1024]{1,0:T(8,128)(2,1)S(1)} collective-permute-done((bf16[32,1024]{1,0:T(8,128)(2,1)S(1)}, bf16[32,1024]{1,0:T(8,128)(2,1)S(1)}, u32[]{:S(2)}, u32[]{:S(2)}) %collective-permute-start.1) | collective-permute-done | bytes 65568 | tf_op jit(solution)/shard_map/ppermute | solution.py:419
  22.8 1.7 %collective-permute-done = bf16[32,1024]{1,0:T(8,128)(2,1)S(1)} collective-permute-done((bf16[32,1024]{1,0:T(8,128)(2,1)S(1)}, bf16[32,1024]{1,0:T(8,128)(2,1)S(1)}, u32[]{:S(2)}, u32[]{:S(2)}) %collective-permute-start) | collective-permute-done | bytes 65568 | tf_op jit(solution)/shard_map/ppermute | solution.py:419
  24.5 2.7 %collective-permute-start.5 = (bf16[128,1024]{1,0:T(8,128)(2,1)S(1)}, bf16[128,1024]{1,0:T(8,128)(2,1)S(1)}, u32[]{:S(2)}, u32[]{:S(2)}) collective-permute-start(bf16[128,1024]{1,0:T(8,128)(2,1)S(1)} %pad_maximum_fusion.refs_0_), channel_id=1, source_target_pairs={{0,12},{1,13},{2,14},{3,15},{4,0},{5,1},{6,2},{7,3},{8,4},{9,5},{1... | collective-permute-start | bytes 786440 | tf_op jit(solution)/shard_map/ppermute | solution.py:421
  27.2 0.4 collective-permute-start.4
  27.6 0.8 collective-permute-start.3
  28.5 4.6 %collective-permute-done.5.refs_3_ = bf16[128,1024]{1,0:T(8,128)(2,1)S(1)} collective-permute-done((bf16[128,1024]{1,0:T(8,128)(2,1)S(1)}, bf16[128,1024]{1,0:T(8,128)(2,1)S(1)}, u32[]{:S(2)}, u32[]{:S(2)}) %collective-permute-start.5) | collective-permute-done | bytes 262176 | tf_op jit(solution)/shard_map/ppermute | solution.py:421
  33.1 2.6 %collective-permute-done.4.refs_2_ = bf16[128,1024]{1,0:T(8,128)(2,1)S(1)} collective-permute-done((bf16[128,1024]{1,0:T(8,128)(2,1)S(1)}, bf16[128,1024]{1,0:T(8,128)(2,1)S(1)}, u32[]{:S(2)}, u32[]{:S(2)}) %collective-permute-start.4) | collective-permute-done | bytes 262176 | tf_op jit(solution)/shard_map/ppermute | solution.py:421
  35.7 0.7 copy-done
  36.3 6.3 %collective-permute-done.3.refs_1_ = bf16[128,1024]{1,0:T(8,128)(2,1)S(1)} collective-permute-done((bf16[128,1024]{1,0:T(8,128)(2,1)S(1)}, bf16[128,1024]{1,0:T(8,128)(2,1)S(1)}, u32[]{:S(2)}, u32[]{:S(2)}) %collective-permute-start.3) | collective-permute-done | bytes 262176 | tf_op jit(solution)/shard_map/ppermute | solution.py:421
  42.7 0.7 copy-done.2
  43.4 0.9 copy-done.1
  44.4 0.9 copy-done.3
  45.3 13.3 %model.1 = (f32[512,1024]{1,0:T(8,128)S(1)}, bf16[256,256]{1,0:T(8,128)(2,1)S(1)}, bf16[2,272,512]{2,1,0:T(8,128)(2,1)S(1)}) custom-call(bf16[128,1024]{1,0:T(8,128)(2,1)S(1)} %pad_maximum_fusion.refs_0_, bf16[128,1024]{1,0:T(8,128)(2,1)S(1)} %copy-done.3, bf16[128,1024]{1,0:T(8,128)(2,1)S(1)} %copy-done.1, ...), custom_call_target="tpu_custom_call" | custom-call | tf_op jit(solution)/shard_map/model/pallas_call | solution.py:240
  58.7 2.9 %pack_extra.1 = (bf16[256,256]{1,0:T(8,128)(2,1)S(1)}, bf16[256,256]{1,0:T(8,128)(2,1)S(1)}, bf16[256,256]{1,0:T(8,128)(2,1)}, bf16[256,256]{1,0:T(8,128)(2,1)},...) custom-call(s32[16]{0:T(128)S(1)} %bitcast.31, ...), custom_call_target="tpu_custom_call" | custom-call | tf_op jit(solution)/shard_map/pack_extra/pallas_call | solution.py:81
  61.5 0.6 copy-done.5
  62.2 0.7 copy-done.6
  62.8 1.4 %collective-permute-start.7 = (bf16[256,256]{1,0:T(8,128)(2,1)}, bf16[256,256]{1,0:T(8,128)(2,1)S(1)}, u32[]{:S(2)}, u32[]{:S(2)}) collective-permute-start(bf16[256,256]{1,0:T(8,128)(2,1)} %get-tuple-element.45), channel_id=1, source_target_pairs={{0,64},{16,80},{32,96},{48,112},{64,128},{80,144},{96,160},{112,17... | collective-permute-start | bytes 393224 | tf_op jit(solution)/shard_map/ppermute | solution.py:446
  64.3 3.4 %collective-permute-start.8 = (bf16[256,256]{1,0:T(8,128)(2,1)}, bf16[256,256]{1,0:T(8,128)(2,1)S(1)}, u32[]{:S(2)}, u32[]{:S(2)}) collective-permute-start(bf16[256,256]{1,0:T(8,128)(2,1)} %get-tuple-element.47), channel_id=1, source_target_pairs={{0,96},{16,112},{32,128},{48,144},{64,160},{80,176},{96,192},{112,... | collective-permute-start | bytes 393224 | tf_op jit(solution)/shard_map/ppermute | solution.py:446
  67.7 1.1 %collective-permute-start.9 = (bf16[256,256]{1,0:T(8,128)(2,1)}, bf16[256,256]{1,0:T(8,128)(2,1)S(1)}, u32[]{:S(2)}, u32[]{:S(2)}) collective-permute-start(bf16[256,256]{1,0:T(8,128)(2,1)} %get-tuple-element.49), channel_id=1, source_target_pairs={{0,128},{16,144},{32,160},{48,176},{64,192},{80,208},{96,224},{112... | collective-permute-start | bytes 393224 | tf_op jit(solution)/shard_map/ppermute | solution.py:446
  68.8 3.2 %collective-permute-start.10 = (bf16[256,256]{1,0:T(8,128)(2,1)}, bf16[256,256]{1,0:T(8,128)(2,1)S(1)}, u32[]{:S(2)}, u32[]{:S(2)}) collective-permute-start(bf16[256,256]{1,0:T(8,128)(2,1)} %get-tuple-element.51), channel_id=1, source_target_pairs={{0,160},{16,176},{32,192},{48,208},{64,224},{80,240},{96,0},{112,1... | collective-permute-start | bytes 393224 | tf_op jit(solution)/shard_map/ppermute | solution.py:446
  72.0 3.5 %collective-permute-start.11 = (bf16[256,256]{1,0:T(8,128)(2,1)}, bf16[256,256]{1,0:T(8,128)(2,1)}, u32[]{:S(2)}, u32[]{:S(2)}) collective-permute-start(bf16[256,256]{1,0:T(8,128)(2,1)} %get-tuple-element.53), channel_id=1, source_target_pairs={{0,192},{16,208},{32,224},{48,240},{64,0},{80,16},{96,32},{112,48}... | collective-permute-start | bytes 393224 | tf_op jit(solution)/shard_map/ppermute | solution.py:446
  75.5 0.8 slice_convert_fusion
  76.3 0.6 compare_reduce_fusion
  77.5 0.2 conditional.1
  77.8 6.3 %collective-permute-done.8.refs_4_ = bf16[256,256]{1,0:T(8,128)(2,1)S(1)} collective-permute-done((bf16[256,256]{1,0:T(8,128)(2,1)}, bf16[256,256]{1,0:T(8,128)(2,1)S(1)}, u32[]{:S(2)}, u32[]{:S(2)}) %collective-permute-start.8) | collective-permute-done | bytes 131104 | tf_op jit(solution)/shard_map/ppermute | solution.py:446
  84.1 2.7 %collective-permute-start.12 = (bf16[256,256]{1,0:T(8,128)(2,1)}, bf16[256,256]{1,0:T(8,128)(2,1)S(1)}, u32[]{:S(2)}, u32[]{:S(2)}) collective-permute-start(bf16[256,256]{1,0:T(8,128)(2,1)} %copy-done.5), channel_id=1, source_target_pairs={{0,224},{16,240},{32,0},{48,16},{64,32},{80,48},{96,64},{112,80},{... | collective-permute-start | bytes 393224 | tf_op jit(solution)/shard_map/ppermute | solution.py:449
  86.8 1.5 %collective-permute-start.13 = (bf16[256,256]{1,0:T(8,128)(2,1)S(1)}, bf16[256,256]{1,0:T(8,128)(2,1)S(1)}, u32[]{:S(2)}, u32[]{:S(2)}) collective-permute-start(bf16[256,256]{1,0:T(8,128)(2,1)S(1)} %get-tuple-element.40.refs_1_), channel_id=1, source_target_pairs={{0,16},{16,0},{32,48},{48,32},{64,80},{80,64},{96,112},{112,96},{1... | collective-permute-start | bytes 393224 | tf_op jit(solution)/shard_map/ppermute | solution.py:452
  88.3 1.8 %collective-permute-start.15 = (bf16[256,256]{1,0:T(8,128)(2,1)S(1)}, bf16[256,256]{1,0:T(8,128)(2,1)S(1)}, u32[]{:S(2)}, u32[]{:S(2)}) collective-permute-start(bf16[256,256]{1,0:T(8,128)(2,1)S(1)} %collective-permute-done.7.refs_3_), channel_id=1, source_target_pairs={{0,16},{16,0},{32,48},{48,32},{64,80},{80,64},{96,112},{112,96},{1... | collective-permute-start | bytes 393224 | tf_op jit(solution)/shard_map/ppermute | solution.py:452
  90.1 3.5 %collective-permute-done.11.refs_7_ = bf16[256,256]{1,0:T(8,128)(2,1)} collective-permute-done((bf16[256,256]{1,0:T(8,128)(2,1)}, bf16[256,256]{1,0:T(8,128)(2,1)}, u32[]{:S(2)}, u32[]{:S(2)}) %collective-permute-start.11) | collective-permute-done | bytes 131104 | tf_op jit(solution)/shard_map/ppermute | solution.py:446
  93.6 0.6 collective-permute-start.16
  94.2 2.5 %add_first.1.refs_18_ = f32[512,1024]{1,0:T(8,128)S(1)} custom-call(s32[16,8]{1,0:T(8,128)S(1)} %bitcast.20, bf16[16,272,256]{2,1,0:T(8,128)(2,1)} %all-to-all-done.1.blocks, f32[512,1024]{1,0:T(8,128)S(1)} %get-tuple-element.43.less), custom_call_target="tpu_custom_call" | custom-call | tf_op jit(solution)/shard_map/add_first/pallas_call | solution.py:285
  96.7 0.1 collective-permute-start.17
  96.9 0.5 collective-permute-start.18
  97.3 0.1 collective-permute-start.19
  97.5 0.4 collective-permute-start.14
  97.9 0.1 collective-permute-start.20
  98.0 0.2 collective-permute-done.17.refs_13_
  98.2 0.2 collective-permute-done.18.refs_14_
  98.4 0.5 collective-permute-done.19.refs_15_
  98.9 0.3 collective-permute-done.20.refs_16_
  99.2 4.0 %finish.1 = f32[512,1024]{1,0:T(8,128)} custom-call(s32[16,8]{1,0:T(8,128)S(1)} %bitcast.21, bf16[256,256]{1,0:T(8,128)(2,1)S(1)} %get-tuple-element.40.refs_1_, bf16[256,256]{1,0:T(8,128)(2,1)S(1)} %collective-permute-done.6.refs_2_, bf16[256,256]{1,0:T(8,128)(2,1)S(1)} %collective-permute-done.7.refs_3_, ...), custom_call_target="tpu_custom_call" | custom-call | tf_op jit(solution)/shard_map/finish/pallas_call | solution.py:368
  (40 shorter events, 0.2 us)
Async XLA Ops:
  0.7 0.7 copy-start.4
  5.1 10.1 %copy-start.8 = (bf16[1,32,1024]{2,1,0:T(8,128)(2,1)S(1)}, bf16[1,32,1024]{2,1,0:T(8,128)(2,1)}, u32[]{:S(2)}) copy-start(bf16[1,32,1024]{2,1,0:T(8,128)(2,1)} %param.16) | copy-start | bytes 196612
  5.1 23.3 %copy-start.13 = (bf16[1,2,25]{2,1,0:T(2,128)(2,1)S(1)}, bf16[1,2,25]{2,1,0:T(2,128)(2,1)}, u32[]{:S(2)}) copy-start(bf16[1,2,25]{2,1,0:T(2,128)(2,1)} %param.21) | copy-start | bytes 304
  5.1 23.3 %copy-start.14 = (bf16[1,2,25]{2,1,0:T(2,128)(2,1)S(1)}, bf16[1,2,25]{2,1,0:T(2,128)(2,1)}, u32[]{:S(2)}) copy-start(bf16[1,2,25]{2,1,0:T(2,128)(2,1)} %param.20) | copy-start | bytes 304
  5.1 23.3 %copy-start.11 = (bf16[9,21]{1,0:T(8,128)(2,1)S(1)}, bf16[9,21]{1,0:T(8,128)(2,1)}, u32[]{:S(2)}) copy-start(bf16[9,21]{1,0:T(8,128)(2,1)} %param.17) | copy-start | bytes 1138
  5.1 23.3 %copy-start.9 = (f32[9,21]{1,0:T(8,128)S(1)}, f32[9,21]{1,0:T(8,128)}, u32[]{:S(2)}) copy-start(f32[9,21]{1,0:T(8,128)} %param.18) | copy-start | bytes 2272
  5.1 23.3 %copy-start.12 = (f32[1,9]{1,0:T(1,128)S(1)}, f32[1,9]{1,0:T(1,128)}, u32[]{:S(2)}) copy-start(f32[1,9]{1,0:T(1,128)} %param.19) | copy-start | bytes 112
  5.1 53.6 %copy-start.10 = (s32[1,1,16,1]{2,3,1,0:T(1,128)S(1)}, s32[1,1,16,1]{2,3,1,0:T(1,128)}, u32[]{:S(2)}) copy-start(s32[1,1,16,1]{2,3,1,0:T(1,128)} %param.13) | copy-start | bytes 196
  5.1 70.4 %all-to-all-start.1 = ((bf16[16,272,256]{2,1,0:T(8,128)(2,1)}), bf16[16,272,256]{2,1,0:T(8,128)(2,1)}, u32[]{:S(2)}, u32[]{:S(2)}) async-start(bf16[16,272,256]{2,1,0:T(8,128)(2,1)} %pack_main.1), calls=%async_computation.1 | async-start | bytes 4456448 | tf_op jit(solution)/shard_map/all_to_all | solution.py:410
  15.2 4.0 %collective-permute-start.2 = (bf16[32,1024]{1,0:T(8,128)(2,1)S(1)}, bf16[32,1024]{1,0:T(8,128)(2,1)S(1)}, u32[]{:S(2)}, u32[]{:S(2)}) collective-permute-start(bf16[32,1024]{1,0:T(8,128)(2,1)S(1)} %bitcast.26), channel_id=1, source_target_pairs={{0,3},{1,0},{2,1},{3,2},{4,7},{5,4},{6,5},{7,6},{8,11},{9,8},{10,9... | collective-permute-start | bytes 196616 | tf_op jit(solution)/shard_map/ppermute | solution.py:419
  17.8 5.0 %collective-permute-start.1 = (bf16[32,1024]{1,0:T(8,128)(2,1)S(1)}, bf16[32,1024]{1,0:T(8,128)(2,1)S(1)}, u32[]{:S(2)}, u32[]{:S(2)}) collective-permute-start(bf16[32,1024]{1,0:T(8,128)(2,1)S(1)} %bitcast.27), channel_id=1, source_target_pairs={{0,2},{1,3},{2,0},{3,1},{4,6},{5,7},{6,4},{7,5},{8,10},{9,11},{10,... | collective-permute-start | bytes 196616 | tf_op jit(solution)/shard_map/ppermute | solution.py:419
  18.2 6.3 %collective-permute-start = (bf16[32,1024]{1,0:T(8,128)(2,1)S(1)}, bf16[32,1024]{1,0:T(8,128)(2,1)S(1)}, u32[]{:S(2)}, u32[]{:S(2)}) collective-permute-start(bf16[32,1024]{1,0:T(8,128)(2,1)S(1)} %bitcast.28), channel_id=1, source_target_pairs={{0,1},{1,2},{2,3},{3,0},{4,5},{5,6},{6,7},{7,4},{8,9},{9,10},{10,1... | collective-permute-start | bytes 196616 | tf_op jit(solution)/shard_map/ppermute | solution.py:419
  24.5 8.6 %collective-permute-start.5 = (bf16[128,1024]{1,0:T(8,128)(2,1)S(1)}, bf16[128,1024]{1,0:T(8,128)(2,1)S(1)}, u32[]{:S(2)}, u32[]{:S(2)}) collective-permute-start(bf16[128,1024]{1,0:T(8,128)(2,1)S(1)} %pad_maximum_fusion.refs_0_), channel_id=1, source_target_pairs={{0,12},{1,13},{2,14},{3,15},{4,0},{5,1},{6,2},{7,3},{8,4},{9,5},{1... | collective-permute-start | bytes 786440 | tf_op jit(solution)/shard_map/ppermute | solution.py:421
  27.2 8.4 %collective-permute-start.4 = (bf16[128,1024]{1,0:T(8,128)(2,1)S(1)}, bf16[128,1024]{1,0:T(8,128)(2,1)S(1)}, u32[]{:S(2)}, u32[]{:S(2)}) collective-permute-start(bf16[128,1024]{1,0:T(8,128)(2,1)S(1)} %pad_maximum_fusion.refs_0_), channel_id=1, source_target_pairs={{0,8},{1,9},{2,10},{3,11},{4,12},{5,13},{6,14},{7,15},{8,0},{9,1},... | collective-permute-start | bytes 786440 | tf_op jit(solution)/shard_map/ppermute | solution.py:421
  27.6 15.1 %collective-permute-start.3 = (bf16[128,1024]{1,0:T(8,128)(2,1)S(1)}, bf16[128,1024]{1,0:T(8,128)(2,1)S(1)}, u32[]{:S(2)}, u32[]{:S(2)}) collective-permute-start(bf16[128,1024]{1,0:T(8,128)(2,1)S(1)} %pad_maximum_fusion.refs_0_), channel_id=1, source_target_pairs={{0,4},{1,5},{2,6},{3,7},{4,8},{5,9},{6,10},{7,11},{8,12},{9,13},{1... | collective-permute-start | bytes 786440 | tf_op jit(solution)/shard_map/ppermute | solution.py:421
  35.7 0.7 copy-start
  42.7 0.7 copy-start.2
  43.4 0.9 copy-start.1
  44.3 0.9 copy-start.3
  61.5 0.6 copy-start.5
  62.2 0.7 copy-start.6
  62.8 21.3 %collective-permute-start.7 = (bf16[256,256]{1,0:T(8,128)(2,1)}, bf16[256,256]{1,0:T(8,128)(2,1)S(1)}, u32[]{:S(2)}, u32[]{:S(2)}) collective-permute-start(bf16[256,256]{1,0:T(8,128)(2,1)} %get-tuple-element.45), channel_id=1, source_target_pairs={{0,64},{16,80},{32,96},{48,112},{64,128},{80,144},{96,160},{112,17... | collective-permute-start | bytes 393224 | tf_op jit(solution)/shard_map/ppermute | solution.py:446
  64.3 19.8 %collective-permute-start.8 = (bf16[256,256]{1,0:T(8,128)(2,1)}, bf16[256,256]{1,0:T(8,128)(2,1)S(1)}, u32[]{:S(2)}, u32[]{:S(2)}) collective-permute-start(bf16[256,256]{1,0:T(8,128)(2,1)} %get-tuple-element.47), channel_id=1, source_target_pairs={{0,96},{16,112},{32,128},{48,144},{64,160},{80,176},{96,192},{112,... | collective-permute-start | bytes 393224 | tf_op jit(solution)/shard_map/ppermute | solution.py:446
  67.7 19.1 %collective-permute-start.9 = (bf16[256,256]{1,0:T(8,128)(2,1)}, bf16[256,256]{1,0:T(8,128)(2,1)S(1)}, u32[]{:S(2)}, u32[]{:S(2)}) collective-permute-start(bf16[256,256]{1,0:T(8,128)(2,1)} %get-tuple-element.49), channel_id=1, source_target_pairs={{0,128},{16,144},{32,160},{48,176},{64,192},{80,208},{96,224},{112... | collective-permute-start | bytes 393224 | tf_op jit(solution)/shard_map/ppermute | solution.py:446
  68.8 19.5 %collective-permute-start.10 = (bf16[256,256]{1,0:T(8,128)(2,1)}, bf16[256,256]{1,0:T(8,128)(2,1)S(1)}, u32[]{:S(2)}, u32[]{:S(2)}) collective-permute-start(bf16[256,256]{1,0:T(8,128)(2,1)} %get-tuple-element.51), channel_id=1, source_target_pairs={{0,160},{16,176},{32,192},{48,208},{64,224},{80,240},{96,0},{112,1... | collective-permute-start | bytes 393224 | tf_op jit(solution)/shard_map/ppermute | solution.py:446
  72.0 21.6 %collective-permute-start.11 = (bf16[256,256]{1,0:T(8,128)(2,1)}, bf16[256,256]{1,0:T(8,128)(2,1)}, u32[]{:S(2)}, u32[]{:S(2)}) collective-permute-start(bf16[256,256]{1,0:T(8,128)(2,1)} %get-tuple-element.53), channel_id=1, source_target_pairs={{0,192},{16,208},{32,224},{48,240},{64,0},{80,16},{96,32},{112,48}... | collective-permute-start | bytes 393224 | tf_op jit(solution)/shard_map/ppermute | solution.py:446
  84.1 12.6 %collective-permute-start.6 = (bf16[256,256]{1,0:T(8,128)(2,1)}, bf16[256,256]{1,0:T(8,128)(2,1)S(1)}, u32[]{:S(2)}, u32[]{:S(2)}) collective-permute-start(bf16[256,256]{1,0:T(8,128)(2,1)} %copy-done.6), channel_id=1, source_target_pairs={{0,32},{16,48},{32,64},{48,80},{64,96},{80,112},{96,128},{112,144}... | collective-permute-start | bytes 393224 | tf_op jit(solution)/shard_map/ppermute | solution.py:449
  84.1 12.7 %collective-permute-start.12 = (bf16[256,256]{1,0:T(8,128)(2,1)}, bf16[256,256]{1,0:T(8,128)(2,1)S(1)}, u32[]{:S(2)}, u32[]{:S(2)}) collective-permute-start(bf16[256,256]{1,0:T(8,128)(2,1)} %copy-done.5), channel_id=1, source_target_pairs={{0,224},{16,240},{32,0},{48,16},{64,32},{80,48},{96,64},{112,80},{... | collective-permute-start | bytes 393224 | tf_op jit(solution)/shard_map/ppermute | solution.py:449
  86.8 10.5 %collective-permute-start.13 = (bf16[256,256]{1,0:T(8,128)(2,1)S(1)}, bf16[256,256]{1,0:T(8,128)(2,1)S(1)}, u32[]{:S(2)}, u32[]{:S(2)}) collective-permute-start(bf16[256,256]{1,0:T(8,128)(2,1)S(1)} %get-tuple-element.40.refs_1_), channel_id=1, source_target_pairs={{0,16},{16,0},{32,48},{48,32},{64,80},{80,64},{96,112},{112,96},{1... | collective-permute-start | bytes 393224 | tf_op jit(solution)/shard_map/ppermute | solution.py:452
  88.3 9.2 %collective-permute-start.15 = (bf16[256,256]{1,0:T(8,128)(2,1)S(1)}, bf16[256,256]{1,0:T(8,128)(2,1)S(1)}, u32[]{:S(2)}, u32[]{:S(2)}) collective-permute-start(bf16[256,256]{1,0:T(8,128)(2,1)S(1)} %collective-permute-done.7.refs_3_), channel_id=1, source_target_pairs={{0,16},{16,0},{32,48},{48,32},{64,80},{80,64},{96,112},{112,96},{1... | collective-permute-start | bytes 393224 | tf_op jit(solution)/shard_map/ppermute | solution.py:452
  93.6 4.3 %collective-permute-start.16 = (bf16[256,256]{1,0:T(8,128)(2,1)S(1)}, bf16[256,256]{1,0:T(8,128)(2,1)S(1)}, u32[]{:S(2)}, u32[]{:S(2)}) collective-permute-start(bf16[256,256]{1,0:T(8,128)(2,1)S(1)} %collective-permute-done.8.refs_4_), channel_id=1, source_target_pairs={{0,16},{16,0},{32,48},{48,32},{64,80},{80,64},{96,112},{112,96},{1... | collective-permute-start | bytes 393224 | tf_op jit(solution)/shard_map/ppermute | solution.py:452
  94.2 5.0 %copy-start.7 = (bf16[16,256,256]{2,1,0:T(8,128)(2,1)S(1)}, bf16[16,256,256]{2,1,0:T(8,128)(2,1)}, u32[]{:S(2)}) copy-start(bf16[16,256,256]{2,1,0:T(8,128)(2,1)} %get-tuple-element.61.refs_17_) | copy-start | bytes 6291460
  96.7 1.4 %collective-permute-start.17 = (bf16[256,256]{1,0:T(8,128)(2,1)S(1)}, bf16[256,256]{1,0:T(8,128)(2,1)S(1)}, u32[]{:S(2)}, u32[]{:S(2)}) collective-permute-start(bf16[256,256]{1,0:T(8,128)(2,1)S(1)} %collective-permute-done.9.refs_5_), channel_id=1, source_target_pairs={{0,16},{16,0},{32,48},{48,32},{64,80},{80,64},{96,112},{112,96},{1... | collective-permute-start | bytes 393224 | tf_op jit(solution)/shard_map/ppermute | solution.py:452
  96.9 1.5 %collective-permute-start.18 = (bf16[256,256]{1,0:T(8,128)(2,1)S(1)}, bf16[256,256]{1,0:T(8,128)(2,1)S(1)}, u32[]{:S(2)}, u32[]{:S(2)}) collective-permute-start(bf16[256,256]{1,0:T(8,128)(2,1)S(1)} %collective-permute-done.10.refs_6_), channel_id=1, source_target_pairs={{0,16},{16,0},{32,48},{48,32},{64,80},{80,64},{96,112},{112,96},{1... | collective-permute-start | bytes 393224 | tf_op jit(solution)/shard_map/ppermute | solution.py:452
  97.3 1.6 %collective-permute-start.19 = (bf16[256,256]{1,0:T(8,128)(2,1)}, bf16[256,256]{1,0:T(8,128)(2,1)S(1)}, u32[]{:S(2)}, u32[]{:S(2)}) collective-permute-start(bf16[256,256]{1,0:T(8,128)(2,1)} %collective-permute-done.11.refs_7_), channel_id=1, source_target_pairs={{0,16},{16,0},{32,48},{48,32},{64,80},{80,64},{96,112},{112,96},{1... | collective-permute-start | bytes 393224 | tf_op jit(solution)/shard_map/ppermute | solution.py:452
  97.5 1.5 %collective-permute-start.14 = (bf16[256,256]{1,0:T(8,128)(2,1)S(1)}, bf16[256,256]{1,0:T(8,128)(2,1)S(1)}, u32[]{:S(2)}, u32[]{:S(2)}) collective-permute-start(bf16[256,256]{1,0:T(8,128)(2,1)S(1)} %collective-permute-done.6.refs_2_), channel_id=1, source_target_pairs={{0,16},{16,0},{32,48},{48,32},{64,80},{80,64},{96,112},{112,96},{1... | collective-permute-start | bytes 393224 | tf_op jit(solution)/shard_map/ppermute | solution.py:452
  97.9 1.3 %collective-permute-start.20 = (bf16[256,256]{1,0:T(8,128)(2,1)S(1)}, bf16[256,256]{1,0:T(8,128)(2,1)S(1)}, u32[]{:S(2)}, u32[]{:S(2)}) collective-permute-start(bf16[256,256]{1,0:T(8,128)(2,1)S(1)} %collective-permute-done.12.refs_8_), channel_id=1, source_target_pairs={{0,16},{16,0},{32,48},{48,32},{64,80},{80,64},{96,112},{112,96},{1... | collective-permute-start | bytes 393224 | tf_op jit(solution)/shard_map/ppermute | solution.py:452

commit v5 on v4

--- a/solution.py
+++ b/solution.py
@@ -425,7 +425,7 @@
         groups, me, basis_rows.astype(F32), scaled, psf_rows[0].astype(F32),
         psf_cols[0].astype(F32),
     )
-    extra = pack_extra(pieces, patches, count, col_table, n_patch)
+    extra = pack_extra(pieces, patches, count, groups[-1], n_patch)
     edge = pieces.shape[1]
     notes = arrived[:, edge, :NOTE_WORDS].astype(jnp.int32)
     total = add_first(notes, arrived, total)

time: 104 us -> 113 us (1.087)
  waiting for transfers between devices: 30.2 us -> 47.6 us
  local copies, waits for them, and re-layouts: 5.36 us -> 0.76 us
  starting transfers between devices: 38 us -> 36.3 us
  Pallas kernels: 26.5 us -> 25.3 us
    ppermute x5, waiting for transfers between devices: 9.78 us -> 36.2 us  [per_device(): own[d] = lax.ppermute(extra[d], 'patch', to_chip(d))]
    ppermute x3, waiting for transfers between devices: 13.5 us -> 4.93 us  [per_device(): lax.ppermute(near, 'visit', along_y(d))]
    unnamed x30 -> x18, local copies, waits for them, and re-layouts: 5.28 us -> 0.69 us
    ppermute x3, starting transfers between devices: 3.87 us -> 7 us  [per_device(): lax.ppermute(near, 'visit', along_y(d))]
    ppermute x5, starting transfers between devices: 12.7 us -> 10.3 us  [per_device(): own[d] = lax.ppermute(extra[d], 'patch', to_chip(d))]
    ppermute x2, starting transfers between devices: 2.68 us -> 0.82 us  [per_device(): own[d] = lax.ppermute(waiting, 'patch', to_chip(d))]
  transfers between devices with their start and end apart: 22 -> 22, of which waited for: 12 -> 11; matrix products, arithmetic and copies ran while one was open for 2% -> 1% of each run, Pallas kernels for 18% -> 16%
where the time goes in v5:
time: 113 us
  waiting for transfers between devices  47.6 us (42%)
  starting transfers between devices  36.3 us (32%)
  Pallas kernels  25.3 us (22%)
  between operations  1.61 us (1%)
  other arithmetic  1.5 us (1%)
    ppermute x5, waiting for transfers between devices, per_device(): own[d] = lax.ppermute(extra[d], 'patch', to_chip(d))  36.2 us
    pallas_call x1, Pallas kernels, make_model(): pl.pallas_call(kernel, out_shape=(jax.ShapeDtypeStruct((height, breadth),...  13.4 us
    ppermute x5, starting transfers between devices, per_device(): own[d] = lax.ppermute(extra[d], 'patch', to_chip(d))  10.3 us
    all_to_all x1, starting transfers between devices, per_device(): arrived = lax.all_to_all(outgoing, 'patch', 0, 0, tiled=True)  10 us
    ppermute x3, starting transfers between devices, per_device(): lax.ppermute(near, 'visit', along_y(d))  7 us
    ppermute x3, waiting for transfers between devices, per_device(): lax.ppermute(rows, 'visit', along_x(d))  5.48 us
    ppermute x3, waiting for transfers between devices, per_device(): lax.ppermute(near, 'visit', along_y(d))  4.93 us
    ppermute x8, starting transfers between devices, per_device(): other[d] = lax.ppermute(own[d], 'patch', neighbour)  4.38 us
  transfers between devices with their start and end apart: 22, of which 11 were waited for; matrix products, arithmetic and copies ran while one was open for 1% of the time, Pallas kernels for 16%

profile of v5, /device:TPU:1, one launch (start us, length us, event | category | flops | bytes accessed | tf_op | source)
XLA Modules:
  0.0 113.1 jit_solution(4761756793605565203)
XLA Ops:
  0.7 0.6 copy-done
  1.3 3.7 %pack_main.1 = bf16[16,272,256]{2,1,0:T(8,128)(2,1)} custom-call(s32[16]{0:T(128)} %bitcast.30, s32[16]{0:T(128)S(1)} %bitcast.22, s32[1]{0:T(128)} %bitcast.18.count, bf16[16,256,256]{2,1,0:T(8,128)(2,1)} %bitcast.23), custom_call_target="tpu_custom_call" | custom-call | tf_op jit(solution)/shard_map/pack_main/pallas_call | solution.py:118
  5.0 10.0 %all-to-all-start.1 = ((bf16[16,272,256]{2,1,0:T(8,128)(2,1)}), bf16[16,272,256]{2,1,0:T(8,128)(2,1)}, u32[]{:S(2)}, u32[]{:S(2)}) async-start(bf16[16,272,256]{2,1,0:T(8,128)(2,1)} %pack_main.1), calls=%async_computation.1 | async-start | bytes 4456448 | tf_op jit(solution)/shard_map/all_to_all | solution.py:410
  15.1 0.0 copy-start.6
  15.1 2.6 %collective-permute-start.2 = (bf16[32,1024]{1,0:T(8,128)(2,1)S(1)}, bf16[32,1024]{1,0:T(8,128)(2,1)S(1)}, u32[]{:S(2)}, u32[]{:S(2)}) collective-permute-start(bf16[32,1024]{1,0:T(8,128)(2,1)S(1)} %bitcast.26), channel_id=1, source_target_pairs={{0,3},{1,0},{2,1},{3,2},{4,7},{5,4},{6,5},{7,6},{8,11},{9,8},{10,9... | collective-permute-start | bytes 196616 | tf_op jit(solution)/shard_map/ppermute | solution.py:419
  17.7 0.5 collective-permute-start.1
  18.2 0.7 collective-permute-start
  18.9 0.1 collective-permute-done.2
  19.0 3.7 %collective-permute-done.1 = bf16[32,1024]{1,0:T(8,128)(2,1)S(1)} collective-permute-done((bf16[32,1024]{1,0:T(8,128)(2,1)S(1)}, bf16[32,1024]{1,0:T(8,128)(2,1)S(1)}, u32[]{:S(2)}, u32[]{:S(2)}) %collective-permute-start.1) | collective-permute-done | bytes 65568 | tf_op jit(solution)/shard_map/ppermute | solution.py:419
  22.7 1.7 %collective-permute-done = bf16[32,1024]{1,0:T(8,128)(2,1)S(1)} collective-permute-done((bf16[32,1024]{1,0:T(8,128)(2,1)S(1)}, bf16[32,1024]{1,0:T(8,128)(2,1)S(1)}, u32[]{:S(2)}, u32[]{:S(2)}) %collective-permute-start) | collective-permute-done | bytes 65568 | tf_op jit(solution)/shard_map/ppermute | solution.py:419
  24.4 2.9 %collective-permute-start.3 = (bf16[128,1024]{1,0:T(8,128)(2,1)S(1)}, bf16[128,1024]{1,0:T(8,128)(2,1)S(1)}, u32[]{:S(2)}, u32[]{:S(2)}) collective-permute-start(bf16[128,1024]{1,0:T(8,128)(2,1)S(1)} %pad_maximum_fusion.refs_0_), channel_id=1, source_target_pairs={{0,12},{1,13},{2,14},{3,15},{4,0},{5,1},{6,2},{7,3},{8,4},{9,5},{1... | collective-permute-start | bytes 786440 | tf_op jit(solution)/shard_map/ppermute | solution.py:421
  27.3 4.9 %collective-permute-done.3.after.refs_3_ = bf16[128,1024]{1,0:T(8,128)(2,1)S(1)} collective-permute-done((bf16[128,1024]{1,0:T(8,128)(2,1)S(1)}, bf16[128,1024]{1,0:T(8,128)(2,1)S(1)}, u32[]{:S(2)}, u32[]{:S(2)}) %collective-permute-start.3) | collective-permute-done | bytes 262176 | tf_op jit(solution)/shard_map/ppermute | solution.py:421
  32.2 2.0 %pack_extra.1 = (bf16[256,256]{1,0:T(8,128)(2,1)S(1)}, bf16[256,256]{1,0:T(8,128)(2,1)S(1)}, bf16[256,256]{1,0:T(8,128)(2,1)S(1)}, bf16[256,256]{1,0:T(8,128)(2,...) custom-call(s32[16]{0:T(128)S(1)} %bitcast.31, ...), custom_call_target="tpu_custom_call" | custom-call | tf_op jit(solution)/shard_map/pack_extra/pallas_call | solution.py:81
  34.3 1.6 %collective-permute-start.7 = (bf16[256,256]{1,0:T(8,128)(2,1)S(1)}, bf16[256,256]{1,0:T(8,128)(2,1)S(1)}, u32[]{:S(2)}, u32[]{:S(2)}) collective-permute-start(bf16[256,256]{1,0:T(8,128)(2,1)S(1)} %get-tuple-element.44), channel_id=1, source_target_pairs={{0,64},{16,80},{32,96},{48,112},{64,128},{80,144},{96,160},{112,17... | collective-permute-start | bytes 393224 | tf_op jit(solution)/shard_map/ppermute | solution.py:446
  35.8 3.5 %collective-permute-start.8 = (bf16[256,256]{1,0:T(8,128)(2,1)S(1)}, bf16[256,256]{1,0:T(8,128)(2,1)S(1)}, u32[]{:S(2)}, u32[]{:S(2)}) collective-permute-start(bf16[256,256]{1,0:T(8,128)(2,1)S(1)} %get-tuple-element.46), channel_id=1, source_target_pairs={{0,96},{16,112},{32,128},{48,144},{64,160},{80,176},{96,192},{112,... | collective-permute-start | bytes 393224 | tf_op jit(solution)/shard_map/ppermute | solution.py:446
  39.3 0.1 broadcast_multiply_fusion.refs_6_
  39.4 1.7 %collective-permute-start.6 = (bf16[128,1024]{1,0:T(8,128)(2,1)S(1)}, bf16[128,1024]{1,0:T(8,128)(2,1)S(1)}, u32[]{:S(2)}, u32[]{:S(2)}) collective-permute-start(bf16[128,1024]{1,0:T(8,128)(2,1)S(1)} %pad_maximum_fusion.refs_0_), channel_id=1, source_target_pairs={{0,8},{1,9},{2,10},{3,11},{4,12},{5,13},{6,14},{7,15},{8,0},{9,1},... | collective-permute-start | bytes 786440 | tf_op jit(solution)/shard_map/ppermute | solution.py:421
  41.1 2.4 %collective-permute-start.5 = (bf16[128,1024]{1,0:T(8,128)(2,1)S(1)}, bf16[128,1024]{1,0:T(8,128)(2,1)S(1)}, u32[]{:S(2)}, u32[]{:S(2)}) collective-permute-start(bf16[128,1024]{1,0:T(8,128)(2,1)S(1)} %pad_maximum_fusion.refs_0_), channel_id=1, source_target_pairs={{0,4},{1,5},{2,6},{3,7},{4,8},{5,9},{6,10},{7,11},{8,12},{9,13},{1... | collective-permute-start | bytes 786440 | tf_op jit(solution)/shard_map/ppermute | solution.py:421
  43.5 1.3 %collective-permute-start.9 = (bf16[256,256]{1,0:T(8,128)(2,1)S(1)}, bf16[256,256]{1,0:T(8,128)(2,1)S(1)}, u32[]{:S(2)}, u32[]{:S(2)}) collective-permute-start(bf16[256,256]{1,0:T(8,128)(2,1)S(1)} %get-tuple-element.48), channel_id=1, source_target_pairs={{0,128},{16,144},{32,160},{48,176},{64,192},{80,208},{96,224},{112... | collective-permute-start | bytes 393224 | tf_op jit(solution)/shard_map/ppermute | solution.py:446
  44.8 26.5 %collective-permute-done.7.refs_3_ = bf16[256,256]{1,0:T(8,128)(2,1)S(1)} collective-permute-done((bf16[256,256]{1,0:T(8,128)(2,1)S(1)}, bf16[256,256]{1,0:T(8,128)(2,1)S(1)}, u32[]{:S(2)}, u32[]{:S(2)}) %collective-permute-start.7) | collective-permute-done | bytes 131104 | tf_op jit(solution)/shard_map/ppermute | solution.py:446
  71.2 3.9 %collective-permute-start.10 = (bf16[256,256]{1,0:T(8,128)(2,1)S(1)}, bf16[256,256]{1,0:T(8,128)(2,1)S(1)}, u32[]{:S(2)}, u32[]{:S(2)}) collective-permute-start(bf16[256,256]{1,0:T(8,128)(2,1)S(1)} %get-tuple-element.50), channel_id=1, source_target_pairs={{0,160},{16,176},{32,192},{48,208},{64,224},{80,240},{96,0},{112,1... | collective-permute-start | bytes 393224 | tf_op jit(solution)/shard_map/ppermute | solution.py:446
  75.2 7.6 %collective-permute-done.8.refs_4_ = bf16[256,256]{1,0:T(8,128)(2,1)S(1)} collective-permute-done((bf16[256,256]{1,0:T(8,128)(2,1)S(1)}, bf16[256,256]{1,0:T(8,128)(2,1)S(1)}, u32[]{:S(2)}, u32[]{:S(2)}) %collective-permute-start.8) | collective-permute-done | bytes 131104 | tf_op jit(solution)/shard_map/ppermute | solution.py:446
  82.7 0.0 collective-permute-start.11
  82.8 0.0 all-to-all-done.1.blocks
  82.8 0.8 slice_convert_fusion
  83.5 0.1 copy.14
  83.6 0.6 compare_reduce_fusion
  84.9 0.0 copy-start.7
  84.9 0.0 copy-start.8
  85.0 1.1 collective-permute-start.13
  86.1 0.8 collective-permute-start.4
  86.9 0.0 collective-permute-done.9.refs_5_
  86.9 0.8 collective-permute-start.15
  87.8 0.0 collective-permute-start.16
  87.8 2.1 %collective-permute-done.11.refs_7_ = bf16[256,256]{1,0:T(8,128)(2,1)S(1)} collective-permute-done((bf16[256,256]{1,0:T(8,128)(2,1)S(1)}, bf16[256,256]{1,0:T(8,128)(2,1)S(1)}, u32[]{:S(2)}, u32[]{:S(2)}) %collective-permute-start.11) | collective-permute-done | bytes 131104 | tf_op jit(solution)/shard_map/ppermute | solution.py:446
  89.9 0.0 collective-permute-start.12
  89.9 13.4 %model.1 = (f32[512,1024]{1,0:T(8,128)S(1)}, bf16[256,256]{1,0:T(8,128)(2,1)S(1)}, bf16[2,272,512]{2,1,0:T(8,128)(2,1)S(1)}) custom-call(bf16[128,1024]{1,0:T(8,128)(2,1)S(1)} %pad_maximum_fusion.refs_0_, bf16[128,1024]{1,0:T(8,128)(2,1)S(1)} %collective-permute-done.5.refs_1_, bf16[128,1024]{1,0:T(8,128)(2,1)S(1)} %collective-permute-done.6.refs_2_, ...), custom_call_target="tpu_custom_call" | custom-call | tf_op jit(solution)/shard_map/model/pallas_call | solution.py:240
  103.3 2.4 %add_first.1.refs_18_ = f32[512,1024]{1,0:T(8,128)S(1)} custom-call(s32[16,8]{1,0:T(8,128)S(1)} %bitcast.20, bf16[16,272,256]{2,1,0:T(8,128)(2,1)} %all-to-all-done.1.blocks, f32[512,1024]{1,0:T(8,128)S(1)} %get-tuple-element.42.less), custom_call_target="tpu_custom_call" | custom-call | tf_op jit(solution)/shard_map/add_first/pallas_call | solution.py:285
  105.7 1.4 %collective-permute-start.17 = (bf16[256,256]{1,0:T(8,128)(2,1)S(1)}, bf16[256,256]{1,0:T(8,128)(2,1)S(1)}, u32[]{:S(2)}, u32[]{:S(2)}) collective-permute-start(bf16[256,256]{1,0:T(8,128)(2,1)S(1)} %collective-permute-done.9.refs_5_), channel_id=1, source_target_pairs={{0,16},{16,0},{32,48},{48,32},{64,80},{80,64},{96,112},{112,96},{1... | collective-permute-start | bytes 393224 | tf_op jit(solution)/shard_map/ppermute | solution.py:452
  107.1 0.1 collective-permute-start.18
  107.2 0.4 collective-permute-start.19
  107.6 0.1 collective-permute-start.14
  107.7 0.4 collective-permute-start.20
  108.1 0.3 collective-permute-done.18.refs_14_
  108.4 0.2 collective-permute-done.19.refs_15_
  108.6 0.3 collective-permute-done.14.refs_10_
  108.9 0.2 collective-permute-done.20.refs_16_
  109.1 3.8 %finish.1 = f32[512,1024]{1,0:T(8,128)} custom-call(s32[16,8]{1,0:T(8,128)S(1)} %bitcast.21, bf16[256,256]{1,0:T(8,128)(2,1)S(1)} %get-tuple-element.39.refs_1_, bf16[256,256]{1,0:T(8,128)(2,1)S(1)} %collective-permute-done.4.refs_2_, bf16[256,256]{1,0:T(8,128)(2,1)S(1)} %collective-permute-done.7.refs_3_, ...), custom_call_target="tpu_custom_call" | custom-call | tf_op jit(solution)/shard_map/finish/pallas_call | solution.py:368
  (28 shorter events, 0.1 us)
Async XLA Ops:
  0.7 0.7 copy-start
  5.0 10.0 %copy-start.2 = (bf16[1,32,1024]{2,1,0:T(8,128)(2,1)S(1)}, bf16[1,32,1024]{2,1,0:T(8,128)(2,1)}, u32[]{:S(2)}) copy-start(bf16[1,32,1024]{2,1,0:T(8,128)(2,1)} %param.16) | copy-start | bytes 196612
  5.0 22.3 %copy-start.5 = (bf16[9,21]{1,0:T(8,128)(2,1)S(1)}, bf16[9,21]{1,0:T(8,128)(2,1)}, u32[]{:S(2)}) copy-start(bf16[9,21]{1,0:T(8,128)(2,1)} %param.17) | copy-start | bytes 1138
  5.0 27.2 %copy-start.4 = (s32[1,1,16,1]{2,3,1,0:T(1,128)S(1)}, s32[1,1,16,1]{2,3,1,0:T(1,128)}, u32[]{:S(2)}) copy-start(s32[1,1,16,1]{2,3,1,0:T(1,128)} %param.13) | copy-start | bytes 196
  5.0 77.7 %all-to-all-start.1 = ((bf16[16,272,256]{2,1,0:T(8,128)(2,1)}), bf16[16,272,256]{2,1,0:T(8,128)(2,1)}, u32[]{:S(2)}, u32[]{:S(2)}) async-start(bf16[16,272,256]{2,1,0:T(8,128)(2,1)} %pack_main.1), calls=%async_computation.1 | async-start | bytes 4456448 | tf_op jit(solution)/shard_map/all_to_all | solution.py:410
  15.1 24.3 %copy-start.3 = (f32[9,21]{1,0:T(8,128)S(1)}, f32[9,21]{1,0:T(8,128)}, u32[]{:S(2)}) copy-start(f32[9,21]{1,0:T(8,128)} %param.18) | copy-start | bytes 2272
  15.1 24.3 %copy-start.6 = (f32[1,9]{1,0:T(1,128)S(1)}, f32[1,9]{1,0:T(1,128)}, u32[]{:S(2)}) copy-start(f32[1,9]{1,0:T(1,128)} %param.19) | copy-start | bytes 112
  15.1 3.9 %collective-permute-start.2 = (bf16[32,1024]{1,0:T(8,128)(2,1)S(1)}, bf16[32,1024]{1,0:T(8,128)(2,1)S(1)}, u32[]{:S(2)}, u32[]{:S(2)}) collective-permute-start(bf16[32,1024]{1,0:T(8,128)(2,1)S(1)} %bitcast.26), channel_id=1, source_target_pairs={{0,3},{1,0},{2,1},{3,2},{4,7},{5,4},{6,5},{7,6},{8,11},{9,8},{10,9... | collective-permute-start | bytes 196616 | tf_op jit(solution)/shard_map/ppermute | solution.py:419
  17.7 5.0 %collective-permute-start.1 = (bf16[32,1024]{1,0:T(8,128)(2,1)S(1)}, bf16[32,1024]{1,0:T(8,128)(2,1)S(1)}, u32[]{:S(2)}, u32[]{:S(2)}) collective-permute-start(bf16[32,1024]{1,0:T(8,128)(2,1)S(1)} %bitcast.27), channel_id=1, source_target_pairs={{0,2},{1,3},{2,0},{3,1},{4,6},{5,7},{6,4},{7,5},{8,10},{9,11},{10,... | collective-permute-start | bytes 196616 | tf_op jit(solution)/shard_map/ppermute | solution.py:419
  18.2 6.2 %collective-permute-start = (bf16[32,1024]{1,0:T(8,128)(2,1)S(1)}, bf16[32,1024]{1,0:T(8,128)(2,1)S(1)}, u32[]{:S(2)}, u32[]{:S(2)}) collective-permute-start(bf16[32,1024]{1,0:T(8,128)(2,1)S(1)} %bitcast.28), channel_id=1, source_target_pairs={{0,1},{1,2},{2,3},{3,0},{4,5},{5,6},{6,7},{7,4},{8,9},{9,10},{10,1... | collective-permute-start | bytes 196616 | tf_op jit(solution)/shard_map/ppermute | solution.py:419
  24.4 7.8 %collective-permute-start.3 = (bf16[128,1024]{1,0:T(8,128)(2,1)S(1)}, bf16[128,1024]{1,0:T(8,128)(2,1)S(1)}, u32[]{:S(2)}, u32[]{:S(2)}) collective-permute-start(bf16[128,1024]{1,0:T(8,128)(2,1)S(1)} %pad_maximum_fusion.refs_0_), channel_id=1, source_target_pairs={{0,12},{1,13},{2,14},{3,15},{4,0},{5,1},{6,2},{7,3},{8,4},{9,5},{1... | collective-permute-start | bytes 786440 | tf_op jit(solution)/shard_map/ppermute | solution.py:421
  34.3 37.0 %collective-permute-start.7 = (bf16[256,256]{1,0:T(8,128)(2,1)S(1)}, bf16[256,256]{1,0:T(8,128)(2,1)S(1)}, u32[]{:S(2)}, u32[]{:S(2)}) collective-permute-start(bf16[256,256]{1,0:T(8,128)(2,1)S(1)} %get-tuple-element.44), channel_id=1, source_target_pairs={{0,64},{16,80},{32,96},{48,112},{64,128},{80,144},{96,160},{112,17... | collective-permute-start | bytes 393224 | tf_op jit(solution)/shard_map/ppermute | solution.py:446
  35.8 46.9 %collective-permute-start.8 = (bf16[256,256]{1,0:T(8,128)(2,1)S(1)}, bf16[256,256]{1,0:T(8,128)(2,1)S(1)}, u32[]{:S(2)}, u32[]{:S(2)}) collective-permute-start(bf16[256,256]{1,0:T(8,128)(2,1)S(1)} %get-tuple-element.46), channel_id=1, source_target_pairs={{0,96},{16,112},{32,128},{48,144},{64,160},{80,176},{96,192},{112,... | collective-permute-start | bytes 393224 | tf_op jit(solution)/shard_map/ppermute | solution.py:446
  39.4 45.5 %collective-permute-start.6 = (bf16[128,1024]{1,0:T(8,128)(2,1)S(1)}, bf16[128,1024]{1,0:T(8,128)(2,1)S(1)}, u32[]{:S(2)}, u32[]{:S(2)}) collective-permute-start(bf16[128,1024]{1,0:T(8,128)(2,1)S(1)} %pad_maximum_fusion.refs_0_), channel_id=1, source_target_pairs={{0,8},{1,9},{2,10},{3,11},{4,12},{5,13},{6,14},{7,15},{8,0},{9,1},... | collective-permute-start | bytes 786440 | tf_op jit(solution)/shard_map/ppermute | solution.py:421
  41.1 45.0 %collective-permute-start.5 = (bf16[128,1024]{1,0:T(8,128)(2,1)S(1)}, bf16[128,1024]{1,0:T(8,128)(2,1)S(1)}, u32[]{:S(2)}, u32[]{:S(2)}) collective-permute-start(bf16[128,1024]{1,0:T(8,128)(2,1)S(1)} %pad_maximum_fusion.refs_0_), channel_id=1, source_target_pairs={{0,4},{1,5},{2,6},{3,7},{4,8},{5,9},{6,10},{7,11},{8,12},{9,13},{1... | collective-permute-start | bytes 786440 | tf_op jit(solution)/shard_map/ppermute | solution.py:421
  43.5 43.4 %collective-permute-start.9 = (bf16[256,256]{1,0:T(8,128)(2,1)S(1)}, bf16[256,256]{1,0:T(8,128)(2,1)S(1)}, u32[]{:S(2)}, u32[]{:S(2)}) collective-permute-start(bf16[256,256]{1,0:T(8,128)(2,1)S(1)} %get-tuple-element.48), channel_id=1, source_target_pairs={{0,128},{16,144},{32,160},{48,176},{64,192},{80,208},{96,224},{112... | collective-permute-start | bytes 393224 | tf_op jit(solution)/shard_map/ppermute | solution.py:446
  71.2 16.5 %collective-permute-start.10 = (bf16[256,256]{1,0:T(8,128)(2,1)S(1)}, bf16[256,256]{1,0:T(8,128)(2,1)S(1)}, u32[]{:S(2)}, u32[]{:S(2)}) collective-permute-start(bf16[256,256]{1,0:T(8,128)(2,1)S(1)} %get-tuple-element.50), channel_id=1, source_target_pairs={{0,160},{16,176},{32,192},{48,208},{64,224},{80,240},{96,0},{112,1... | collective-permute-start | bytes 393224 | tf_op jit(solution)/shard_map/ppermute | solution.py:446
  82.7 7.1 %collective-permute-start.11 = (bf16[256,256]{1,0:T(8,128)(2,1)S(1)}, bf16[256,256]{1,0:T(8,128)(2,1)S(1)}, u32[]{:S(2)}, u32[]{:S(2)}) collective-permute-start(bf16[256,256]{1,0:T(8,128)(2,1)S(1)} %get-tuple-element.52), channel_id=1, source_target_pairs={{0,192},{16,208},{32,224},{48,240},{64,0},{80,16},{96,32},{112,48}... | collective-permute-start | bytes 393224 | tf_op jit(solution)/shard_map/ppermute | solution.py:446
  84.9 5.0 %copy-start.7 = (bf16[1,2,25]{2,1,0:T(2,128)(2,1)S(1)}, bf16[1,2,25]{2,1,0:T(2,128)(2,1)}, u32[]{:S(2)}) copy-start(bf16[1,2,25]{2,1,0:T(2,128)(2,1)} %param.21) | copy-start | bytes 304
  84.9 5.0 %copy-start.8 = (bf16[1,2,25]{2,1,0:T(2,128)(2,1)S(1)}, bf16[1,2,25]{2,1,0:T(2,128)(2,1)}, u32[]{:S(2)}) copy-start(bf16[1,2,25]{2,1,0:T(2,128)(2,1)} %param.20) | copy-start | bytes 304
  85.0 22.2 %collective-permute-start.13 = (bf16[256,256]{1,0:T(8,128)(2,1)S(1)}, bf16[256,256]{1,0:T(8,128)(2,1)S(1)}, u32[]{:S(2)}, u32[]{:S(2)}) collective-permute-start(bf16[256,256]{1,0:T(8,128)(2,1)S(1)} %get-tuple-element.39.refs_1_), channel_id=1, source_target_pairs={{0,16},{16,0},{32,48},{48,32},{64,80},{80,64},{96,112},{112,96},{1... | collective-permute-start | bytes 393224 | tf_op jit(solution)/shard_map/ppermute | solution.py:452
  86.1 19.6 %collective-permute-start.4 = (bf16[256,256]{1,0:T(8,128)(2,1)S(1)}, bf16[256,256]{1,0:T(8,128)(2,1)S(1)}, u32[]{:S(2)}, u32[]{:S(2)}) collective-permute-start(bf16[256,256]{1,0:T(8,128)(2,1)S(1)} %get-tuple-element.41), channel_id=1, source_target_pairs={{0,32},{16,48},{32,64},{48,80},{64,96},{80,112},{96,128},{112,144}... | collective-permute-start | bytes 393224 | tf_op jit(solution)/shard_map/ppermute | solution.py:449
  86.9 20.7 %collective-permute-start.15 = (bf16[256,256]{1,0:T(8,128)(2,1)S(1)}, bf16[256,256]{1,0:T(8,128)(2,1)S(1)}, u32[]{:S(2)}, u32[]{:S(2)}) collective-permute-start(bf16[256,256]{1,0:T(8,128)(2,1)S(1)} %collective-permute-done.7.refs_3_), channel_id=1, source_target_pairs={{0,16},{16,0},{32,48},{48,32},{64,80},{80,64},{96,112},{112,96},{1... | collective-permute-start | bytes 393224 | tf_op jit(solution)/shard_map/ppermute | solution.py:452
  87.8 19.9 %collective-permute-start.16 = (bf16[256,256]{1,0:T(8,128)(2,1)S(1)}, bf16[256,256]{1,0:T(8,128)(2,1)S(1)}, u32[]{:S(2)}, u32[]{:S(2)}) collective-permute-start(bf16[256,256]{1,0:T(8,128)(2,1)S(1)} %collective-permute-done.8.refs_4_), channel_id=1, source_target_pairs={{0,16},{16,0},{32,48},{48,32},{64,80},{80,64},{96,112},{112,96},{1... | collective-permute-start | bytes 393224 | tf_op jit(solution)/shard_map/ppermute | solution.py:452
  89.9 17.2 %collective-permute-start.12 = (bf16[256,256]{1,0:T(8,128)(2,1)S(1)}, bf16[256,256]{1,0:T(8,128)(2,1)S(1)}, u32[]{:S(2)}, u32[]{:S(2)}) collective-permute-start(bf16[256,256]{1,0:T(8,128)(2,1)S(1)} %get-tuple-element.55), channel_id=1, source_target_pairs={{0,224},{16,240},{32,0},{48,16},{64,32},{80,48},{96,64},{112,80},{... | collective-permute-start | bytes 393224 | tf_op jit(solution)/shard_map/ppermute | solution.py:449
  103.3 5.9 %copy-start.1 = (bf16[16,256,256]{2,1,0:T(8,128)(2,1)S(1)}, bf16[16,256,256]{2,1,0:T(8,128)(2,1)}, u32[]{:S(2)}) copy-start(bf16[16,256,256]{2,1,0:T(8,128)(2,1)} %get-tuple-element.61.refs_17_) | copy-start | bytes 6291460
  105.7 2.4 %collective-permute-start.17 = (bf16[256,256]{1,0:T(8,128)(2,1)S(1)}, bf16[256,256]{1,0:T(8,128)(2,1)S(1)}, u32[]{:S(2)}, u32[]{:S(2)}) collective-permute-start(bf16[256,256]{1,0:T(8,128)(2,1)S(1)} %collective-permute-done.9.refs_5_), channel_id=1, source_target_pairs={{0,16},{16,0},{32,48},{48,32},{64,80},{80,64},{96,112},{112,96},{1... | collective-permute-start | bytes 393224 | tf_op jit(solution)/shard_map/ppermute | solution.py:452
  107.1 1.3 %collective-permute-start.18 = (bf16[256,256]{1,0:T(8,128)(2,1)S(1)}, bf16[256,256]{1,0:T(8,128)(2,1)S(1)}, u32[]{:S(2)}, u32[]{:S(2)}) collective-permute-start(bf16[256,256]{1,0:T(8,128)(2,1)S(1)} %collective-permute-done.10.refs_6_), channel_id=1, source_target_pairs={{0,16},{16,0},{32,48},{48,32},{64,80},{80,64},{96,112},{112,96},{1... | collective-permute-start | bytes 393224 | tf_op jit(solution)/shard_map/ppermute | solution.py:452
  107.2 1.4 %collective-permute-start.19 = (bf16[256,256]{1,0:T(8,128)(2,1)S(1)}, bf16[256,256]{1,0:T(8,128)(2,1)S(1)}, u32[]{:S(2)}, u32[]{:S(2)}) collective-permute-start(bf16[256,256]{1,0:T(8,128)(2,1)S(1)} %collective-permute-done.11.refs_7_), channel_id=1, source_target_pairs={{0,16},{16,0},{32,48},{48,32},{64,80},{80,64},{96,112},{112,96},{1... | collective-permute-start | bytes 393224 | tf_op jit(solution)/shard_map/ppermute | solution.py:452
  107.6 1.3 %collective-permute-start.14 = (bf16[256,256]{1,0:T(8,128)(2,1)S(1)}, bf16[256,256]{1,0:T(8,128)(2,1)S(1)}, u32[]{:S(2)}, u32[]{:S(2)}) collective-permute-start(bf16[256,256]{1,0:T(8,128)(2,1)S(1)} %collective-permute-done.4.refs_2_), channel_id=1, source_target_pairs={{0,16},{16,0},{32,48},{48,32},{64,80},{80,64},{96,112},{112,96},{1... | collective-permute-start | bytes 393224 | tf_op jit(solution)/shard_map/ppermute | solution.py:452
  107.7 1.4 %collective-permute-start.20 = (bf16[256,256]{1,0:T(8,128)(2,1)S(1)}, bf16[256,256]{1,0:T(8,128)(2,1)S(1)}, u32[]{:S(2)}, u32[]{:S(2)}) collective-permute-start(bf16[256,256]{1,0:T(8,128)(2,1)S(1)} %collective-permute-done.12.refs_8_), channel_id=1, source_target_pairs={{0,16},{16,0},{32,48},{48,32},{64,80},{80,64},{96,112},{112,96},{1... | collective-permute-start | bytes 393224 | tf_op jit(solution)/shard_map/ppermute | solution.py:452
